TPU v7x, 32 devices: a whole 2x2x4 slice. The times are simulated.
32 devices in a mesh: dp: 8 (over z, y), fsdp: 4 (over x, core).
Axes of the slice: x: 2, y: 2, z: 4, core: 2. Of those that a mesh axis runs over, the one named last changes fastest.
Arguments:
- codes: int32 [64, 256], P(('dp', 'fsdp')), may hold values from 0 to 2024
- mask_pos: int32 [64, 128], P(('dp', 'fsdp')), may hold values from 0 to 255, as said below
- mask_count: int32 [64], P(('dp', 'fsdp')), may hold values from 1 to 128, as said below
- table: float32 [2026, 768], P(None, ('dp', 'fsdp')), may hold values from -0.4330127 to 0.4330127
- w_qkv: float32 [2, 768, 2304], P(None, ('dp', 'fsdp')), may hold values from -0.21875 to 0.21875
- w_out: float32 [2, 768, 768], P(None, ('dp', 'fsdp')), may hold values from -0.875 to 0.875
- w_up: float32 [2, 768, 3072], P(None, ('dp', 'fsdp')), may hold values from -0.21875 to 0.21875
- w_down: float32 [2, 3072, 768], P(None, ('dp', 'fsdp')), may hold values from -0.109375 to 0.109375
- layer_vecs: float32 [2, 9216], P(None, ('dp', 'fsdp')), may hold values from -0.8 to 2.4
- final_norm: float32 [2, 768], P(None, ('dp', 'fsdp')), may hold values from -0.8 to 2.4
- head_bias: float32 [2026], replicated, may hold values from -0.625 to 0.625
- moment_table: float32 [2026, 768], P(None, ('dp', 'fsdp')), may hold values from -1.5258789e-05 to 1.5258789e-05
- moment_qkv: float32 [2, 768, 2304], P(None, ('dp', 'fsdp')), may hold values from -1.5258789e-05 to 1.5258789e-05
- moment_out: float32 [2, 768, 768], P(None, ('dp', 'fsdp')), may hold values from -1.5258789e-05 to 1.5258789e-05
- moment_up: float32 [2, 768, 3072], P(None, ('dp', 'fsdp')), may hold values from -1.5258789e-05 to 1.5258789e-05
- moment_down: float32 [2, 3072, 768], P(None, ('dp', 'fsdp')), may hold values from -1.5258789e-05 to 1.5258789e-05
- moment_vecs: float32 [2, 9216], P(None, ('dp', 'fsdp')), may hold values from -4.5776367e-05 to 4.5776367e-05
- moment_final: float32 [2, 768], P(None, ('dp', 'fsdp')), may hold values from -4.5776367e-05 to 4.5776367e-05
- moment_bias: float32 [2026], replicated, may hold values from -1.5258789e-05 to 1.5258789e-05
- average_table: float32 [2026, 768], P(None, ('dp', 'fsdp')), may hold values from -0.4375 to 0.4375
- average_qkv: float32 [2, 768, 2304], P(None, ('dp', 'fsdp')), may hold values from -0.21875 to 0.21875
- average_out: float32 [2, 768, 768], P(None, ('dp', 'fsdp')), may hold values from -0.875 to 0.875
- average_up: float32 [2, 768, 3072], P(None, ('dp', 'fsdp')), may hold values from -0.21875 to 0.21875
- average_down: float32 [2, 3072, 768], P(None, ('dp', 'fsdp')), may hold values from -0.109375 to 0.109375
- average_vecs: float32 [2, 9216], P(None, ('dp', 'fsdp')), may hold values from 0.5 to 1.5
- average_final: float32 [2, 768], P(None, ('dp', 'fsdp')), may hold values from 0.5 to 1.5
- average_bias: float32 [2026], replicated, may hold values from -0.625 to 0.625
Outputs:
- loss_sum: float32 [], replicated
- mask_total: float32 [], replicated
- grad_norm: float32 [], replicated
- table_new: float32 [2026, 768], P(None, ('dp', 'fsdp'))
- qkv_new: float32 [2, 768, 2304], P(None, ('dp', 'fsdp'))
- out_new: float32 [2, 768, 768], P(None, ('dp', 'fsdp'))
- up_new: float32 [2, 768, 3072], P(None, ('dp', 'fsdp'))
- down_new: float32 [2, 3072, 768], P(None, ('dp', 'fsdp'))
- vecs_new: float32 [2, 9216], P(None, ('dp', 'fsdp'))
- final_new: float32 [2, 768], P(None, ('dp', 'fsdp'))
- bias_new: float32 [2026], replicated
- table_moment: float32 [2026, 768], P(None, ('dp', 'fsdp'))
- qkv_moment: float32 [2, 768, 2304], P(None, ('dp', 'fsdp'))
- out_moment: float32 [2, 768, 768], P(None, ('dp', 'fsdp'))
- up_moment: float32 [2, 768, 3072], P(None, ('dp', 'fsdp'))
- down_moment: float32 [2, 3072, 768], P(None, ('dp', 'fsdp'))
- vecs_moment: float32 [2, 9216], P(None, ('dp', 'fsdp'))
- final_moment: float32 [2, 768], P(None, ('dp', 'fsdp'))
- bias_moment: float32 [2026], replicated
- table_average: float32 [2026, 768], P(None, ('dp', 'fsdp'))
- qkv_average: float32 [2, 768, 2304], P(None, ('dp', 'fsdp'))
- out_average: float32 [2, 768, 768], P(None, ('dp', 'fsdp'))
- up_average: float32 [2, 768, 3072], P(None, ('dp', 'fsdp'))
- down_average: float32 [2, 3072, 768], P(None, ('dp', 'fsdp'))
- vecs_average: float32 [2, 9216], P(None, ('dp', 'fsdp'))
- final_average: float32 [2, 768], P(None, ('dp', 'fsdp'))
- bias_average: float32 [2026], replicated
Inputs may be any that keep to these rules, and one draw needn't show every extreme that they name: `mask_pos`: each row holds 128 different positions of its image; the first mask_count entries of the row are the masked ones. `mask_count`: some image has 128 masked positions.
All inputs are finite; a program needn't handle non-finite values.
Results may differ from a plain program's by a relative error of at most 0.012.
The roundings to bfloat16 on the way count: a program that leaves them out, or rounds other values in their place, can miss the bound.
Values may be sent and summed in bfloat16 or wider, within the bound.
No kernel may reach another device: no remote copies, remote signals or barrier semaphores. Data moves between devices by JAX's collectives and lax.ppermute only.
A program may use at most 320 MiB of HBM per device.

v0:
```python
from functools import reduce

import jax
import jax.numpy as jnp
from jax import lax
from jax.sharding import PartitionSpec as P

D = 768
HEADS = 12
HEAD_DIM = 64
FF = 3072
V = 2026
M = 128
L = 2
MB = 2


epsilon = 1e-06
step_rate = 10000.0
inertia = 0.5
average_decay = 0.5
clip_bound = 0.01
highest = lax.Precision.HIGHEST


def normalize(stream, gain, shift):
    centre = stream - jnp.mean(stream, -1, keepdims=True)
    spread = lax.rsqrt(jnp.mean(centre * centre, -1, keepdims=True) + epsilon)
    scaled = centre * spread
    return (scaled * gain + shift, scaled, spread)


def normalize_back(upstream, scaled, spread, gain):
    weighted = upstream * gain
    inner = (
        weighted
        - jnp.mean(weighted, -1, keepdims=True)
        - scaled * jnp.mean(weighted * scaled, -1, keepdims=True)
    )
    return (spread * inner, jnp.sum(upstream * scaled, (0, 1)), jnp.sum(upstream, (0, 1)))


def split_vector(vector):
    return [vector[segment * D : (segment + 1) * D] for segment in range(8)] + [vector[8 * D :]]


def project(left, right):
    return jnp.einsum("bsd,de->bse", left, right, preferred_element_type=jnp.float32)


def heads_view(tensor):
    return tensor.reshape(tensor.shape[0], tensor.shape[1], HEADS, HEAD_DIM)


def raw_scores(queries, key_rows):
    product = jnp.einsum("bqhe,bkhe->bhqk", queries, key_rows, preferred_element_type=jnp.float32)
    return product * HEAD_DIM ** (-0.5)


def fetch_forward(shards, layer_idx):
    qkv_part, out_part, up_part, down_part, vector_part = [
        weight[layer_idx].astype(jnp.bfloat16) for weight in shards
    ]
    return (
        lax.all_gather(qkv_part, ("dp", "fsdp"), axis=0, tiled=True),
        lax.all_gather(out_part, ("dp", "fsdp"), axis=0, tiled=True),
        lax.all_gather(up_part, ("dp", "fsdp"), axis=0, tiled=True),
        lax.all_gather(down_part, ("dp", "fsdp"), axis=0, tiled=True),
        lax.all_gather(vector_part, ("dp", "fsdp"), axis=0, tiled=True),
    )


def fetch_backward(shards, layer_idx):
    qkv_part, out_part, up_part, down_part, vector_part = [
        weight[layer_idx].astype(jnp.bfloat16) for weight in shards
    ]
    return (
        lax.all_gather(qkv_part, ("dp", "fsdp"), axis=0, tiled=True),
        lax.all_gather(out_part, ("dp", "fsdp"), axis=0, tiled=True),
        lax.all_gather(up_part, ("dp", "fsdp"), axis=0, tiled=True),
        lax.all_gather(down_part, ("dp", "fsdp"), axis=0, tiled=True),
        lax.all_gather(vector_part, ("dp", "fsdp"), axis=0, tiled=True),
    )


def layer_forward(stream, weights):
    qkv_weight, out_weight, up_weight, down_weight, vector = weights
    (
        gain_one,
        shift_one,
        query_bias,
        value_bias,
        out_bias,
        gain_two,
        shift_two,
        down_bias,
        up_bias,
    ) = split_vector(vector.astype(jnp.float32))
    normed, scaled_one, spread_one = normalize(stream, gain_one, shift_one)
    normed_low = normed.astype(jnp.bfloat16)
    bias_all = jnp.concatenate([query_bias, jnp.zeros_like(query_bias), value_bias])
    triple = (project(normed_low, qkv_weight) + bias_all).astype(jnp.bfloat16)
    queries = heads_view(triple[..., :D])
    key_rows = heads_view(triple[..., D : 2 * D])
    values = heads_view(triple[..., 2 * D :])
    scores = raw_scores(queries, key_rows)
    peak = jnp.max(scores, -1)
    log_total = peak + jnp.log(jnp.sum(jnp.exp(scores - peak[..., None]), -1))
    probs = jnp.exp(scores - log_total[..., None]).astype(jnp.bfloat16)
    mixed = jnp.einsum("bhqk,bkhe->bqhe", probs, values, preferred_element_type=jnp.float32)
    mixed_low = mixed.reshape(stream.shape).astype(jnp.bfloat16)
    middle = stream + project(mixed_low, out_weight) + out_bias
    normed_two, scaled_two, spread_two = normalize(middle, gain_two, shift_two)
    normed_two_low = normed_two.astype(jnp.bfloat16)
    hidden = project(normed_two_low, up_weight) + up_bias
    active = jax.nn.gelu(hidden).astype(jnp.bfloat16)
    result = middle + project(active, down_weight) + down_bias
    kept = (
        scaled_one,
        spread_one,
        normed_low,
        triple,
        log_total,
        mixed_low,
        scaled_two,
        spread_two,
        normed_two_low,
        hidden,
        active,
    )
    return (result, kept)


def layer_backward(upstream, weights, kept):
    qkv_weight, out_weight, up_weight, down_weight, vector = weights
    (
        gain_one,
        shift_one,
        query_bias,
        value_bias,
        out_bias,
        gain_two,
        shift_two,
        down_bias,
        up_bias,
    ) = split_vector(vector.astype(jnp.float32))
    (
        scaled_one,
        spread_one,
        normed_low,
        triple,
        log_total,
        mixed_low,
        scaled_two,
        spread_two,
        normed_two_low,
        hidden,
        active,
    ) = kept
    grad_branch = upstream.astype(jnp.bfloat16)
    grad_down = jnp.einsum("bsf,bsd->fd", active, grad_branch, preferred_element_type=jnp.float32)
    grad_active = jnp.einsum(
        "bsd,fd->bsf", grad_branch, down_weight, preferred_element_type=jnp.float32
    )
    unused, gelu_back = jax.vjp(jax.nn.gelu, hidden)
    grad_hidden = gelu_back(grad_active)[0].astype(jnp.bfloat16)
    grad_up = jnp.einsum(
        "bsd,bsf->df", normed_two_low, grad_hidden, preferred_element_type=jnp.float32
    )
    grad_normed_two = jnp.einsum(
        "bsf,df->bsd", grad_hidden, up_weight, preferred_element_type=jnp.float32
    )
    back_two, grad_gain_two, grad_shift_two = normalize_back(
        grad_normed_two, scaled_two, spread_two, gain_two
    )
    grad_middle = upstream + back_two
    grad_out_low = grad_middle.astype(jnp.bfloat16)
    grad_out = jnp.einsum(
        "bsd,bse->de", mixed_low, grad_out_low, preferred_element_type=jnp.float32
    )
    grad_mixed = jnp.einsum(
        "bse,de->bsd", grad_out_low, out_weight, preferred_element_type=jnp.float32
    )
    grad_mixed = heads_view(grad_mixed.astype(jnp.bfloat16))
    queries = heads_view(triple[..., :D])
    key_rows = heads_view(triple[..., D : 2 * D])
    values = heads_view(triple[..., 2 * D :])
    probs = jnp.exp(raw_scores(queries, key_rows) - log_total[..., None])
    probs_low = probs.astype(jnp.bfloat16)
    grad_values = jnp.einsum(
        "bhqk,bqhe->bkhe", probs_low, grad_mixed, preferred_element_type=jnp.float32
    )
    grad_probs = jnp.einsum(
        "bqhe,bkhe->bhqk", grad_mixed, values, preferred_element_type=jnp.float32
    )
    inner = jnp.sum(probs * grad_probs, -1, keepdims=True)
    grad_scores = (probs * (grad_probs - inner)).astype(jnp.bfloat16)
    grad_queries = jnp.einsum(
        "bhqk,bkhe->bqhe", grad_scores, key_rows, preferred_element_type=jnp.float32
    ) * HEAD_DIM ** (-0.5)
    grad_keys = jnp.einsum(
        "bhqk,bqhe->bkhe", grad_scores, queries, preferred_element_type=jnp.float32
    ) * HEAD_DIM ** (-0.5)
    flat_shape = upstream.shape
    grad_triple = jnp.concatenate(
        [
            grad_queries.reshape(flat_shape),
            grad_keys.reshape(flat_shape),
            grad_values.reshape(flat_shape),
        ],
        -1,
    ).astype(jnp.bfloat16)
    grad_qkv = jnp.einsum(
        "bsd,bse->de", normed_low, grad_triple, preferred_element_type=jnp.float32
    )
    grad_normed = jnp.einsum(
        "bse,de->bsd", grad_triple, qkv_weight, preferred_element_type=jnp.float32
    )
    back_one, grad_gain_one, grad_shift_one = normalize_back(
        grad_normed, scaled_one, spread_one, gain_one
    )
    grad_stream = grad_middle + back_one
    triple_sums = jnp.sum(grad_triple.astype(jnp.float32), (0, 1))
    grad_vector = jnp.concatenate(
        [
            grad_gain_one,
            grad_shift_one,
            triple_sums[:D],
            triple_sums[2 * D :],
            jnp.sum(grad_out_low.astype(jnp.float32), (0, 1)),
            grad_gain_two,
            grad_shift_two,
            jnp.sum(grad_branch.astype(jnp.float32), (0, 1)),
            jnp.sum(grad_hidden.astype(jnp.float32), (0, 1)),
        ]
    )
    return (grad_stream, (grad_qkv, grad_out, grad_up, grad_down, grad_vector))


def update(weight, moment, average, grad, factor):
    clipped = grad * factor
    moment_next = inertia * moment + clipped
    weight_next = weight - step_rate * (clipped + inertia * moment_next)
    return (weight_next, moment_next, average_decay * average + (1.0 - average_decay) * weight_next)


def body(
    codes,
    mask_pos,
    mask_count,
    table,
    w_qkv,
    w_out,
    w_up,
    w_down,
    layer_vecs,
    final_norm,
    head_bias,
    moment_table,
    moment_qkv,
    moment_out,
    moment_up,
    moment_down,
    moment_vecs,
    moment_final,
    moment_bias,
    average_table,
    average_qkv,
    average_out,
    average_up,
    average_down,
    average_vecs,
    average_final,
    average_bias,
):
    shards = (w_qkv, w_out, w_up, w_down, layer_vecs)
    mask_total = lax.psum(jnp.sum(mask_count.astype(jnp.float32)), ("dp", "fsdp"))
    inverse = 1.0 / mask_total
    rows = codes.shape[0] // MB
    seq_len = codes.shape[1]
    grad_table = jnp.zeros((V, D), jnp.float32)
    grad_final = jnp.zeros((2, D), jnp.float32)
    grad_bias = jnp.zeros((V,), jnp.float32)
    loss_local = jnp.zeros((), jnp.float32)
    layer_shapes = [(D, 3 * D), (D, D), (D, FF), (FF, D), (8 * D + FF,)]
    grad_layers = [
        tuple((jnp.zeros(shape_one, jnp.float32) for shape_one in layer_shapes))
        for layer_idx in range(L)
    ]
    for batch_idx in range(MB):
        batch_codes = codes[batch_idx * rows : (batch_idx + 1) * rows]
        batch_pos = mask_pos[batch_idx * rows : (batch_idx + 1) * rows]
        batch_counts = mask_count[batch_idx * rows : (batch_idx + 1) * rows]
        table_low, final_low = (
            lax.all_gather(table.astype(jnp.bfloat16), ("dp", "fsdp"), axis=1, tiled=True),
            lax.all_gather(final_norm.astype(jnp.bfloat16), ("dp", "fsdp"), axis=1, tiled=True),
        )
        final_float = final_low.astype(jnp.float32)
        slots = jnp.arange(M, dtype=jnp.int32)
        valid = (slots[None, :] < batch_counts[:, None]).astype(jnp.float32)
        hits = batch_pos[:, :, None] == jnp.arange(seq_len, dtype=jnp.int32)[None, None, :]
        masked = jnp.any(hits & (valid[:, :, None] > 0), axis=1)
        inputs = jnp.where(masked, V - 1, batch_codes)
        targets = jnp.take_along_axis(batch_codes, batch_pos, axis=1)
        picker = hits.astype(jnp.float32)
        stream = jnp.take(table_low, inputs, axis=0).astype(jnp.float32)
        saved = []
        for layer_idx in range(L):
            weights = fetch_forward(shards, layer_idx)
            stream, kept = layer_forward(stream, weights)
            saved.append(kept)
        normed_final, scaled_final, spread_final = normalize(stream, final_float[0], final_float[1])
        normed_low = normed_final.astype(jnp.bfloat16)
        chosen = jnp.einsum(
            "bms,bsd->bmd",
            picker.astype(jnp.bfloat16),
            normed_low,
            preferred_element_type=jnp.float32,
        ).astype(jnp.bfloat16)
        logits = (
            jnp.einsum("bmd,vd->bmv", chosen, table_low, preferred_element_type=jnp.float32)
            + head_bias
        )
        peak = jnp.max(logits, -1, keepdims=True)
        log_total = peak[..., 0] + jnp.log(jnp.sum(jnp.exp(logits - peak), -1))
        picked = jnp.take_along_axis(logits, targets[:, :, None], axis=2)[..., 0]
        loss_local = loss_local + jnp.sum(valid * (log_total - picked))
        target_hot = (targets[:, :, None] == jnp.arange(V, dtype=jnp.int32)[None, None, :]).astype(
            jnp.float32
        )
        grad_logits = (
            (jnp.exp(logits - log_total[..., None]) - target_hot) * (valid * inverse)[..., None]
        ).astype(jnp.bfloat16)
        grad_bias = grad_bias + jnp.sum(grad_logits.astype(jnp.float32), (0, 1))
        head_table = jnp.einsum(
            "bmv,bmd->vd", grad_logits, chosen, preferred_element_type=jnp.float32
        )
        grad_chosen = jnp.einsum(
            "bmv,vd->bmd", grad_logits, table_low, preferred_element_type=jnp.float32
        )
        grad_normed = jnp.einsum("bms,bmd->bsd", picker, grad_chosen, precision=highest)
        upstream, grad_gain_final, grad_shift_final = normalize_back(
            grad_normed, scaled_final, spread_final, final_float[0]
        )
        grad_final = grad_final + jnp.stack([grad_gain_final, grad_shift_final])
        for layer_idx in reversed(range(L)):
            weights = fetch_backward(shards, layer_idx)
            upstream, layer_grads = layer_backward(upstream, weights, saved[layer_idx])
            summed = tuple(
                (earlier + latest for earlier, latest in zip(grad_layers[layer_idx], layer_grads))
            )
            grad_layers[layer_idx] = summed
        embed_grad = jax.ops.segment_sum(
            upstream.reshape(-1, D), inputs.reshape(-1), num_segments=V
        )
        grad_table = grad_table + head_table + embed_grad
    stacked = [
        jnp.stack([grad_layers[layer_idx][member] for layer_idx in range(L)]) for member in range(5)
    ]
    shares = (
        lax.psum_scatter(grad_table, ("dp", "fsdp"), scatter_dimension=1, tiled=True),
        lax.psum_scatter(grad_final, ("dp", "fsdp"), scatter_dimension=1, tiled=True),
        lax.psum_scatter(stacked[0], ("dp", "fsdp"), scatter_dimension=1, tiled=True),
        lax.psum_scatter(stacked[1], ("dp", "fsdp"), scatter_dimension=1, tiled=True),
        lax.psum_scatter(stacked[2], ("dp", "fsdp"), scatter_dimension=1, tiled=True),
        lax.psum_scatter(stacked[3], ("dp", "fsdp"), scatter_dimension=1, tiled=True),
        lax.psum_scatter(stacked[4], ("dp", "fsdp"), scatter_dimension=1, tiled=True),
    )
    head_grad, loss_sum = lax.psum((grad_bias, loss_local), ("dp", "fsdp"))
    local_squares = reduce(jnp.add, [jnp.sum(share * share) for share in shares])
    squares = lax.psum(local_squares, ("dp", "fsdp"))
    grad_norm = jnp.sqrt(squares + jnp.sum(head_grad * head_grad))
    factor = jnp.minimum(1.0, clip_bound / (grad_norm + epsilon))
    params = (table, w_qkv, w_out, w_up, w_down, layer_vecs, final_norm, head_bias)
    moments = (
        moment_table,
        moment_qkv,
        moment_out,
        moment_up,
        moment_down,
        moment_vecs,
        moment_final,
        moment_bias,
    )
    averages = (
        average_table,
        average_qkv,
        average_out,
        average_up,
        average_down,
        average_vecs,
        average_final,
        average_bias,
    )
    grads = (shares[0], shares[2], shares[3], shares[4], shares[5], shares[6], shares[1], head_grad)
    results = [
        update(weight, moment, average, grad, factor)
        for weight, moment, average, grad in zip(params, moments, averages, grads)
    ]
    return (
        loss_sum,
        mask_total,
        grad_norm,
        results[0][0],
        results[1][0],
        results[2][0],
        results[3][0],
        results[4][0],
        results[5][0],
        results[6][0],
        results[7][0],
        results[0][1],
        results[1][1],
        results[2][1],
        results[3][1],
        results[4][1],
        results[5][1],
        results[6][1],
        results[7][1],
        results[0][2],
        results[1][2],
        results[2][2],
        results[3][2],
        results[4][2],
        results[5][2],
        results[6][2],
        results[7][2],
    )


def solution(mesh):
    return jax.shard_map(
        body,
        mesh=mesh,
        in_specs=(
            P(("dp", "fsdp"), None),
            P(("dp", "fsdp"), None),
            P(("dp", "fsdp")),
            P(None, ("dp", "fsdp")),
            P(None, ("dp", "fsdp"), None),
            P(None, ("dp", "fsdp"), None),
            P(None, ("dp", "fsdp"), None),
            P(None, ("dp", "fsdp"), None),
            P(None, ("dp", "fsdp")),
            P(None, ("dp", "fsdp")),
            P(),
            P(None, ("dp", "fsdp")),
            P(None, ("dp", "fsdp"), None),
            P(None, ("dp", "fsdp"), None),
            P(None, ("dp", "fsdp"), None),
            P(None, ("dp", "fsdp"), None),
            P(None, ("dp", "fsdp")),
            P(None, ("dp", "fsdp")),
            P(),
            P(None, ("dp", "fsdp")),
            P(None, ("dp", "fsdp"), None),
            P(None, ("dp", "fsdp"), None),
            P(None, ("dp", "fsdp"), None),
            P(None, ("dp", "fsdp"), None),
            P(None, ("dp", "fsdp")),
            P(None, ("dp", "fsdp")),
            P(),
        ),
        out_specs=(
            P(),
            P(),
            P(),
            P(None, ("dp", "fsdp")),
            P(None, ("dp", "fsdp"), None),
            P(None, ("dp", "fsdp"), None),
            P(None, ("dp", "fsdp"), None),
            P(None, ("dp", "fsdp"), None),
            P(None, ("dp", "fsdp")),
            P(None, ("dp", "fsdp")),
            P(),
            P(None, ("dp", "fsdp")),
            P(None, ("dp", "fsdp"), None),
            P(None, ("dp", "fsdp"), None),
            P(None, ("dp", "fsdp"), None),
            P(None, ("dp", "fsdp"), None),
            P(None, ("dp", "fsdp")),
            P(None, ("dp", "fsdp")),
            P(),
            P(None, ("dp", "fsdp")),
            P(None, ("dp", "fsdp"), None),
            P(None, ("dp", "fsdp"), None),
            P(None, ("dp", "fsdp"), None),
            P(None, ("dp", "fsdp"), None),
            P(None, ("dp", "fsdp")),
            P(None, ("dp", "fsdp")),
            P(),
        ),
        check_vma=False,
    )
```

profile of v0, /device:TPU:0, one launch (start us, length us, event | category | flops | bytes accessed | tf_op | source)
XLA Modules:
  0.0 1741.0 jit_solution(11908599807452092291)
XLA Ops:
  22.5 42.7 %all-reduce.4 = (bf16[9216]{0:T(1024)(128)(2,1)S(1)}, bf16[9216]{0:T(1024)(128)(2,1)S(1)}) all-reduce(bf16[9216]{0:T(1024)(128)(2,1)S(1)} %dynamic-update-slice, bf16[9216]{0:T(1024)(128)(2,1)S(1)} %dynamic-update-slice.1), channel_id=2, replica_groups=mesh['dp'=8,'fsdp'=4] {'dp','fsdp'}, use_global_device_ids=true, to_apply=%add | all-reduce | flops 18432 | bytes 73728
  67.7 40.7 %psum.29 = f32[]{:T(128)} all-reduce(f32[]{:T(128)} %convert_reduce_fusion.20), channel_id=1, replica_groups=mesh['dp'=8,'fsdp'=4] {'dp','fsdp'}, use_global_device_ids=true, to_apply=%region_38.42 | all-reduce | flops 1 | bytes 8 | tf_op jit(solution)/shard_map/psum | solution.py:277
  115.3 41.0 %all-gather.10 = bf16[32,24,2]{1,2,0:T(2,128)(2,1)S(1)} all-gather(bf16[1,24,2]{1,2,0:T(2,128)(2,1)S(1)} %convert_bitcast_fusion), channel_id=1, replica_groups=mesh['dp'=8,'fsdp'=4] {'dp','fsdp'}, dimensions={0}, use_global_device_ids=true | all-gather | bytes 3168 | tf_op jit(solution)/shard_map/all_gather | solution.py:296
  157.8 3.8 copy.231
  168.2 3.4 fusion.49
  183.6 9.4 all-gather.25.cloned.1.call-done
  201.0 58.0 %all-gather.27.cloned.1.call-done = bf16[1,768,3072]{2,1,0:T(8,128)(2,1)} async-done(((bf16[1,24,3072]{2,1,0:T(8,128)(2,1)}), bf16[1,768,3072]{2,1,0:T(8,128)(2,1)}) %all-gather.27.cloned.1.call-update) | async-done | bytes 4718608 | tf_op jit(solution)/shard_map/all_gather | solution.py:67
  259.0 5.8 fusion.32
  264.8 60.0 %all-gather.29.cloned.1.call-done = bf16[1,3072,768]{2,1,0:T(8,128)(2,1)} async-done(((bf16[1,96,768]{2,1,0:T(8,128)(2,1)}), bf16[1,3072,768]{2,1,0:T(8,128)(2,1)}) %all-gather.29.cloned.1.call-update) | async-done | bytes 4718608 | tf_op jit(solution)/shard_map/all_gather | solution.py:68
  324.8 5.7 fusion.388
  332.2 54.8 %all-gather.31.cloned.1.call-done = bf16[1,768,2304]{2,1,0:T(8,128)(2,1)} async-done(((bf16[1,24,2304]{2,1,0:T(8,128)(2,1)}), bf16[1,768,2304]{2,1,0:T(8,128)(2,1)}) %all-gather.31.cloned.1.call-update) | async-done | bytes 3538960 | tf_op jit(solution)/shard_map/all_gather | solution.py:65
  387.0 3.4 fusion.50
  402.0 40.7 %all-gather.33.cloned.1.call-done = bf16[1,768,768]{2,1,0:T(8,128)(2,1)} async-done(((bf16[1,24,768]{2,1,0:T(8,128)(2,1)}), bf16[1,768,768]{2,1,0:T(8,128)(2,1)}) %all-gather.33.cloned.1.call-update) | async-done | bytes 1179664 | tf_op jit(solution)/shard_map/all_gather | solution.py:66
  446.7 62.1 %all-gather.35.cloned.1.call-done = bf16[1,768,3072]{2,1,0:T(8,128)(2,1)} async-done(((bf16[1,24,3072]{2,1,0:T(8,128)(2,1)}), bf16[1,768,3072]{2,1,0:T(8,128)(2,1)}) %all-gather.35.cloned.1.call-update) | async-done | bytes 4718608 | tf_op jit(solution)/shard_map/all_gather | solution.py:67
  508.8 5.7 fusion.38
  514.6 60.2 %all-gather.37.cloned.1.call-done = bf16[1,3072,768]{2,1,0:T(8,128)(2,1)} async-done(((bf16[1,96,768]{2,1,0:T(8,128)(2,1)}), bf16[1,3072,768]{2,1,0:T(8,128)(2,1)}) %all-gather.37.cloned.1.call-update) | async-done | bytes 4718608 | tf_op jit(solution)/shard_map/all_gather | solution.py:68
  574.8 5.6 fusion.390
  581.7 2.9 fusion.391
  584.6 2.9 gather_fusion.2
  593.4 3.3 fusion.398
  599.6 3.9 fusion.35
  638.0 3.2 fusion.399
  643.9 6.7 convert_reduce_fusion.1
  653.6 3.8 convert_reduce_fusion
  666.0 3.5 convolution_convert_fusion.6
  692.1 3.8 convert_reduce_fusion.3
  699.9 3.8 convert_reduce_fusion.2
  712.3 3.5 convolution_convert_fusion.4
  748.2 4.9 pad_maximum_fusion.3
  757.6 3.6 convolution_add_fusion.4
  761.3 10.1 scatter_custom_fusion
  771.3 6.7 copy.284
  783.2 4.2 add_bitcast_fusion.5
  787.4 4.3 add_bitcast_fusion.4
  791.7 11.4 pad_maximum_fusion.2
  804.2 3.0 fusion.353
  812.3 6.8 pad_maximum_fusion
  820.2 4.5 fusion.253
  827.0 3.5 add_bitcast_fusion.1
  830.4 4.5 add_bitcast_fusion
  834.9 6.9 pad_maximum_fusion.1
  843.8 39.6 %all-reduce.2 = f32[2,768]{1,0:T(2,128)S(1)} all-reduce(f32[2,768]{1,0:T(2,128)S(1)} %maximum_add_fusion), channel_id=13, replica_groups=mesh['dp'=8,'fsdp'=4] {'dp','fsdp'}, use_global_device_ids=true, to_apply=%region_70.74.clone | all-reduce | flops 1536 | bytes 12288
  885.8 80.9 %reduce-scatter.14.cloned.1.call-done = f32[2,24,768]{2,1,0:T(8,128)} async-done(((f32[2,768,768]{2,1,0:T(8,128)}), f32[2,24,768]{2,1,0:T(8,128)}) %reduce-scatter.14.cloned.1.call-update) | async-done | bytes 147472 | tf_op jit(solution)/shard_map/reduce_scatter | solution.py:364
  968.3 117.7 %reduce-scatter.20.cloned.1.call-done = f32[24,2026]{1,0:T(8,128)} async-done(((f32[768,2026]{1,0:T(8,128)}), f32[24,2026]{1,0:T(8,128)}) %reduce-scatter.20.cloned.1.call-update) | async-done | bytes 194512
  1089.5 165.6 %reduce-scatter.12.cloned.1.call-done = f32[2,24,2304]{2,1,0:T(8,128)} async-done(((f32[2,768,2304]{2,1,0:T(8,128)}), f32[2,24,2304]{2,1,0:T(8,128)}) %reduce-scatter.12.cloned.1.call-update) | async-done | bytes 442384 | tf_op jit(solution)/shard_map/reduce_scatter | solution.py:363
  1258.2 208.2 %reduce-scatter.16.cloned.1.call-done = f32[2,24,3072]{2,1,0:T(8,128)} async-done(((f32[2,768,3072]{2,1,0:T(8,128)}), f32[2,24,3072]{2,1,0:T(8,128)}) %reduce-scatter.16.cloned.1.call-update) | async-done | bytes 589840 | tf_op jit(solution)/shard_map/reduce_scatter | solution.py:365
  1469.0 208.7 %reduce-scatter.18.cloned.1.call-done = f32[2,96,768]{2,1,0:T(8,128)} async-done(((f32[2,3072,768]{2,1,0:T(8,128)}), f32[2,96,768]{2,1,0:T(8,128)}) %reduce-scatter.18.cloned.1.call-update) | async-done | bytes 589840 | tf_op jit(solution)/shard_map/reduce_scatter | solution.py:366
  1680.8 39.3 %all-reduce.3 = (f32[]{:T(128)}, f32[]{:T(128)}, f32[2026]{0:T(1024)S(1)}) all-reduce(f32[]{:T(128)S(6)} %add.749, f32[]{:T(128)S(6)} %add.776, f32[2026]{0:T(1024)S(1)} %add.777), channel_id=1, replica_groups=mesh['dp'=8,'fsdp'=4] {'dp','fsdp'}, use_global_device_ids=true, to_apply=%region_36.40 | all-reduce | flops 2028 | bytes 16224 | tf_op jit(solution)/shard_map/psum | solution.py:369
  (1005 shorter events, 235.0 us)
Async XLA Ops:
  7.2 10.8 copy-start.316
  7.2 13.3 copy-start.309
  7.2 13.5 copy-start.297
  7.2 14.6 copy-start.287
  7.3 101.1 %copy-start.317 = (f32[2,24]{1,0:T(2,128)S(1)}, f32[2,24]{1,0:T(2,128)}, u32[]{:S(2)}) copy-start(f32[2,24]{1,0:T(2,128)} %param.42) | copy-start | bytes 580
  7.3 150.5 %all-gather.21.cloned.1.call-start = ((), (), s32[]{:S(2)}) async-start(), calls=%async_computation.6 | async-start | bytes 3244032 | tf_op jit(solution)/shard_map/all_gather | solution.py:295
  9.0 159.1 %all-gather.23.cloned.1.call-start = ((), (), s32[]{:S(2)}) async-start(), calls=%async_computation.11 | async-start | bytes 3649536 | tf_op jit(solution)/shard_map/all_gather | solution.py:65
  10.8 182.2 %all-gather.25.cloned.1.call-start = ((), (), s32[]{:S(2)}) async-start(), calls=%async_computation.12 | async-start | bytes 1216512 | tf_op jit(solution)/shard_map/all_gather | solution.py:66
  12.4 246.5 %all-gather.27.cloned.1.call-start = ((), (), s32[]{:S(2)}) async-start(), calls=%async_computation.13 | async-start | bytes 4866048 | tf_op jit(solution)/shard_map/all_gather | solution.py:67
  14.3 310.4 %all-gather.29.cloned.1.call-start = ((), (), s32[]{:S(2)}) async-start(), calls=%async_computation.14 | async-start | bytes 4866048 | tf_op jit(solution)/shard_map/all_gather | solution.py:68
  15.2 371.8 %all-gather.31.cloned.1.call-start = ((), (), s32[]{:S(2)}) async-start(), calls=%async_computation.15 | async-start | bytes 3649536 | tf_op jit(solution)/shard_map/all_gather | solution.py:65
  15.8 427.0 %all-gather.33.cloned.1.call-start = ((), (), s32[]{:S(2)}) async-start(), calls=%async_computation.16 | async-start | bytes 1216512 | tf_op jit(solution)/shard_map/all_gather | solution.py:66
  16.5 492.3 %all-gather.35.cloned.1.call-start = ((), (), s32[]{:S(2)}) async-start(), calls=%async_computation.17 | async-start | bytes 4866048 | tf_op jit(solution)/shard_map/all_gather | solution.py:67
  17.3 557.5 %all-gather.37.cloned.1.call-start = ((), (), s32[]{:S(2)}) async-start(), calls=%async_computation.18 | async-start | bytes 4866048 | tf_op jit(solution)/shard_map/all_gather | solution.py:68
  18.0 866.2 %reduce-scatter.22.cloned.1.call-start = ((), (), s32[]{:S(2)}) async-start(), calls=%async_computation.20 | async-start | bytes 4866048
  21.3 146.5 %copy-start.237 = (pred[256]{0:T(512)(128)(4,1)}, pred[256]{0:T(512)(128)(4,1)S(1)}, u32[]{:S(2)}) copy-start(pred[256]{0:T(512)(128)(4,1)S(1)} %get-tuple-element.251) | copy-start | bytes 772
  631.4 9.8 copy-start.291
  642.6 10.9 slice-start.12
  643.8 15.9 copy-start.57
  643.9 9.7 slice-start.13
  691.4 14.6 copy-start.55
  727.0 14.8 copy-start.130
  729.6 12.3 copy-start.108
  731.1 10.8 copy-start.110
  748.2 218.5 %reduce-scatter.14.cloned.1.call-start = ((), (), s32[]{:S(2)}) async-start(), calls=%async_computation.8 | async-start | bytes 4866048 | tf_op jit(solution)/shard_map/reduce_scatter | solution.py:364
  753.2 332.8 %reduce-scatter.20.cloned.1.call-start = ((), (), s32[]{:S(2)}) async-start(), calls=%async_computation.19 | async-start | bytes 6488064
  778.1 477.0 %reduce-scatter.12.cloned.1.call-start = ((), (), s32[]{:S(2)}) async-start(), calls=%async_computation.7 | async-start | bytes 14598144 | tf_op jit(solution)/shard_map/reduce_scatter | solution.py:363
  803.2 663.2 %reduce-scatter.16.cloned.1.call-start = ((), (), s32[]{:S(2)}) async-start(), calls=%async_computation.9 | async-start | bytes 19464192 | tf_op jit(solution)/shard_map/reduce_scatter | solution.py:365
  819.1 858.5 %reduce-scatter.18.cloned.1.call-start = ((), (), s32[]{:S(2)}) async-start(), calls=%async_computation.10 | async-start | bytes 19464192 | tf_op jit(solution)/shard_map/reduce_scatter | solution.py:366
  841.9 880.2 %copy-start.318 = (f32[2,24]{1,0:T(2,128)S(1)}, f32[2,24]{1,0:T(2,128)}, u32[]{:S(2)}) copy-start(f32[2,24]{1,0:T(2,128)} %param.42) | copy-start | bytes 580
  841.9 880.2 %copy-start.319 = (f32[2,24]{1,0:T(2,128)S(1)}, f32[2,24]{1,0:T(2,128)}, u32[]{:S(2)}) copy-start(f32[2,24]{1,0:T(2,128)} %param.58) | copy-start | bytes 580
  841.9 880.2 %copy-start.320 = (f32[2,24]{1,0:T(2,128)S(1)}, f32[2,24]{1,0:T(2,128)}, u32[]{:S(2)}) copy-start(f32[2,24]{1,0:T(2,128)} %param.50) | copy-start | bytes 580
  841.9 880.8 %copy-start.288 = (f32[2,288]{1,0:T(2,128)S(1)}, f32[2,288]{1,0:T(2,128)}, u32[]{:S(2)}) copy-start(f32[2,288]{1,0:T(2,128)} %param.41) | copy-start | bytes 6916
  841.9 880.8 %copy-start.314 = (f32[2,288]{1,0:T(2,128)S(1)}, f32[2,288]{1,0:T(2,128)}, u32[]{:S(2)}) copy-start(f32[2,288]{1,0:T(2,128)} %param.57) | copy-start | bytes 6916
  841.9 880.8 %copy-start.315 = (f32[2,288]{1,0:T(2,128)S(1)}, f32[2,288]{1,0:T(2,128)}, u32[]{:S(2)}) copy-start(f32[2,288]{1,0:T(2,128)} %param.49) | copy-start | bytes 6916
  841.9 881.4 %copy-start.186 = (f32[2026]{0:T(1024)S(1)}, f32[2026]{0:T(1024)}, u32[]{:S(2)}) copy-start(f32[2026]{0:T(1024)} %param.43) | copy-start | bytes 24316
  841.9 881.4 %copy-start.295 = (f32[2026]{0:T(1024)S(1)}, f32[2026]{0:T(1024)}, u32[]{:S(2)}) copy-start(f32[2026]{0:T(1024)} %param.59) | copy-start | bytes 24316
  842.0 881.4 %copy-start.296 = (f32[2026]{0:T(1024)S(1)}, f32[2026]{0:T(1024)}, u32[]{:S(2)}) copy-start(f32[2026]{0:T(1024)} %param.51) | copy-start | bytes 24316
  842.0 882.0 %copy-start.156 = (f32[2,24,768]{2,1,0:T(8,128)S(1)}, f32[2,24,768]{2,1,0:T(8,128)}, u32[]{:S(2)}) copy-start(f32[2,24,768]{2,1,0:T(8,128)} %param.38) | copy-start | bytes 442372
  842.0 882.0 %copy-start.183 = (f32[2,24,768]{2,1,0:T(8,128)S(1)}, f32[2,24,768]{2,1,0:T(8,128)}, u32[]{:S(2)}) copy-start(f32[2,24,768]{2,1,0:T(8,128)} %param.54) | copy-start | bytes 442372
  842.0 883.7 %copy-start.153 = (f32[2026,24]{0,1:T(8,128)S(1)}, f32[2026,24]{0,1:T(8,128)}, u32[]{:S(2)}) copy-start(f32[2026,24]{0,1:T(8,128)} %param.36) | copy-start | bytes 583492
  842.0 883.7 %copy-start.181 = (f32[2026,24]{0,1:T(8,128)S(1)}, f32[2026,24]{0,1:T(8,128)}, u32[]{:S(2)}) copy-start(f32[2026,24]{0,1:T(8,128)} %param.52) | copy-start | bytes 583492
  842.0 883.6 %copy-start.182 = (f32[2026,24]{0,1:T(8,128)S(1)}, f32[2026,24]{0,1:T(8,128)}, u32[]{:S(2)}) copy-start(f32[2026,24]{0,1:T(8,128)} %param.44) | copy-start | bytes 583492
  966.6 757.3 %copy-start.157 = (f32[2,24,768]{2,1,0:T(8,128)S(1)}, f32[2,24,768]{2,1,0:T(8,128)}, u32[]{:S(2)}) copy-start(f32[2,24,768]{2,1,0:T(8,128)} %reduce-scatter.14.cloned.1.call-done) | copy-start | bytes 442372
  1086.0 639.7 %copy-start.152 = (f32[24,2026]{1,0:T(8,128)S(1)}, f32[24,2026]{1,0:T(8,128)}, u32[]{:S(2)}) copy-start(f32[24,2026]{1,0:T(8,128)} %reduce-scatter.20.cloned.1.call-done) | copy-start | bytes 583492
  1086.0 640.5 %copy-start.141 = (f32[2,24,2304]{2,1,0:T(8,128)S(1)}, f32[2,24,2304]{2,1,0:T(8,128)}, u32[]{:S(2)}) copy-start(f32[2,24,2304]{2,1,0:T(8,128)} %param.37) | copy-start | bytes 1327108
  1468.2 260.9 %copy-start.133 = (f32[2,24,3072]{2,1,0:T(8,128)S(1)}, f32[2,24,3072]{2,1,0:T(8,128)}, u32[]{:S(2)}) copy-start(f32[2,24,3072]{2,1,0:T(8,128)} %param.39) | copy-start | bytes 1769476
  1468.2 260.9 %copy-start.136 = (f32[2,24,3072]{2,1,0:T(8,128)S(1)}, f32[2,24,3072]{2,1,0:T(8,128)}, u32[]{:S(2)}) copy-start(f32[2,24,3072]{2,1,0:T(8,128)} %reduce-scatter.16.cloned.1.call-done) | copy-start | bytes 1769476
  (306 other events, 914.1 us)
Sparse Core Ops, SparseCore 0:
  11.5 62.3 all-gather.20
  77.4 59.2 all-gather.22
  140.2 52.8 all-gather.24
  196.4 62.5 all-gather.26
  262.3 62.4 all-gather.28
  328.1 58.8 all-gather.30
  389.9 52.8 all-gather.32
  446.2 62.5 all-gather.34
  512.3 62.4 all-gather.36
  748.3 105.7 reduce-scatter.21
  860.5 106.1 reduce-scatter.13
  972.1 113.8 reduce-scatter.19
  1093.0 162.0 reduce-scatter.11
  1262.5 203.8 reduce-scatter.15
  1473.8 203.8 reduce-scatter.17
where the time goes:
time: 1750 us; the launch traced here: 1740 us
  waiting for transfers between devices  1130 us (65%)
  blocking collectives  203 us (12%)
  matrix products  179 us (10%)
  other arithmetic  116 us (7%)
  local copies, waits for them, and re-layouts  85.1 us (5%)
  between operations  27.5 us (2%)
    reduce_scatter x1, waiting for transfers between devices, body(): lax.psum_scatter(stacked[3], ('dp', 'fsdp'), scatter_dimension=1, tiled=T...  209 us
    reduce_scatter x1, waiting for transfers between devices, body(): lax.psum_scatter(stacked[2], ('dp', 'fsdp'), scatter_dimension=1, tiled=T...  208 us
    reduce_scatter x1, waiting for transfers between devices, body(): lax.psum_scatter(stacked[0], ('dp', 'fsdp'), scatter_dimension=1, tiled=T...  166 us
    unnamed x17, waiting for transfers between devices  121 us
    all_gather x2, waiting for transfers between devices, fetch_forward(): lax.all_gather(down_part, ('dp', 'fsdp'), axis=0, tiled=True)  120 us
    all_gather x2, waiting for transfers between devices, fetch_forward(): lax.all_gather(up_part, ('dp', 'fsdp'), axis=0, tiled=True)  120 us
    unnamed x2, blocking collectives  82.3 us
    reduce_scatter x1, waiting for transfers between devices, body(): lax.psum_scatter(stacked[1], ('dp', 'fsdp'), scatter_dimension=1, tiled=T...  80.9 us
  transfers between devices with their start and end apart: 15, of which 12 were waited for; matrix products, arithmetic and copies ran while one was open for 11% of the time, Pallas kernels for 0%

commit v1 on v0

v1 whole, which is shorter than its diff:
```python
from functools import partial, reduce

import jax
import jax.numpy as jnp
from jax import lax
from jax.experimental import pallas as pl
from jax.experimental.pallas import tpu as pltpu
from jax.sharding import PartitionSpec as P

D = 768
HEADS = 12
HEAD_DIM = 64
FF = 3072
V = 2026
M = 128
L = 2
UNIT = 384
VPAD = 2304
BOTH = ("dp", "fsdp")


epsilon = 1e-06
step_rate = 10000.0
inertia = 0.5
average_decay = 0.5
clip_bound = 0.01


HOPS = {
    "zhi": ("dp", 4, 8, 0),
    "zlo": ("dp", 2, 8, 1),
    "y": ("dp", 1, 8, 2),
    "x": ("fsdp", 2, 4, 3),
    "core": ("fsdp", 1, 4, None),
}


def swap(tensor, hop):
    axis, flip, size, unused = HOPS[hop]
    return lax.ppermute(tensor, axis, [(i, i ^ flip) for i in range(size)])


def side(hop):
    axis, flip, unused, unused = HOPS[hop]
    return (lax.axis_index(axis) // flip) % 2


def in_order(bit, own, other, axis):
    return jnp.where(
        bit == 0, jnp.concatenate([own, other], axis), jnp.concatenate([other, own], axis)
    )


def pick(tensor, index, axis):
    return lax.dynamic_slice_in_dim(tensor, index, 1, axis)


def gather_chips(tensor, order):
    tensor = tensor[None, None, None, None]
    for hop in order:
        tensor = in_order(side(hop), tensor, swap(tensor, hop), HOPS[hop][3])
    return tensor


def scatter_chips(parts, order):
    for hop in order:
        axis, bit = HOPS[hop][3], side(hop)
        leaving = reduce(jnp.add, [pick(part, 1 - bit, axis).astype(jnp.float32) for part in parts])
        arrived = swap(leaving.astype(jnp.bfloat16), hop)
        parts = [pick(part, bit, axis) for part in parts] + [arrived]
    return reduce(jnp.add, [part.astype(jnp.float32) for part in parts])[0, 0, 0, 0]


def column_units(shard):
    rows, columns = shard.shape
    return shard.reshape(rows, 2, columns // (2 * UNIT), UNIT).transpose(1, 2, 0, 3)


PIECES = {
    "table": [(3, 24)],
    "attention": [(3, 24), (1, 24)],
    "forward": [(1, 96), (4, 24)],
}


def natural_weight(halves, offset, units, rows):
    chips = halves.shape[1]
    block = halves[:, :, offset : offset + units * rows].reshape(2, chips, units, rows, UNIT)
    return block.transpose(1, 3, 0, 2, 4).reshape(chips * rows, 2 * units * UNIT)


def weight_blocks(grad, units, rows):
    chips = grad.shape[0] // rows
    block = grad.reshape(chips, rows, 2, units, UNIT).transpose(2, 0, 3, 1, 4)
    return block.reshape(2, chips, units * rows, UNIT)


TOKENS = 512
SLOTS = 256
ANY = pl.BlockSpec(memory_space=pl.ANY)
SMEM = pl.BlockSpec(memory_space=pltpu.SMEM)
VMEM = pl.BlockSpec(memory_space=pltpu.VMEM)
low = jnp.bfloat16
full = jnp.float32


def dot(left, right):
    return lax.dot_general(left, right, (((1,), (0,)), ((), ())), preferred_element_type=full)


def dot_right(left, right):
    return lax.dot_general(left, right, (((1,), (1,)), ((), ())), preferred_element_type=full)


def dot_left(left, right):
    return lax.dot_general(left, right, (((0,), (0,)), ((), ())), preferred_element_type=full)


def norm_parts(stream):
    centre = stream - jnp.mean(stream, -1, keepdims=True)
    spread = lax.rsqrt(jnp.mean(centre * centre, -1, keepdims=True) + epsilon)
    return centre * spread, spread


def norm_back(upstream, scaled, spread, gain):
    weighted = upstream * gain
    return spread * (
        weighted
        - jnp.mean(weighted, -1, keepdims=True)
        - scaled * jnp.mean(weighted * scaled, -1, keepdims=True)
    )


def rows_sum(tensor):
    return jnp.sum(tensor, 0, keepdims=True)


def columns(start, size):
    return pl.ds(pl.multiple_of(start, 128), size)


def unit_copies(core, halves, at, units, target, sems):
    copies = []
    for which, source in enumerate(halves):
        half = core if which == 0 else 1 - core
        for unit in range(units):
            copies.append(
                pltpu.make_async_copy(
                    source.at[:, pl.ds(at + 48 * unit, 48), :],
                    target.at[:, :, columns((half * units + unit) * UNIT, UNIT)],
                    sems.at[which * units + unit],
                )
            )
    return copies


def flat(block):
    return block.reshape(block.shape[0] * block.shape[1], block.shape[2])


def head_mask(shape, which):
    lane = lax.broadcasted_iota(jnp.int32, shape, 1)
    return lane < HEAD_DIM if which == 0 else lane >= HEAD_DIM


def embed_kernel(at, core, codes, pos, valid, mine, yours, ids, stream, weight, sems):
    copies = unit_copies(core[0], (mine, yours), at, 3, weight, sems)
    for copy in copies:
        copy.start()
    place = lax.broadcasted_iota(jnp.int32, (TOKENS, SLOTS), 0)
    masked = jnp.max(jnp.where(place == pos[...], valid[...], 0.0), -1, keepdims=True)
    tokens = jnp.where(masked > 0, V - 1, codes[...])
    ids[...] = tokens
    for copy in copies:
        copy.wait()
    acc = jnp.zeros((TOKENS, D), full)
    for tile in range(3):
        word = lax.broadcasted_iota(jnp.int32, (TOKENS, D), 1) + tile * D
        hot = jnp.where(word == tokens, 1.0, 0.0).astype(low)
        acc += dot_right(hot, flat(weight[:, :, tile * D : (tile + 1) * D]))
    stream[...] = acc


def attention_kernel(
    at, core, stream, vector, mine, yours, triple, lse, mixed, middle, w_in, w_out, sems
):
    in_copies = unit_copies(core[0], (mine, yours), at, 3, w_in, sems.at[pl.ds(0, 6)])
    out_copies = unit_copies(core[0], (mine, yours), at + 144, 1, w_out, sems.at[pl.ds(6, 2)])
    for copy in in_copies + out_copies:
        copy.start()
    scaled, unused = norm_parts(stream[...])
    normed = (scaled * vector[0:1] + vector[1:2]).astype(low)
    for copy in in_copies:
        copy.wait()
    for part in range(3):
        block = dot(normed, flat(w_in[:, :, part * D : (part + 1) * D]))
        if part == 0:
            block = block + vector[2:3]
        if part == 2:
            block = block + vector[3:4]
        triple[part] = block.astype(low)
    lse[...] = jnp.zeros_like(lse)
    shape = (256, 128)
    lane = lax.broadcasted_iota(jnp.int32, shape, 1)

    def pair(step, carry):
        here = columns(step * 128, 128)
        for image in range(2):
            rows = slice(256 * image, 256 * image + 256)
            queries, key_rows, values = triple[0, rows, here], triple[1, rows, here], triple[2, rows, here]
            results = []
            for which in range(2):
                query = jnp.where(head_mask(shape, which), queries, jnp.zeros_like(queries))
                scores = dot_right(query, key_rows) * HEAD_DIM ** (-0.5)
                peak = jnp.max(scores, -1, keepdims=True)
                raised = jnp.exp(scores - peak)
                total = jnp.sum(raised, -1, keepdims=True)
                probs = (raised * (1.0 / total)).astype(low)
                results.append(dot(probs, values))
                lse[rows] = jnp.where(lane == 2 * step + which, peak + jnp.log(total), lse[rows])
            mixed[rows, here] = jnp.where(head_mask(shape, 0), results[0], results[1]).astype(low)
        return carry

    lax.fori_loop(0, HEADS // 2, pair, 0)
    for copy in out_copies:
        copy.wait()
    middle[...] = stream[...] + dot(mixed[...], flat(w_out[...])) + vector[4:5]


def forward_copies(core, mine, yours, w_up, w_down, sems):
    up = unit_copies(core, (mine, yours), 192, 4, w_up, sems.at[pl.ds(0, 8)])
    down = []
    for tile in range(4):
        chips = pl.ds(4 * lax.rem(2 * core + tile, 4), 4)
        for which, source in enumerate((mine, yours)):
            half = core if which == 0 else 1 - core
            down.append(
                pltpu.make_async_copy(
                    source.at[chips, pl.ds(0, 192), :],
                    w_down.at[chips, :, columns(half * UNIT, UNIT)],
                    sems.at[8 + 2 * tile + which],
                )
            )
    return [up[2 * tile : 2 * tile + 2] + down[2 * tile : 2 * tile + 2] for tile in range(4)]


CURVE = 0.7978845608028654


def forward_kernel(core, middle, vector, mine, yours, hidden, result, w_up, w_down, normed, stage, sems, out_sems):
    copies = forward_copies(core[0], mine, yours, w_up, w_down, sems)
    for group in copies:
        for copy in group:
            copy.start()
    scaled, unused = norm_parts(middle[...])
    normed[...] = (scaled * vector[5:6] + vector[6:7]).astype(low)
    result[...] = middle[...] + vector[7:8]
    sent = []
    for step in range(4):
        tile = lax.rem(2 * core[0] + step, 4)
        for copy in copies[step]:
            copy.wait()
        block = dot(normed[...], flat(w_up[:, :, columns(tile * D, D)])) + vector[pl.ds(8 + tile, 1)]
        if step >= 2:
            sent[step - 2].wait()
        stage[step % 2] = block
        copy = pltpu.make_async_copy(stage.at[step % 2], hidden.at[tile], out_sems.at[step % 2])
        copy.start()
        sent.append(copy)
        bent = jnp.tanh(CURVE * (block + 0.044715 * (block * block * block)))
        active = (0.5 * block * (1.0 + bent)).astype(low)
        result[...] += dot(active, flat(w_down[pl.ds(4 * tile, 4)]))
    for copy in sent[2:]:
        copy.wait()


def head_kernel(
    at,
    core,
    stream,
    final,
    codes,
    pos_column,
    pos_row,
    scale,
    valid,
    bias,
    mine,
    yours,
    upstream,
    chosen_out,
    grad_logits_out,
    bias_grad,
    final_grad,
    loss,
    weight,
    logits,
    sems,
):
    copies = unit_copies(core[0], (mine, yours), at, 3, weight, sems)
    for copy in copies:
        copy.start()
    scaled, spread = norm_parts(stream[...])
    normed = (scaled * final[0:1] + final[1:2]).astype(low)
    picker = lax.broadcasted_iota(jnp.int32, (SLOTS, TOKENS), 1) == pos_column[...]
    target = jnp.sum(jnp.where(picker, codes[...], 0), -1, keepdims=True)
    chosen = dot(picker.astype(full).astype(low), normed).astype(low)
    chosen_out[...] = chosen
    for copy in copies:
        copy.wait()
    peak = jnp.full((SLOTS, 1), -jnp.inf, full)
    picked = jnp.zeros((SLOTS, 1), full)
    for tile in range(3):
        here = slice(tile * D, tile * D + D)
        block = dot(chosen, flat(weight[:, :, here])) + bias[:, here]
        logits[:, here] = block
        peak = jnp.maximum(peak, jnp.max(block, -1, keepdims=True))
        word = lax.broadcasted_iota(jnp.int32, (SLOTS, D), 1) + tile * D
        picked += jnp.sum(jnp.where(word == target, block, 0.0), -1, keepdims=True)
    total = jnp.zeros((SLOTS, 1), full)
    for tile in range(3):
        total += jnp.sum(jnp.exp(logits[:, tile * D : tile * D + D] - peak), -1, keepdims=True)
    log_total = peak + jnp.log(total)
    loss[...] = jnp.broadcast_to(rows_sum(valid[...] * (log_total - picked)), (1, 128))
    grad_chosen = jnp.zeros((SLOTS, D), full)
    for tile in range(3):
        here = slice(tile * D, tile * D + D)
        word = lax.broadcasted_iota(jnp.int32, (SLOTS, D), 1) + tile * D
        chance = jnp.exp(logits[:, here] - log_total)
        block = ((chance - jnp.where(word == target, 1.0, 0.0)) * scale[...]).astype(low)
        grad_logits_out[:, here] = block
        bias_grad[:, here] = rows_sum(block.astype(full))
        grad_chosen += dot_right(block, flat(weight[:, :, here]))
    back = lax.broadcasted_iota(jnp.int32, (TOKENS, SLOTS), 0) == pos_row[...]
    back = back.astype(full).astype(low)
    grad_normed = jnp.zeros((TOKENS, D), full)
    for unused in range(3):
        piece = grad_chosen.astype(low)
        grad_normed += dot(back, piece)
        grad_chosen -= piece.astype(full)
    final_grad[0:1] = rows_sum(grad_normed * scaled)
    final_grad[1:2] = rows_sum(grad_normed)
    upstream[...] = norm_back(grad_normed, scaled, spread, final[0:1])


def leave(core, half, source, keep, send, place, sem):
    @pl.when(half == core)
    def _():
        pltpu.make_async_copy(source, keep.at[place], sem).start()

    @pl.when(half != core)
    def _():
        pltpu.make_async_copy(source, send.at[place], sem).start()


def arrive(source, keep, place, sem):
    pltpu.make_async_copy(source, keep.at[place], sem).wait()


def forward_back_kernel(
    core,
    upstream,
    middle,
    vector,
    hidden,
    mine,
    yours,
    grad_middle,
    vector_grad,
    keep,
    send,
    w_up,
    w_down,
    normed_t,
    branch,
    hidden_tile,
    down_stage,
    up_stage,
    acc,
    sems,
    hidden_sems,
    out_sems,
):
    own = core[0]
    tiles = [lax.rem(2 * own + step, 4) for step in range(4)]
    fetch = [
        pltpu.make_async_copy(hidden.at[tiles[step]], hidden_tile.at[step % 2], hidden_sems.at[step % 2])
        for step in range(4)
    ]
    fetch[0].start()
    copies = forward_copies(own, mine, yours, w_up, w_down, sems)
    for group in copies:
        for copy in group:
            copy.start()
    scaled, spread = norm_parts(middle[...])
    normed_t[...] = (scaled * vector[5:6] + vector[6:7]).T.astype(low)
    branch[...] = upstream[...].astype(low)
    vector_grad[...] = jnp.zeros_like(vector_grad)
    vector_grad[7:8] = rows_sum(branch[...].astype(full))
    acc[...] = jnp.zeros_like(acc)
    every = slice(None)
    flights = []

    def land(step):
        for args in flights[step]:
            arrive(*args)

    for step in range(4):
        tile, slot = tiles[step], step % 2
        if step < 3:
            fetch[step + 1].start()
        for copy in copies[step]:
            copy.wait()
        fetch[step].wait()
        block = hidden_tile[slot]
        square = block * block
        bent = jnp.tanh(CURVE * (block + 0.044715 * (square * block)))
        active = (0.5 * block * (1.0 + bent)).astype(low)
        slope = 0.5 * (1.0 + bent) + 0.5 * block * (1.0 - bent * bent) * (
            CURVE * (1.0 + (3.0 * 0.044715) * square)
        )
        back = dot_right(branch[...], flat(w_down[pl.ds(4 * tile, 4)]))
        grad_hidden = (slope * back).astype(low)
        vector_grad[pl.ds(8 + tile, 1)] = rows_sum(grad_hidden.astype(full))
        if step >= 2:
            land(step - 2)
        grad_down = dot(active.T, branch[...]).astype(low)
        down_stage[slot] = grad_down.reshape(4, 192, D)
        flight = []
        place = (pl.ds(4 * tile, 4), pl.ds(0, 192), every)
        for which, target in enumerate((keep, send)):
            half = own if which == 0 else 1 - own
            source = down_stage.at[slot, :, :, columns(half * UNIT, UNIT)]
            sem = out_sems.at[slot, which]
            pltpu.make_async_copy(source, target.at[place], sem).start()
            flight.append((source, target, place, sem))
        grad_up = dot(normed_t[...], grad_hidden).astype(low)
        up_stage[slot] = grad_up.reshape(16, 48, D)
        target = keep if step < 2 else send
        for unit in range(2):
            source = up_stage.at[slot, :, :, pl.ds(unit * UNIT, UNIT)]
            place = (every, pl.ds(192 + 48 * (2 * slot + unit), 48), every)
            sem = out_sems.at[slot, 2 + unit]
            pltpu.make_async_copy(source, target.at[place], sem).start()
            flight.append((source, target, place, sem))
        flights.append(flight)
        acc[...] += dot_right(grad_hidden, flat(w_up[:, :, columns(tile * D, D)]))
    grad_normed = acc[...]
    scaled, spread = norm_parts(middle[...])
    vector_grad[5:6] = rows_sum(grad_normed * scaled)
    vector_grad[6:7] = rows_sum(grad_normed)
    grad_middle[...] = upstream[...] + norm_back(grad_normed, scaled, spread, vector[5:6])
    land(2)
    land(3)


def attention_back_kernel(
    at,
    core,
    grad_middle,
    stream,
    vector,
    triple,
    lse,
    mixed,
    mine,
    yours,
    upstream,
    vector_grad,
    keep,
    send,
    w_in,
    w_out,
    grad_mixed,
    grad_triple,
    stage,
    sems,
    out_sems,
):
    own = core[0]
    out_copies = unit_copies(own, (mine, yours), at + 144, 1, w_out, sems.at[pl.ds(6, 2)])
    in_copies = unit_copies(own, (mine, yours), at, 3, w_in, sems.at[pl.ds(0, 6)])
    for copy in out_copies + in_copies:
        copy.start()
    every = slice(None)
    grad_out_low = grad_middle[...].astype(low)
    vector_grad[...] = jnp.zeros_like(vector_grad)
    vector_grad[4:5] = rows_sum(grad_out_low.astype(full))
    stage[3] = dot(mixed[...].T, grad_out_low).astype(low).reshape(16, 48, D)
    for half in range(2):
        source = stage.at[3, :, :, pl.ds(half * UNIT, UNIT)]
        leave(own, half, source, keep, send, (every, pl.ds(at + 144, 48), every), out_sems.at[6 + half])
    for copy in out_copies:
        copy.wait()
    grad_mixed[...] = dot_right(grad_out_low, flat(w_out[...])).astype(low)
    shape = (256, 128)
    lane = lax.broadcasted_iota(jnp.int32, shape, 1)

    def pair(step, carry):
        here = columns(step * 128, 128)
        for image in range(2):
            rows = slice(256 * image, 256 * image + 256)
            queries, key_rows, values = triple[0, rows, here], triple[1, rows, here], triple[2, rows, here]
            grads = grad_mixed[rows, here]
            outs = []
            for which in range(2):
                mask = head_mask(shape, which)
                none = jnp.zeros_like(queries)
                scores = dot_right(jnp.where(mask, queries, none), key_rows) * HEAD_DIM ** (-0.5)
                total = jnp.sum(jnp.where(lane == 2 * step + which, lse[rows], 0.0), -1, keepdims=True)
                probs = jnp.exp(scores - total)
                grad_values = dot_left(probs.astype(low), grads)
                grad_probs = dot_right(jnp.where(mask, grads, none), values)
                inner = jnp.sum(probs * grad_probs, -1, keepdims=True)
                grad_scores = (probs * (grad_probs - inner)).astype(low)
                grad_queries = dot(grad_scores, key_rows) * HEAD_DIM ** (-0.5)
                grad_keys = dot_left(grad_scores, queries) * HEAD_DIM ** (-0.5)
                outs.append((grad_queries, grad_keys, grad_values))
            first = head_mask(shape, 0)
            for part in range(3):
                grad_triple[part, rows, here] = jnp.where(first, outs[0][part], outs[1][part]).astype(low)
        return carry

    lax.fori_loop(0, HEADS // 2, pair, 0)
    scaled, spread = norm_parts(stream[...])
    normed_t = (scaled * vector[0:1] + vector[1:2]).T.astype(low)
    for copy in in_copies:
        copy.wait()
    grad_normed = jnp.zeros((TOKENS, D), full)
    for part in range(3):
        block = grad_triple[part]
        if part == 0:
            vector_grad[2:3] = rows_sum(block.astype(full))
        if part == 2:
            vector_grad[3:4] = rows_sum(block.astype(full))
        stage[part] = dot(normed_t, block).astype(low).reshape(16, 48, D)
        for side_unit in range(2):
            unit = 2 * part + side_unit
            source = stage.at[part, :, :, pl.ds(side_unit * UNIT, UNIT)]
            place = (every, pl.ds(at + 48 * (unit % 3), 48), every)
            leave(own, unit // 3, source, keep, send, place, out_sems.at[unit])
        grad_normed += dot_right(block, flat(w_in[:, :, part * D : (part + 1) * D]))
    vector_grad[0:1] = rows_sum(grad_normed * scaled)
    vector_grad[1:2] = rows_sum(grad_normed)
    upstream[...] = grad_middle[...] + norm_back(grad_normed, scaled, spread, vector[0:1])
    for unit in range(6):
        source = stage.at[unit // 2, :, :, pl.ds((unit % 2) * UNIT, UNIT)]
        arrive(source, keep, (every, pl.ds(at + 48 * (unit % 3), 48), every), out_sems.at[unit])
    for half in range(2):
        source = stage.at[3, :, :, pl.ds(half * UNIT, UNIT)]
        arrive(source, keep, (every, pl.ds(at + 144, 48), every), out_sems.at[6 + half])


def embed_back_kernel(
    core, upstream, ids, chosen, grad_logits, small, keep_in, send_in, keep, send, stage, sems
):
    own = core[0]
    every = slice(None)
    for which, target in enumerate((keep, send)):
        half = own if which == 0 else 1 - own
        pltpu.make_async_copy(small.at[half], target.at[:, pl.ds(144, 16), :], sems.at[6 + which]).start()
    stream_t = upstream[...].T.astype(low)
    chosen_t = chosen[...].astype(full).T.astype(low)
    for tile in range(3):
        word = lax.broadcasted_iota(jnp.int32, (TOKENS, D), 1) + tile * D
        hot = jnp.where(word == ids[...], 1.0, 0.0).astype(low)
        block = dot(stream_t, hot) + dot(chosen_t, grad_logits[:, tile * D : tile * D + D])
        stage[tile] = block.astype(low).reshape(16, 48, D)
        for side_unit in range(2):
            unit = 2 * tile + side_unit
            source = stage.at[tile, :, :, pl.ds(side_unit * UNIT, UNIT)]
            place = (every, pl.ds(48 * (unit % 3), 48), every)
            leave(own, unit // 3, source, keep, send, place, sems.at[unit])
    for unit in range(6):
        source = stage.at[unit // 2, :, :, pl.ds((unit % 2) * UNIT, UNIT)]
        arrive(source, keep, (every, pl.ds(48 * (unit % 3), 48), every), sems.at[unit])
    for which, target in enumerate((keep, send)):
        half = own if which == 0 else 1 - own
        pltpu.make_async_copy(small.at[half], target.at[:, pl.ds(144, 16), :], sems.at[6 + which]).wait()


def shape_of(*dims, kind=full):
    return jax.ShapeDtypeStruct(dims, kind)


def call(kernel, outs, out_specs, in_specs, scratch, flops, moved, **more):
    return pl.pallas_call(
        kernel,
        out_shape=outs,
        in_specs=in_specs,
        out_specs=out_specs,
        scratch_shapes=scratch,
        compiler_params=pltpu.CompilerParams(vmem_limit_bytes=56 * 2**20),
        cost_estimate=pl.CostEstimate(flops=flops, bytes_accessed=moved, transcendentals=0),
        **more,
    )


DMA = pltpu.SemaphoreType.DMA
MEG = 10**6
GIG = 10**9


def embed(core, codes, pos, valid, mine, yours, at):
    return call(
        partial(embed_kernel, at),
        (shape_of(TOKENS, 1, kind=jnp.int32), shape_of(TOKENS, D)),
        (VMEM, VMEM),
        [SMEM, VMEM, VMEM, VMEM, ANY, ANY],
        [pltpu.VMEM((16, 48, VPAD), low), DMA((6,))],
        3 * GIG,
        5 * MEG,
    )(core, codes, pos, valid, mine, yours)


def attention(core, stream, vector, mine, yours, at):
    return call(
        partial(attention_kernel, at),
        (
            shape_of(3, TOKENS, D, kind=low),
            shape_of(TOKENS, 128),
            shape_of(TOKENS, D, kind=low),
            shape_of(TOKENS, D),
        ),
        (VMEM,) * 4,
        [SMEM, VMEM, VMEM, ANY, ANY],
        [pltpu.VMEM((16, 48, 3 * D), low), pltpu.VMEM((16, 48, D), low), DMA((8,))],
        8 * GIG,
        12 * MEG,
    )(core, stream, vector, mine, yours)


def feed_forward(core, middle, vector, mine, yours):
    return call(
        forward_kernel,
        (shape_of(4, TOKENS, D), shape_of(TOKENS, D)),
        (ANY, VMEM),
        [SMEM, VMEM, VMEM, ANY, ANY],
        [
            pltpu.VMEM((16, 48, FF), low),
            pltpu.VMEM((16, 192, D), low),
            pltpu.VMEM((TOKENS, D), low),
            pltpu.VMEM((2, TOKENS, D), full),
            DMA((16,)),
            DMA((2,)),
        ],
        8 * GIG,
        20 * MEG,
    )(core, middle, vector, mine, yours)


def head(core, stream, final, codes, pos_column, pos_row, scale, valid, bias, mine, yours, at):
    return call(
        partial(head_kernel, at),
        (
            shape_of(TOKENS, D),
            shape_of(SLOTS, D, kind=low),
            shape_of(SLOTS, VPAD, kind=low),
            shape_of(1, VPAD),
            shape_of(2, D),
            shape_of(1, 128),
        ),
        (VMEM,) * 6,
        [SMEM] + [VMEM] * 8 + [ANY, ANY],
        [pltpu.VMEM((16, 48, VPAD), low), pltpu.VMEM((SLOTS, VPAD), full), DMA((6,))],
        6 * GIG,
        10 * MEG,
    )(core, stream, final, codes, pos_column, pos_row, scale, valid, bias, mine, yours)


def feed_forward_back(core, upstream, middle, vector, hidden, mine, yours):
    return call(
        forward_back_kernel,
        (
            shape_of(TOKENS, D),
            shape_of(12, D),
            shape_of(16, 384, UNIT, kind=low),
            shape_of(16, 384, UNIT, kind=low),
        ),
        (VMEM, VMEM, ANY, ANY),
        [SMEM, VMEM, VMEM, VMEM, ANY, ANY, ANY],
        [
            pltpu.VMEM((16, 48, FF), low),
            pltpu.VMEM((16, 192, D), low),
            pltpu.VMEM((D, TOKENS), low),
            pltpu.VMEM((TOKENS, D), low),
            pltpu.VMEM((2, TOKENS, D), full),
            pltpu.VMEM((2, 4, 192, D), low),
            pltpu.VMEM((2, 16, 48, D), low),
            pltpu.VMEM((TOKENS, D), full),
            DMA((16,)),
            DMA((2,)),
            DMA((2, 4)),
        ],
        16 * GIG,
        30 * MEG,
    )(core, upstream, middle, vector, hidden, mine, yours)


def attention_back(core, grad_middle, stream, vector, triple, lse, mixed, mine, yours, at):
    rows = 192 + at
    return call(
        partial(attention_back_kernel, at),
        (
            shape_of(TOKENS, D),
            shape_of(12, D),
            shape_of(16, rows, UNIT, kind=low),
            shape_of(16, rows, UNIT, kind=low),
        ),
        (VMEM, VMEM, ANY, ANY),
        [SMEM] + [VMEM] * 6 + [ANY, ANY],
        [
            pltpu.VMEM((16, 48, 3 * D), low),
            pltpu.VMEM((16, 48, D), low),
            pltpu.VMEM((TOKENS, D), low),
            pltpu.VMEM((3, TOKENS, D), low),
            pltpu.VMEM((4, 16, 48, D), low),
            DMA((8,)),
            DMA((8,)),
        ],
        18 * GIG,
        20 * MEG,
    )(core, grad_middle, stream, vector, triple, lse, mixed, mine, yours)


def embed_back(core, upstream, ids, chosen, grad_logits, small, keep, send):
    shape = shape_of(*keep.shape, kind=low)
    return call(
        embed_back_kernel,
        (shape, shape),
        (ANY, ANY),
        [SMEM] + [VMEM] * 4 + [ANY] * 3,
        [pltpu.VMEM((3, 16, 48, D), low), DMA((8,))],
        5 * GIG,
        10 * MEG,
        input_output_aliases={6: 0, 7: 1},
    )(core, upstream, ids, chosen, grad_logits, small, keep, send)


def update(weight, moment, average, grad, factor):
    clipped = grad * factor
    moment_next = inertia * moment + clipped
    weight_next = weight - step_rate * (clipped + inertia * moment_next)
    return (weight_next, moment_next, average_decay * average + (1.0 - average_decay) * weight_next)


def pack_small(vecs, final_norm, counts):
    own = jnp.concatenate(
        [vecs[0], vecs[1], final_norm[0], final_norm[1], counts.astype(full)]
    ).astype(low)
    own = jnp.pad(own, (0, 2 * UNIT - own.shape[0])).reshape(2, UNIT)
    return jnp.pad(own, ((0, 14), (0, 0)))


def body(hops, *arguments):
    codes, mask_pos, mask_count, table, w_qkv, w_out, w_up, w_down = arguments[:8]
    layer_vecs, final_norm, head_bias = arguments[8:11]
    moments, averages = arguments[11:19], arguments[19:27]
    core = side("core") if hops else jnp.zeros((), jnp.int32)
    own = core.astype(jnp.int32).reshape(1)
    images, seq_len = codes.shape
    table_t = jnp.pad(table.T, ((0, 0), (0, VPAD - V)))
    shards = {"table": [table_t]}
    for l in range(L):
        shards["attention", l] = [w_qkv[l], w_out[l]]
        shards["forward", l] = [w_down[l], w_up[l]]
    if hops:

        def chip_rows(name):
            pieces = PIECES[name if isinstance(name, str) else name[0]]
            halves = [column_units(shard).reshape(2, -1, UNIT) for shard in shards[name]]
            halves = jnp.concatenate(halves, 1).astype(low)
            mine_half = pick(halves, core, 0)[0]
            other = swap(pick(halves, 1 - core, 0)[0], "core")
            blocks, start = [], 0
            for units, rows in pieces:
                size = units * rows
                mine = mine_half[start : start + size].reshape(units, 1, rows, UNIT)
                yours = other[start : start + size].reshape(units, 1, rows, UNIT)
                blocks.append(in_order(core, mine, yours, 1).reshape(-1, UNIT))
                start += size
            return jnp.concatenate(blocks)

        def gathered(chunk, order):
            mine = gather_chips(chunk, order)
            yours = swap(mine, "core")
            return mine.reshape(16, -1, UNIT), yours.reshape(16, -1, UNIT)

        first, second = ("zlo", "zhi", "y", "x"), ("zlo", "zhi", "x", "y")
        small_part = pack_small(layer_vecs, final_norm, mask_count)
        chunk = jnp.concatenate([chip_rows("table"), small_part, chip_rows(("attention", 0))])
        pair_zero = gathered(chunk, first)
        forward_pairs = [gathered(chip_rows(("forward", 0)), second)]
        attention_pairs = [pair_zero, gathered(chip_rows(("attention", 1)), first)]
        forward_pairs.append(gathered(chip_rows(("forward", 1)), second))
        table_pair = pair_zero
        small = [part[:, 144:146].reshape(16, 1, 2 * UNIT) for part in pair_zero]
        small = in_order(core, small[0], small[1], 1).reshape(32, 2 * UNIT).astype(full)
        vectors = [small[:, 288 * l : 288 * l + 288].reshape(12, D) for l in range(L)]
        final_float = small[:, 576:624].reshape(32, 2, 24).transpose(1, 0, 2).reshape(2, D)
        mask_total = jnp.sum(small[:, 624 : 624 + images])
    else:

        def everywhere(shard):
            return lax.all_gather(shard.astype(low), BOTH, axis=0, tiled=True)

        def pair_of(name):
            pieces = PIECES[name if isinstance(name, str) else name[0]]
            blocks = [
                weight_blocks(everywhere(shard), units, 2 * rows)
                for shard, (units, rows) in zip(shards[name], pieces)
            ]
            blocks = jnp.concatenate(blocks, 2)
            return blocks[0], blocks[1]

        table_pair = pair_of("table")
        attention_pairs = [
            tuple(jnp.pad(part, ((0, 0), (160 * (1 - l), 0), (0, 0))) for part in pair_of(("attention", l)))
            for l in range(L)
        ]
        forward_pairs = [pair_of(("forward", l)) for l in range(L)]
        vectors = [everywhere(layer_vecs[l]).astype(full).reshape(12, D) for l in range(L)]
        final_float = everywhere(final_norm.T).T.astype(full)
        mask_total = lax.psum(jnp.sum(mask_count.astype(full)), BOTH)

    slots = jnp.arange(M, dtype=jnp.int32)
    valid = (slots[None, :] < mask_count[:, None]).astype(full)
    places = mask_pos + seq_len * jnp.arange(images, dtype=jnp.int32)[:, None]
    codes_row, codes_column = codes.reshape(1, TOKENS), codes.reshape(TOKENS, 1)
    pos_row, pos_column = places.reshape(1, SLOTS), places.reshape(SLOTS, 1)
    valid_row, valid_column = valid.reshape(1, SLOTS), valid.reshape(SLOTS, 1)
    scale = valid_column * (1.0 / mask_total)
    bias = jnp.pad(head_bias, (0, VPAD - V), constant_values=-1e30).reshape(1, VPAD)

    starts = (160, 0)
    ids, stream = embed(own, codes_column, pos_row, valid_row, *table_pair, 0)
    kept = []
    for l in range(L):
        triple, lse, mixed, middle = attention(own, stream, vectors[l], *attention_pairs[l], starts[l])
        hidden, result = feed_forward(own, middle, vectors[l], *forward_pairs[l])
        kept.append((stream, triple, lse, mixed, middle, hidden))
        stream = result
    upstream, chosen, grad_logits, bias_grad, final_grad, loss = head(
        own, stream, final_float, codes_row, pos_column, pos_row, scale, valid_column, bias, *table_pair, 0
    )

    def scattered(keep, send, order):
        shape = (2, 2, 2, 2) + keep.shape[1:]
        return scatter_chips([keep.reshape(shape), swap(send, "core").reshape(shape)], order)

    back_first, back_second = ("x", "y", "zhi", "zlo"), ("y", "x", "zhi", "zlo")
    reduced, blocks, vector_grads = {}, {}, [None] * L
    for l in reversed(range(L)):
        stream, triple, lse, mixed, middle, hidden = kept[l]
        grad_middle, late, keep, send = feed_forward_back(
            own, upstream, middle, vectors[l], hidden, *forward_pairs[l]
        )
        blocks["forward", l] = keep, send
        if hops:
            reduced["forward", l] = scattered(keep, send, back_second)
        upstream, early, keep, send = attention_back(
            own, grad_middle, stream, vectors[l], triple, lse, mixed, *attention_pairs[l], starts[l]
        )
        blocks["attention", l] = keep, send
        if hops and l:
            reduced["attention", l] = scattered(keep, send, back_first)
        vector_grads[l] = (early + late).reshape(-1)
    small_grads = [vector_grads[0], vector_grads[1], final_grad[0], final_grad[1]]
    if hops:
        small_grads.append(bias_grad[0, :2048])
        small_grads = jnp.concatenate([grad.reshape(32, -1) for grad in small_grads], 1)
        small_grads = jnp.pad(small_grads, ((0, 0), (0, 2 * UNIT - 688))).astype(low)
        small_grads = small_grads.reshape(16, 2, 2, UNIT).transpose(1, 0, 2, 3)
        small_grads = jnp.pad(small_grads, ((0, 0), (0, 0), (0, 14), (0, 0)))
    else:
        head_grad, loss_sum = lax.psum((bias_grad[0, :V], loss[0, 0]), BOTH)
        small_sum = [lax.psum_scatter(g, BOTH, scatter_dimension=0, tiled=True) for g in small_grads]
        small_sum = jnp.concatenate(small_sum)
        small_grads = jnp.zeros((2, 16, 16, UNIT), low)
    keep, send = embed_back(own, upstream, ids, chosen, grad_logits, small_grads, *blocks["attention", 0])
    if hops:
        zero = scattered(keep, send, back_first)
        reduced["table"] = zero[:144]
        reduced["attention", 0] = zero[160:]
        small_sum = zero[144:146].reshape(-1)
    else:
        blocks["table"] = keep[:, :144], send[:, :144]
        blocks["attention", 0] = keep[:, 160:], send[:, 160:]

    def own_rows(name):
        pieces = PIECES[name if isinstance(name, str) else name[0]]
        if not hops:
            total = jnp.stack(blocks[name])
            pairs, start = [], 0
            for units, rows in pieces:
                whole = natural_weight(total, start, units, 2 * rows).astype(full)
                pairs.append(lax.psum_scatter(whole, BOTH, scatter_dimension=0, tiled=True))
                start += 2 * units * rows
            return pairs
        total = reduced[name]
        mine, leaving, start = [], [], 0
        for units, rows in pieces:
            block = total[start : start + 2 * units * rows].reshape(units, 2, rows, UNIT)
            mine.append(pick(block, core, 1).reshape(-1, UNIT))
            leaving.append(pick(block, 1 - core, 1).reshape(-1, UNIT))
            start += 2 * units * rows
        mine, arrived = jnp.concatenate(mine), swap(jnp.concatenate(leaving), "core")
        both = in_order(core, mine[None], arrived[None], 0)
        pairs, start = [], 0
        for units, rows in pieces:
            block = both[:, start : start + units * rows].reshape(2, units, rows, UNIT)
            pairs.append(block.transpose(2, 0, 1, 3).reshape(rows, 2 * units * UNIT))
            start += units * rows
        return pairs

    attention_shares = [own_rows(("attention", l)) for l in range(L)]
    forward_shares = [own_rows(("forward", l)) for l in range(L)]
    width, narrow = layer_vecs.shape[1], final_norm.shape[1]
    shares = [
        own_rows("table")[0][:, :V].T,
        jnp.stack([attention_shares[l][0] for l in range(L)]),
        jnp.stack([attention_shares[l][1] for l in range(L)]),
        jnp.stack([forward_shares[l][1] for l in range(L)]),
        jnp.stack([forward_shares[l][0] for l in range(L)]),
        small_sum[: 2 * width].reshape(L, width),
        small_sum[2 * width : 2 * width + 2 * narrow].reshape(2, narrow),
    ]
    squares = reduce(jnp.add, [jnp.sum(share * share) for share in shares])
    if hops:
        bias_share = small_sum[624:688]
        squares = squares + jnp.sum(bias_share * bias_share)
        tail = jnp.concatenate([bias_share, squares[None], loss[0, :1], jnp.zeros(62)])
        tail = tail.reshape(1, 1, 1, 1, 1, 128)
        for hop in ("core", "x", "y", "zlo", "zhi"):
            axis = HOPS[hop][3]
            tail = in_order(side(hop), tail, swap(tail, hop), 4 if axis is None else axis)
        tail = tail.reshape(32, 128)
        head_grad = tail[:, :64].reshape(-1)[:V]
        squares, loss_sum = jnp.sum(tail[:, 64]), jnp.sum(tail[:, 65])
    else:
        squares = lax.psum(squares, BOTH) + jnp.sum(head_grad * head_grad)
    grad_norm = jnp.sqrt(squares)
    factor = jnp.minimum(1.0, clip_bound / (grad_norm + epsilon))
    results = [
        update(weight, moment, average, grad, factor)
        for weight, moment, average, grad in zip(arguments[3:11], moments, averages, shares + [head_grad])
    ]
    return (
        (loss_sum, mask_total, grad_norm)
        + tuple(result[0] for result in results)
        + tuple(result[1] for result in results)
        + tuple(result[2] for result in results)
    )


def solution(mesh):
    return jax.shard_map(
        partial(body, mesh.shape["dp"] == 8 and mesh.shape["fsdp"] == 4),
        mesh=mesh,
        in_specs=(
            P(("dp", "fsdp"), None),
            P(("dp", "fsdp"), None),
            P(("dp", "fsdp")),
            P(None, ("dp", "fsdp")),
            P(None, ("dp", "fsdp"), None),
            P(None, ("dp", "fsdp"), None),
            P(None, ("dp", "fsdp"), None),
            P(None, ("dp", "fsdp"), None),
            P(None, ("dp", "fsdp")),
            P(None, ("dp", "fsdp")),
            P(),
            P(None, ("dp", "fsdp")),
            P(None, ("dp", "fsdp"), None),
            P(None, ("dp", "fsdp"), None),
            P(None, ("dp", "fsdp"), None),
            P(None, ("dp", "fsdp"), None),
            P(None, ("dp", "fsdp")),
            P(None, ("dp", "fsdp")),
            P(),
            P(None, ("dp", "fsdp")),
            P(None, ("dp", "fsdp"), None),
            P(None, ("dp", "fsdp"), None),
            P(None, ("dp", "fsdp"), None),
            P(None, ("dp", "fsdp"), None),
            P(None, ("dp", "fsdp")),
            P(None, ("dp", "fsdp")),
            P(),
        ),
        out_specs=(
            P(),
            P(),
            P(),
            P(None, ("dp", "fsdp")),
            P(None, ("dp", "fsdp"), None),
            P(None, ("dp", "fsdp"), None),
            P(None, ("dp", "fsdp"), None),
            P(None, ("dp", "fsdp"), None),
            P(None, ("dp", "fsdp")),
            P(None, ("dp", "fsdp")),
            P(),
            P(None, ("dp", "fsdp")),
            P(None, ("dp", "fsdp"), None),
            P(None, ("dp", "fsdp"), None),
            P(None, ("dp", "fsdp"), None),
            P(None, ("dp", "fsdp"), None),
            P(None, ("dp", "fsdp")),
            P(None, ("dp", "fsdp")),
            P(),
            P(None, ("dp", "fsdp")),
            P(None, ("dp", "fsdp"), None),
            P(None, ("dp", "fsdp"), None),
            P(None, ("dp", "fsdp"), None),
            P(None, ("dp", "fsdp"), None),
            P(None, ("dp", "fsdp")),
            P(None, ("dp", "fsdp")),
            P(),
        ),
        check_vma=False,
    )
```

time: 1750 us -> 773 us (0.44)
  waiting for transfers between devices: 1130 us -> 393 us
  blocking collectives: 203 us -> 0 us
  matrix products: 179 us -> 0 us
  Pallas kernels: 0 us -> 178 us
  local copies, waits for them, and re-layouts: 85.1 us -> 23 us
  starting transfers between devices: 0.99 us -> 51.6 us
    reduce_scatter x4 -> x0, waiting for transfers between devices: 663 us -> none  [the longest x1 209 us: body(): lax.psum_scatter(stacked[3], ('dp', 'fsdp'), scatter_dimension=1, tiled=T...]
    ppermute x0 -> x55, waiting for transfers between devices: none -> 393 us  [swap(): return lax.ppermute(tensor, axis, [(i, i ^ flip) for i in range(size)])]
    all_gather x9 -> x0, waiting for transfers between devices: 345 us -> none  [the longest x2 120 us: fetch_forward(): lax.all_gather(down_part, ('dp', 'fsdp'), axis=0, tiled=True)]
    dot_general x82 -> x0, matrix products: 179 us -> none  [the longest x16 47.2 us: project(): jnp.einsum('bsd,de->bse', left, right, preferred_element_type=jnp.float32)]
    pallas_call x0 -> x11, Pallas kernels: none -> 178 us  [the longest x2 49.1 us: attention_back(): call(partial(attention_back_kernel, at), (shape_of(TOKENS, D), shape_of(1...]
    unnamed x17 -> x0, waiting for transfers between devices: 121 us -> none
    unnamed x2 -> x0, blocking collectives: 82.3 us -> none
    psum x2 -> x0, blocking collectives: 79.9 us -> none  [the longest x1 40.7 us: body(): lax.psum(jnp.sum(mask_count.astype(jnp.float32)), ('dp', 'fsdp'))]
  transfers between devices with their start and end apart: 15 -> 55, of which waited for: 12 -> 36; matrix products, arithmetic and copies ran while one was open for 11% -> 14% of each run, Pallas kernels for 0% -> 6%
where the time goes in v1:
time: 773 us; the launch traced here: 766 us
  waiting for transfers between devices  393 us (51%)
  Pallas kernels  178 us (23%)
  other arithmetic  109 us (14%)
  starting transfers between devices  51.6 us (7%)
  local copies, waits for them, and re-layouts  23 us (3%)
  between operations  10.5 us (1%)
    ppermute x55, waiting for transfers between devices, swap(): return lax.ppermute(tensor, axis, [(i, i ^ flip) for i in range(size)])  393 us
    ppermute x55, starting transfers between devices, swap(): return lax.ppermute(tensor, axis, [(i, i ^ flip) for i in range(size)])  51.6 us
    pallas_call x2, Pallas kernels, attention_back(): call(partial(attention_back_kernel, at), (shape_of(TOKENS, D), shape_of(1...  49.1 us
    pallas_call x2, Pallas kernels, feed_forward_back(): call(forward_back_kernel, (shape_of(TOKENS, D), shape_of(12, D), shape_of...  44.5 us
    convert_element_type x16, other arithmetic, scatter_chips(): arrived = swap(leaving.astype(jnp.bfloat16), hop)  41.7 us
    select_n x34, other arithmetic, in_order(): jnp.where(bit == 0, jnp.concatenate([own, other], axis), jnp.concatenate(...  33.9 us
    pallas_call x2, Pallas kernels, attention(): call(partial(attention_kernel, at), (shape_of(3, TOKENS, D, kind=low), sh...  29.5 us
    pallas_call x2, Pallas kernels, feed_forward(): call(forward_kernel, (shape_of(4, TOKENS, D), shape_of(TOKENS, D)), (ANY,...  23.9 us
  transfers between devices with their start and end apart: 55, of which 36 were waited for; matrix products, arithmetic and copies ran while one was open for 14% of the time, Pallas kernels for 6%

profile of v1, /device:TPU:0, one launch (start us, length us, event | category | flops | bytes accessed | tf_op | source)
XLA Modules:
  0.0 765.7 jit_solution(3190877201994921445)
XLA Ops:
  12.0 6.9 collective-permute-done.2
  25.4 14.0 %collective-permute-done.8 = bf16[1,1,1,1,384,384]{5,4,3,2,1,0:T(8,128)(2,1)S(1)} collective-permute-done((bf16[1,1,1,1,384,384]{5,4,3,2,1,0:T(8,128)(2,1)S(1)}, bf16[1,1,1,1,384,384]{5,4,3,2,1,0:T(8,128)(2,1)S(1)}, u32[]{:S(2)}, u32[]{:S(2)}) %collective-permute-start.8) | collective-permute-done | bytes 294944 | tf_op jit(solution)/shard_map/ppermute | solution.py:40
  41.9 17.2 %collective-permute-done.3 = bf16[1,2,1,1,352,384]{5,4,3,2,1,0:T(8,128)(2,1)S(1)} collective-permute-done((bf16[1,2,1,1,352,384]{5,4,3,2,1,0:T(8,128)(2,1)S(1)}, bf16[1,2,1,1,352,384]{5,4,3,2,1,0:T(8,128)(2,1)S(1)}, u32[]{:S(2)}, u32[]{:S(2)}) %collective-permute-start.3) | collective-permute-done | bytes 540704 | tf_op jit(solution)/shard_map/ppermute | solution.py:40
  64.7 6.1 collective-permute-done.9
  73.6 3.5 collective-permute-done.20
  80.4 4.0 collective-permute-done.4
  84.5 3.3 maximum_select_fusion.6
  90.5 17.3 %collective-permute-done.21 = bf16[1,2,1,1,384,384]{5,4,3,2,1,0:T(8,128)(2,1)S(1)} collective-permute-done((bf16[1,2,1,1,384,384]{5,4,3,2,1,0:T(8,128)(2,1)}, bf16[1,2,1,1,384,384]{5,4,3,2,1,0:T(8,128)(2,1)S(1)}, u32[]{:S(2)}, u32[]{:S(2)}) %collective-permute-start.21) | collective-permute-done | bytes 589856 | tf_op jit(solution)/shard_map/ppermute | solution.py:40
  113.9 56.9 %collective-permute-done.22 = bf16[2,2,1,1,384,384]{5,4,3,2,1,0:T(8,128)(2,1)S(1)} collective-permute-done((bf16[2,2,1,1,384,384]{5,4,3,2,1,0:T(8,128)(2,1)S(1)}, bf16[2,2,1,1,384,384]{5,4,3,2,1,0:T(8,128)(2,1)S(1)}, u32[]{:S(2)}, u32[]{:S(2)}) %collective-permute-start.22) | collective-permute-done | bytes 1179680 | tf_op jit(solution)/shard_map/ppermute | solution.py:40
  174.0 6.0 maximum_select_fusion.2
  180.8 6.3 collective-permute-done.13
  187.2 5.7 maximum_select_fusion
  195.1 4.1 collective-permute-done.14
  199.3 3.4 collective-permute-start.15
  202.8 13.2 %collective-permute-done.15 = bf16[1,2,1,1,192,384]{5,4,3,2,1,0:T(8,128)(2,1)S(1)} collective-permute-done((bf16[1,2,1,1,192,384]{5,4,3,2,1,0:T(8,128)(2,1)S(1)}, bf16[1,2,1,1,192,384]{5,4,3,2,1,0:T(8,128)(2,1)S(1)}, u32[]{:S(2)}, u32[]{:S(2)}) %collective-permute-start.15) | collective-permute-done | bytes 294944 | tf_op jit(solution)/shard_map/ppermute | solution.py:40
  216.8 10.3 %collective-permute-done.23 = bf16[2,2,1,2,384,384]{5,4,3,2,1,0:T(8,128)(2,1)} collective-permute-done((bf16[2,2,1,2,384,384]{5,4,3,2,1,0:T(8,128)(2,1)}, bf16[2,2,1,2,384,384]{5,4,3,2,1,0:T(8,128)(2,1)}, u32[]{:S(2)}, u32[]{:S(2)}) %collective-permute-start.23) | collective-permute-done | bytes 2359328 | tf_op jit(solution)/shard_map/ppermute | solution.py:40
  227.1 6.8 maximum_select_fusion.1
  241.4 21.3 %collective-permute-done.17 = bf16[2,2,2,1,192,384]{5,4,3,2,1,0:T(8,128)(2,1)} collective-permute-done((bf16[2,2,2,1,192,384]{5,4,3,2,1,0:T(8,128)(2,1)S(1)}, bf16[2,2,2,1,192,384]{5,4,3,2,1,0:T(8,128)(2,1)}, u32[]{:S(2)}, u32[]{:S(2)}) %collective-permute-start.17) | collective-permute-done | bytes 1179680 | tf_op jit(solution)/shard_map/ppermute | solution.py:40
  271.9 6.3 shard_map.466
  278.2 14.7 %shard_map.467 = (bf16[3,512,768]{2,1,0:T(8,128)(2,1)}, f32[512,128]{1,0:T(8,128)}, bf16[512,768]{1,0:T(8,128)(2,1)}, f32[512,768]{1,0:T(8,128)}) custom-call(s32[1]{0:T(128)} %bitcast.core, f32[512,768]{1,0:T(8,128)} %get-tuple-element.65.stream, f32[12,768]{1,0:T(8,128)} %reshape.3191.vector, bf16[16,352,384]{2,1,0:T(8,128)(2,1)} %bitcast.30.mine, ...), custom_call_target="tpu_custom_call" | custom-call | flops 8000000000 | bytes 12000000 | tf_op jit(solution)/shard_map/pallas_call | solution.py:617
  293.0 12.0 %shard_map.468 = (f32[4,512,768]{2,1,0:T(8,128)}, f32[512,768]{1,0:T(8,128)}) custom-call(s32[1]{0:T(128)} %bitcast.core, f32[512,768]{1,0:T(8,128)} %get-tuple-element.66.middle, f32[12,768]{1,0:T(8,128)} %reshape.3191.vector, bf16[16,384,384]{2,1,0:T(8,128)(2,1)} %bitcast.52.mine, bf16[16,384,384]{2,1,0:T(8,128)(2,1)} %bitcast.53.yours), custom_call_target="tpu_custom_call" | custom-call | flops 8000000000 | bytes 20000000 | tf_op jit(solution)/shard_map/pallas_call | solution.py:634
  304.9 14.8 %shard_map.469 = (bf16[3,512,768]{2,1,0:T(8,128)(2,1)}, f32[512,128]{1,0:T(8,128)}, bf16[512,768]{1,0:T(8,128)(2,1)}, f32[512,768]{1,0:T(8,128)}) custom-call(s32[1]{0:T(128)} %bitcast.core, f32[512,768]{1,0:T(8,128)} %get-tuple-element.67.stream, f32[12,768]{1,0:T(8,128)} %reshape.3197.vector, bf16[16,192,384]{2,1,0:T(8,128)(2,1)} %bitcast.323, ...), custom_call_target="tpu_custom_call" | custom-call | flops 8000000000 | bytes 12000000 | tf_op jit(solution)/shard_map/pallas_call | solution.py:617
  319.7 12.0 %shard_map.470 = (f32[4,512,768]{2,1,0:T(8,128)}, f32[512,768]{1,0:T(8,128)}) custom-call(s32[1]{0:T(128)} %bitcast.core, f32[512,768]{1,0:T(8,128)} %get-tuple-element.68.middle, f32[12,768]{1,0:T(8,128)} %reshape.3197.vector, bf16[16,384,384]{2,1,0:T(8,128)(2,1)} %bitcast.89.mine, bf16[16,384,384]{2,1,0:T(8,128)(2,1)} %bitcast.90.yours), custom_call_target="tpu_custom_call" | custom-call | flops 8000000000 | bytes 20000000 | tf_op jit(solution)/shard_map/pallas_call | solution.py:634
  331.7 10.1 %shard_map.471 = (f32[512,768]{1,0:T(8,128)}, bf16[256,768]{1,0:T(8,128)(2,1)}, bf16[256,2304]{1,0:T(8,128)(2,1)}, f32[1,2304]{1,0:T(1,128)}, f32[2,768]{1,0:T(2,128)}, /*index=5*/f32[1,128]{1,0:T(1,128)}) custom-call(s32[1]{0:T(128)} %bitcast.core, f32[512,768]{1,0:T(8,128)} %get-tuple-element.69.stream, f32[2,768]{1,0:T(2,128)} %reshape.3209.final, ...), custom_call_target="tpu_custom_call" | custom-call | flops 6000000000 | bytes 10000000 | tf_op jit(solution)/shard_map/pallas_call | solution.py:653
  341.8 22.2 %shard_map.472 = (f32[512,768]{1,0:T(8,128)}, f32[12,768]{1,0:T(8,128)}, bf16[16,384,384]{2,1,0:T(8,128)(2,1)}, bf16[16,384,384]{2,1,0:T(8,128)(2,1)}) custom-call(s32[1]{0:T(128)} %bitcast.core, f32[512,768]{1,0:T(8,128)} %get-tuple-element.70.upstream, f32[512,768]{1,0:T(8,128)} %get-tuple-element.68.middle, f32[12,768]{1,0:T(8,128)} %reshape.3197.vector, ...), custom_call_target="tpu_custom_call" | custom-call | flops 16000000000 | bytes 30000000 | tf_op jit(solution)/shard_map/pallas_call | solution.py:672
  364.0 24.5 %shard_map.473 = (f32[512,768]{1,0:T(8,128)}, f32[12,768]{1,0:T(8,128)}, bf16[16,192,384]{2,1,0:T(8,128)(2,1)}, bf16[16,192,384]{2,1,0:T(8,128)(2,1)}) custom-call(s32[1]{0:T(128)} %bitcast.core, f32[512,768]{1,0:T(8,128)} %get-tuple-element.72.grad_middle, f32[512,768]{1,0:T(8,128)} %get-tuple-element.67.stream, f32[12,768]{1,0:T(8,128)} %reshape.3197.vector, ...), custom_call_target="tpu_custom_call" | custom-call | flops 17999998976 | bytes 20000000 | tf_op jit(solution)/shard_map/pallas_call | solution.py:702
  389.4 22.4 %shard_map.474 = (f32[512,768]{1,0:T(8,128)}, f32[12,768]{1,0:T(8,128)}, bf16[16,384,384]{2,1,0:T(8,128)(2,1)}, bf16[16,384,384]{2,1,0:T(8,128)(2,1)}) custom-call(s32[1]{0:T(128)} %bitcast.core, f32[512,768]{1,0:T(8,128)} %get-tuple-element.76.upstream, f32[512,768]{1,0:T(8,128)} %get-tuple-element.66.middle, f32[12,768]{1,0:T(8,128)} %reshape.3191.vector, ...), custom_call_target="tpu_custom_call" | custom-call | flops 16000000000 | bytes 30000000 | tf_op jit(solution)/shard_map/pallas_call | solution.py:672
  411.8 24.6 %shard_map.475 = (f32[512,768]{1,0:T(8,128)}, f32[12,768]{1,0:T(8,128)}, bf16[16,352,384]{2,1,0:T(8,128)(2,1)}, bf16[16,352,384]{2,1,0:T(8,128)(2,1)}) custom-call(s32[1]{0:T(128)} %bitcast.core, f32[512,768]{1,0:T(8,128)} %get-tuple-element.78.grad_middle, f32[512,768]{1,0:T(8,128)} %get-tuple-element.65.stream, f32[12,768]{1,0:T(8,128)} %reshape.3191.vector, ...), custom_call_target="tpu_custom_call" | custom-call | flops 17999998976 | bytes 20000000 | tf_op jit(solution)/shard_map/pallas_call | solution.py:702
  438.7 15.0 %shard_map.476 = (bf16[16,352,384]{2,1,0:T(8,128)(2,1)}, bf16[16,352,384]{2,1,0:T(8,128)(2,1)}) custom-call(s32[1]{0:T(128)} %bitcast.core, f32[512,768]{1,0:T(8,128)} %get-tuple-element.82.upstream, s32[512,1]{1,0:T(8,128)} %get-tuple-element.83.ids, bf16[256,768]{1,0:T(8,128)(2,1)} %get-tuple-element.84.chosen, ...), custom_call_target="tpu_custom_call", output_to_operand_aliasing={{0}: (6, {}), {1}: (7, {})} | custom-call | flops 5000000000 | bytes 10000000 | tf_op jit(solution)/shard_map/pallas_call | solution.py:728
  454.8 6.9 collective-permute-done.25
  461.8 4.2 add_convert_fusion.2
  478.4 4.4 add_convert_fusion.1
  484.4 56.4 %collective-permute-done.33 = bf16[2,2,2,1,192,384]{5,4,3,2,1,0:T(8,128)(2,1)S(1)} collective-permute-done((bf16[2,2,2,1,192,384]{5,4,3,2,1,0:T(8,128)(2,1)}, bf16[2,2,2,1,192,384]{5,4,3,2,1,0:T(8,128)(2,1)S(1)}, u32[]{:S(2)}, u32[]{:S(2)}) %collective-permute-start.33) | collective-permute-done | bytes 1179680 | tf_op jit(solution)/shard_map/ppermute | solution.py:40
  544.4 3.3 add_convert_fusion.6
  548.4 43.7 %collective-permute-done.34 = bf16[2,2,1,1,192,384]{5,4,3,2,1,0:T(8,128)(2,1)} collective-permute-done((bf16[2,2,1,1,192,384]{5,4,3,2,1,0:T(8,128)(2,1)}, bf16[2,2,1,1,192,384]{5,4,3,2,1,0:T(8,128)(2,1)}, u32[]{:S(2)}, u32[]{:S(2)}) %collective-permute-start.34) | collective-permute-done | bytes 589856 | tf_op jit(solution)/shard_map/ppermute | solution.py:40
  594.1 15.4 %collective-permute-done.35 = bf16[1,2,1,1,192,384]{5,4,3,2,1,0:T(8,128)(2,1)} collective-permute-done((bf16[1,2,1,1,192,384]{5,4,3,2,1,0:T(8,128)(2,1)}, bf16[1,2,1,1,192,384]{5,4,3,2,1,0:T(8,128)(2,1)}, u32[]{:S(2)}, u32[]{:S(2)}) %collective-permute-start.35) | collective-permute-done | bytes 294944 | tf_op jit(solution)/shard_map/ppermute | solution.py:40
  611.4 5.5 collective-permute-done.36
  618.2 3.6 add_convert_fusion.3
  623.1 3.5 add_convert_fusion.4
  631.2 21.3 %collective-permute-done.28 = bf16[1,2,1,1,352,384]{5,4,3,2,1,0:T(8,128)(2,1)S(1)} collective-permute-done((bf16[1,2,1,1,352,384]{5,4,3,2,1,0:T(8,128)(2,1)S(1)}, bf16[1,2,1,1,352,384]{5,4,3,2,1,0:T(8,128)(2,1)S(1)}, u32[]{:S(2)}, u32[]{:S(2)}) %collective-permute-start.28) | collective-permute-done | bytes 540704 | tf_op jit(solution)/shard_map/ppermute | solution.py:40
  658.3 3.4 collective-permute-start.47
  661.7 10.7 %collective-permute-done.40 = bf16[2,2,1,1,384,384]{5,4,3,2,1,0:T(8,128)(2,1)S(1)} collective-permute-done((bf16[2,2,1,1,384,384]{5,4,3,2,1,0:T(8,128)(2,1)}, bf16[2,2,1,1,384,384]{5,4,3,2,1,0:T(8,128)(2,1)S(1)}, u32[]{:S(2)}, u32[]{:S(2)}) %collective-permute-start.40) | collective-permute-done | bytes 1179680 | tf_op jit(solution)/shard_map/ppermute | solution.py:40
  688.0 13.4 %collective-permute-done.47 = bf16[1,2,1,1,384,384]{5,4,3,2,1,0:T(8,128)(2,1)} collective-permute-done((bf16[1,2,1,1,384,384]{5,4,3,2,1,0:T(8,128)(2,1)}, bf16[1,2,1,1,384,384]{5,4,3,2,1,0:T(8,128)(2,1)}, u32[]{:S(2)}, u32[]{:S(2)}) %collective-permute-start.47) | collective-permute-done | bytes 589856 | tf_op jit(solution)/shard_map/ppermute | solution.py:40
  705.8 7.4 collective-permute-done.41
  714.7 4.7 collective-permute-done.48
  721.1 4.5 collective-permute-done.42
  744.9 3.6 collective-permute-done.53
  749.5 3.6 collective-permute-done.54
  (441 shorter events, 150.6 us)
Async XLA Ops:
  4.7 57.2 %collective-permute-start.19 = (bf16[192,384]{1,0:T(8,128)(2,1)}, bf16[192,384]{1,0:T(8,128)(2,1)}, u32[]{:S(2)}, u32[]{:S(2)}) collective-permute-start(bf16[192,384]{1,0:T(8,128)(2,1)} %bitcast.295), channel_id=1, source_target_pairs={{0,1},{1,0},{2,3},{3,2},{4,5},{5,4},{6,7},{7,6},{8,9},{9,8},{10,11... | collective-permute-start | bytes 442376 | tf_op jit(solution)/shard_map/ppermute | solution.py:40
  5.3 6.6 collective-permute-start.7
  9.1 9.8 %collective-permute-start.2 = (bf16[1,1,1,1,352,384]{5,4,3,2,1,0:T(8,128)(2,1)S(1)}, bf16[1,1,1,1,352,384]{5,4,3,2,1,0:T(8,128)(2,1)S(1)}, u32[]{:S(2)}, u32[]{:S(2)}) collective-permute-start(bf16[1,1,1,1,352,384]{5,4,3,2,1,0:T(8,128)(2,1)S(1)} %get-tuple-element.179), channel_id=1, source_target_pairs={{0,8},{4,12},{8,0},{12,4},{16,24},{20,28},{24,16},{28,20},{1,9},{5... | collective-permute-start | bytes 811016 | tf_op jit(solution)/shard_map/ppermute | solution.py:40
  19.0 40.2 %collective-permute-start.3 = (bf16[1,2,1,1,352,384]{5,4,3,2,1,0:T(8,128)(2,1)S(1)}, bf16[1,2,1,1,352,384]{5,4,3,2,1,0:T(8,128)(2,1)S(1)}, u32[]{:S(2)}, u32[]{:S(2)}) collective-permute-start(bf16[1,2,1,1,352,384]{5,4,3,2,1,0:T(8,128)(2,1)S(1)} %maximum_select_fusion.22), channel_id=1, source_target_pairs={{0,16},{4,20},{8,24},{12,28},{16,0},{20,4},{24,8},{28,12},{1,17},{... | collective-permute-start | bytes 1622024 | tf_op jit(solution)/shard_map/ppermute | solution.py:40
  21.8 17.6 %collective-permute-start.8 = (bf16[1,1,1,1,384,384]{5,4,3,2,1,0:T(8,128)(2,1)S(1)}, bf16[1,1,1,1,384,384]{5,4,3,2,1,0:T(8,128)(2,1)S(1)}, u32[]{:S(2)}, u32[]{:S(2)}) collective-permute-start(bf16[1,1,1,1,384,384]{5,4,3,2,1,0:T(8,128)(2,1)S(1)} %get-tuple-element.172), channel_id=1, source_target_pairs={{0,8},{4,12},{8,0},{12,4},{16,24},{20,28},{24,16},{28,20},{1,9},{5... | collective-permute-start | bytes 884744 | tf_op jit(solution)/shard_map/ppermute | solution.py:40
  39.5 31.3 %collective-permute-start.9 = (bf16[1,2,1,1,384,384]{5,4,3,2,1,0:T(8,128)(2,1)S(1)}, bf16[1,2,1,1,384,384]{5,4,3,2,1,0:T(8,128)(2,1)S(1)}, u32[]{:S(2)}, u32[]{:S(2)}) collective-permute-start(bf16[1,2,1,1,384,384]{5,4,3,2,1,0:T(8,128)(2,1)S(1)} %maximum_select_fusion.14), channel_id=1, source_target_pairs={{0,16},{4,20},{8,24},{12,28},{16,0},{20,4},{24,8},{28,12},{1,17},{... | collective-permute-start | bytes 1769480 | tf_op jit(solution)/shard_map/ppermute | solution.py:40
  60.4 24.0 %collective-permute-start.4 = (bf16[2,2,1,1,352,384]{5,4,3,2,1,0:T(8,128)(2,1)}, bf16[2,2,1,1,352,384]{5,4,3,2,1,0:T(8,128)(2,1)}, u32[]{:S(2)}, u32[]{:S(2)}) collective-permute-start(bf16[2,2,1,1,352,384]{5,4,3,2,1,0:T(8,128)(2,1)} %maximum_select_fusion.12), channel_id=1, source_target_pairs={{0,4},{4,0},{8,12},{12,8},{16,20},{20,16},{24,28},{28,24},{1,5},{5... | collective-permute-start | bytes 3244040 | tf_op jit(solution)/shard_map/ppermute | solution.py:40
  63.8 13.3 %collective-permute-start.20 = (bf16[1,1,1,1,384,384]{5,4,3,2,1,0:T(8,128)(2,1)S(1)}, bf16[1,1,1,1,384,384]{5,4,3,2,1,0:T(8,128)(2,1)S(1)}, u32[]{:S(2)}, u32[]{:S(2)}) collective-permute-start(bf16[1,1,1,1,384,384]{5,4,3,2,1,0:T(8,128)(2,1)S(1)} %get-tuple-element.161), channel_id=1, source_target_pairs={{0,8},{4,12},{8,0},{12,4},{16,24},{20,28},{24,16},{28,20},{1,9},{5... | collective-permute-start | bytes 884744 | tf_op jit(solution)/shard_map/ppermute | solution.py:40
  72.1 38.9 %collective-permute-start.10 = (bf16[2,2,1,1,384,384]{5,4,3,2,1,0:T(8,128)(2,1)}, bf16[2,2,1,1,384,384]{5,4,3,2,1,0:T(8,128)(2,1)S(1)}, u32[]{:S(2)}, u32[]{:S(2)}) collective-permute-start(bf16[2,2,1,1,384,384]{5,4,3,2,1,0:T(8,128)(2,1)} %fusion), channel_id=1, source_target_pairs={{0,2},{1,3},{2,0},{3,1},{4,6},{5,7},{6,4},{7,5},{8,10},{9,11},{10,... | collective-permute-start | bytes 3538952 | tf_op jit(solution)/shard_map/ppermute | solution.py:40
  78.7 29.1 %collective-permute-start.21 = (bf16[1,2,1,1,384,384]{5,4,3,2,1,0:T(8,128)(2,1)}, bf16[1,2,1,1,384,384]{5,4,3,2,1,0:T(8,128)(2,1)S(1)}, u32[]{:S(2)}, u32[]{:S(2)}) collective-permute-start(bf16[1,2,1,1,384,384]{5,4,3,2,1,0:T(8,128)(2,1)} %maximum_select_fusion.18), channel_id=1, source_target_pairs={{0,16},{4,20},{8,24},{12,28},{16,0},{20,4},{24,8},{28,12},{1,17},{... | collective-permute-start | bytes 1769480 | tf_op jit(solution)/shard_map/ppermute | solution.py:40
  87.8 86.2 %collective-permute-start.5 = (bf16[2,2,2,1,352,384]{5,4,3,2,1,0:T(8,128)(2,1)}, bf16[2,2,2,1,352,384]{5,4,3,2,1,0:T(8,128)(2,1)}, u32[]{:S(2)}, u32[]{:S(2)}) collective-permute-start(bf16[2,2,2,1,352,384]{5,4,3,2,1,0:T(8,128)(2,1)} %maximum_select_fusion.6), channel_id=1, source_target_pairs={{0,2},{1,3},{2,0},{3,1},{4,6},{5,7},{6,4},{7,5},{8,10},{9,11},{10,... | collective-permute-start | bytes 6488072 | tf_op jit(solution)/shard_map/ppermute | solution.py:40
  108.0 62.8 %collective-permute-start.22 = (bf16[2,2,1,1,384,384]{5,4,3,2,1,0:T(8,128)(2,1)S(1)}, bf16[2,2,1,1,384,384]{5,4,3,2,1,0:T(8,128)(2,1)S(1)}, u32[]{:S(2)}, u32[]{:S(2)}) collective-permute-start(bf16[2,2,1,1,384,384]{5,4,3,2,1,0:T(8,128)(2,1)S(1)} %maximum_select_fusion.10), channel_id=1, source_target_pairs={{0,2},{1,3},{2,0},{3,1},{4,6},{5,7},{6,4},{7,5},{8,10},{9,11},{10,... | collective-permute-start | bytes 3538952 | tf_op jit(solution)/shard_map/ppermute | solution.py:40
  112.1 75.0 %collective-permute-start.11 = (bf16[2,2,1,2,384,384]{5,4,3,2,1,0:T(8,128)(2,1)S(1)}, bf16[2,2,1,2,384,384]{5,4,3,2,1,0:T(8,128)(2,1)}, u32[]{:S(2)}, u32[]{:S(2)}) collective-permute-start(bf16[2,2,1,2,384,384]{5,4,3,2,1,0:T(8,128)(2,1)S(1)} %maximum_select_fusion.3), channel_id=1, source_target_pairs={{0,4},{4,0},{8,12},{12,8},{16,20},{20,16},{24,28},{28,24},{1,5},{5... | collective-permute-start | bytes 7077896 | tf_op jit(solution)/shard_map/ppermute | solution.py:40
  172.6 54.5 %collective-permute-start.23 = (bf16[2,2,1,2,384,384]{5,4,3,2,1,0:T(8,128)(2,1)}, bf16[2,2,1,2,384,384]{5,4,3,2,1,0:T(8,128)(2,1)}, u32[]{:S(2)}, u32[]{:S(2)}) collective-permute-start(bf16[2,2,1,2,384,384]{5,4,3,2,1,0:T(8,128)(2,1)} %maximum_select_fusion.5), channel_id=1, source_target_pairs={{0,4},{4,0},{8,12},{12,8},{16,20},{20,16},{24,28},{28,24},{1,5},{5... | collective-permute-start | bytes 7077896 | tf_op jit(solution)/shard_map/ppermute | solution.py:40
  180.0 85.9 %collective-permute-start.6 = (bf16[2,2,2,2,352,384]{5,4,3,2,1,0:T(8,128)(2,1)}, bf16[2,2,2,2,352,384]{5,4,3,2,1,0:T(8,128)(2,1)}, u32[]{:S(2)}, u32[]{:S(2)}) collective-permute-start(bf16[2,2,2,2,352,384]{5,4,3,2,1,0:T(8,128)(2,1)} %maximum_select_fusion.2), channel_id=1, source_target_pairs={{0,1},{1,0},{2,3},{3,2},{4,5},{5,4},{6,7},{7,6},{8,9},{9,8},{10,11... | collective-permute-start | bytes 12976136 | tf_op jit(solution)/shard_map/ppermute | solution.py:40
  180.2 6.9 collective-permute-start.13
  192.9 100.1 %collective-permute-start.12 = (bf16[2,2,2,2,384,384]{5,4,3,2,1,0:T(8,128)(2,1)}, bf16[2,2,2,2,384,384]{5,4,3,2,1,0:T(8,128)(2,1)}, u32[]{:S(2)}, u32[]{:S(2)}) collective-permute-start(bf16[2,2,2,2,384,384]{5,4,3,2,1,0:T(8,128)(2,1)} %maximum_select_fusion), channel_id=1, source_target_pairs={{0,1},{1,0},{2,3},{3,2},{4,5},{5,4},{6,7},{7,6},{8,9},{9,8},{10,11... | collective-permute-start | bytes 14155784 | tf_op jit(solution)/shard_map/ppermute | solution.py:40
  193.3 6.0 collective-permute-start.14
  199.3 16.7 %collective-permute-start.15 = (bf16[1,2,1,1,192,384]{5,4,3,2,1,0:T(8,128)(2,1)S(1)}, bf16[1,2,1,1,192,384]{5,4,3,2,1,0:T(8,128)(2,1)S(1)}, u32[]{:S(2)}, u32[]{:S(2)}) collective-permute-start(bf16[1,2,1,1,192,384]{5,4,3,2,1,0:T(8,128)(2,1)S(1)} %maximum_select_fusion.24), channel_id=1, source_target_pairs={{0,16},{4,20},{8,24},{12,28},{16,0},{20,4},{24,8},{28,12},{1,17},{... | collective-permute-start | bytes 884744 | tf_op jit(solution)/shard_map/ppermute | solution.py:40
  216.1 20.6 %collective-permute-start.16 = (bf16[2,2,1,1,192,384]{5,4,3,2,1,0:T(8,128)(2,1)S(1)}, bf16[2,2,1,1,192,384]{5,4,3,2,1,0:T(8,128)(2,1)S(1)}, u32[]{:S(2)}, u32[]{:S(2)}) collective-permute-start(bf16[2,2,1,1,192,384]{5,4,3,2,1,0:T(8,128)(2,1)S(1)} %maximum_select_fusion.16), channel_id=1, source_target_pairs={{0,4},{4,0},{8,12},{12,8},{16,20},{20,16},{24,28},{28,24},{1,5},{5... | collective-permute-start | bytes 1769480 | tf_op jit(solution)/shard_map/ppermute | solution.py:40
  234.0 85.8 %collective-permute-start.24 = (bf16[2,2,2,2,384,384]{5,4,3,2,1,0:T(8,128)(2,1)}, bf16[2,2,2,2,384,384]{5,4,3,2,1,0:T(8,128)(2,1)}, u32[]{:S(2)}, u32[]{:S(2)}) collective-permute-start(bf16[2,2,2,2,384,384]{5,4,3,2,1,0:T(8,128)(2,1)} %maximum_select_fusion.1), channel_id=1, source_target_pairs={{0,1},{1,0},{2,3},{3,2},{4,5},{5,4},{6,7},{7,6},{8,9},{9,8},{10,11... | collective-permute-start | bytes 14155784 | tf_op jit(solution)/shard_map/ppermute | solution.py:40
  236.9 25.9 %collective-permute-start.17 = (bf16[2,2,2,1,192,384]{5,4,3,2,1,0:T(8,128)(2,1)S(1)}, bf16[2,2,2,1,192,384]{5,4,3,2,1,0:T(8,128)(2,1)}, u32[]{:S(2)}, u32[]{:S(2)}) collective-permute-start(bf16[2,2,2,1,192,384]{5,4,3,2,1,0:T(8,128)(2,1)S(1)} %maximum_select_fusion.8), channel_id=1, source_target_pairs={{0,2},{1,3},{2,0},{3,1},{4,6},{5,7},{6,4},{7,5},{8,10},{9,11},{10,... | collective-permute-start | bytes 3538952 | tf_op jit(solution)/shard_map/ppermute | solution.py:40
  264.8 40.1 %collective-permute-start.18 = (bf16[2,2,2,2,192,384]{5,4,3,2,1,0:T(8,128)(2,1)S(1)}, bf16[2,2,2,2,192,384]{5,4,3,2,1,0:T(8,128)(2,1)}, u32[]{:S(2)}, u32[]{:S(2)}) collective-permute-start(bf16[2,2,2,2,192,384]{5,4,3,2,1,0:T(8,128)(2,1)S(1)} %maximum_select_fusion.4), channel_id=1, source_target_pairs={{0,1},{1,0},{2,3},{3,2},{4,5},{5,4},{6,7},{7,6},{8,9},{9,8},{10,11... | collective-permute-start | bytes 7077896 | tf_op jit(solution)/shard_map/ppermute | solution.py:40
  453.8 8.0 %collective-permute-start.25 = (bf16[16,352,384]{2,1,0:T(8,128)(2,1)}, bf16[16,352,384]{2,1,0:T(8,128)(2,1)}, u32[]{:S(2)}, u32[]{:S(2)}) collective-permute-start(bf16[16,352,384]{2,1,0:T(8,128)(2,1)} %get-tuple-element.95), channel_id=1, source_target_pairs={{0,1},{1,0},{2,3},{3,2},{4,5},{5,4},{6,7},{7,6},{8,9},{9,8},{10,11... | collective-permute-start | bytes 12976136 | tf_op jit(solution)/shard_map/ppermute | solution.py:40
  454.2 17.4 %collective-permute-start.44 = (bf16[16,384,384]{2,1,0:T(8,128)(2,1)}, bf16[16,384,384]{2,1,0:T(8,128)(2,1)}, u32[]{:S(2)}, u32[]{:S(2)}) collective-permute-start(bf16[16,384,384]{2,1,0:T(8,128)(2,1)} %get-tuple-element.101), channel_id=1, source_target_pairs={{0,1},{1,0},{2,3},{3,2},{4,5},{5,4},{6,7},{7,6},{8,9},{9,8},{10,11... | collective-permute-start | bytes 14155784 | tf_op jit(solution)/shard_map/ppermute | solution.py:40
  454.3 24.1 %collective-permute-start.38 = (bf16[16,384,384]{2,1,0:T(8,128)(2,1)}, bf16[16,384,384]{2,1,0:T(8,128)(2,1)}, u32[]{:S(2)}, u32[]{:S(2)}) collective-permute-start(bf16[16,384,384]{2,1,0:T(8,128)(2,1)} %get-tuple-element.99), channel_id=1, source_target_pairs={{0,1},{1,0},{2,3},{3,2},{4,5},{5,4},{6,7},{7,6},{8,9},{9,8},{10,11... | collective-permute-start | bytes 14155784 | tf_op jit(solution)/shard_map/ppermute | solution.py:40
  454.8 13.4 %collective-permute-start.32 = (bf16[16,192,384]{2,1,0:T(8,128)(2,1)}, bf16[16,192,384]{2,1,0:T(8,128)(2,1)S(1)}, u32[]{:S(2)}, u32[]{:S(2)}) collective-permute-start(bf16[16,192,384]{2,1,0:T(8,128)(2,1)} %get-tuple-element.97), channel_id=1, source_target_pairs={{0,1},{1,0},{2,3},{3,2},{4,5},{5,4},{6,7},{7,6},{8,9},{9,8},{10,11... | collective-permute-start | bytes 7077896 | tf_op jit(solution)/shard_map/ppermute | solution.py:40
  466.0 78.4 %collective-permute-start.26 = (bf16[2,2,2,1,352,384]{5,4,3,2,1,0:T(8,128)(2,1)}, bf16[2,2,2,1,352,384]{5,4,3,2,1,0:T(8,128)(2,1)}, u32[]{:S(2)}, u32[]{:S(2)}) collective-permute-start(bf16[2,2,2,1,352,384]{5,4,3,2,1,0:T(8,128)(2,1)} %add_convert_fusion.2), channel_id=1, source_target_pairs={{0,2},{1,3},{2,0},{3,1},{4,6},{5,7},{6,4},{7,5},{8,10},{9,11},{10,... | collective-permute-start | bytes 6488072 | tf_op jit(solution)/shard_map/ppermute | solution.py:40
  469.7 71.1 %collective-permute-start.33 = (bf16[2,2,2,1,192,384]{5,4,3,2,1,0:T(8,128)(2,1)}, bf16[2,2,2,1,192,384]{5,4,3,2,1,0:T(8,128)(2,1)S(1)}, u32[]{:S(2)}, u32[]{:S(2)}) collective-permute-start(bf16[2,2,2,1,192,384]{5,4,3,2,1,0:T(8,128)(2,1)} %add_convert_fusion.5), channel_id=1, source_target_pairs={{0,2},{1,3},{2,0},{3,1},{4,6},{5,7},{6,4},{7,5},{8,10},{9,11},{10,... | collective-permute-start | bytes 3538952 | tf_op jit(solution)/shard_map/ppermute | solution.py:40
  474.7 143.6 %collective-permute-start.45 = (bf16[2,2,1,2,384,384]{5,4,3,2,1,0:T(8,128)(2,1)S(1)}, bf16[2,2,1,2,384,384]{5,4,3,2,1,0:T(8,128)(2,1)}, u32[]{:S(2)}, u32[]{:S(2)}) collective-permute-start(bf16[2,2,1,2,384,384]{5,4,3,2,1,0:T(8,128)(2,1)S(1)} %add_convert_fusion), channel_id=1, source_target_pairs={{0,4},{4,0},{8,12},{12,8},{16,20},{20,16},{24,28},{28,24},{1,5},{5... | collective-permute-start | bytes 7077896 | tf_op jit(solution)/shard_map/ppermute | solution.py:40
  482.8 140.3 %collective-permute-start.39 = (bf16[2,2,1,2,384,384]{5,4,3,2,1,0:T(8,128)(2,1)}, bf16[2,2,1,2,384,384]{5,4,3,2,1,0:T(8,128)(2,1)}, u32[]{:S(2)}, u32[]{:S(2)}) collective-permute-start(bf16[2,2,1,2,384,384]{5,4,3,2,1,0:T(8,128)(2,1)} %add_convert_fusion.1), channel_id=1, source_target_pairs={{0,4},{4,0},{8,12},{12,8},{16,20},{20,16},{24,28},{28,24},{1,5},{5... | collective-permute-start | bytes 7077896 | tf_op jit(solution)/shard_map/ppermute | solution.py:40
  543.1 49.0 %collective-permute-start.34 = (bf16[2,2,1,1,192,384]{5,4,3,2,1,0:T(8,128)(2,1)}, bf16[2,2,1,1,192,384]{5,4,3,2,1,0:T(8,128)(2,1)}, u32[]{:S(2)}, u32[]{:S(2)}) collective-permute-start(bf16[2,2,1,1,192,384]{5,4,3,2,1,0:T(8,128)(2,1)} %add_convert_fusion.9), channel_id=1, source_target_pairs={{0,4},{4,0},{8,12},{12,8},{16,20},{20,16},{24,28},{28,24},{1,5},{5... | collective-permute-start | bytes 1769480 | tf_op jit(solution)/shard_map/ppermute | solution.py:40
  547.7 79.7 %collective-permute-start.27 = (bf16[2,2,1,1,352,384]{5,4,3,2,1,0:T(8,128)(2,1)}, bf16[2,2,1,1,352,384]{5,4,3,2,1,0:T(8,128)(2,1)}, u32[]{:S(2)}, u32[]{:S(2)}) collective-permute-start(bf16[2,2,1,1,352,384]{5,4,3,2,1,0:T(8,128)(2,1)} %add_convert_fusion.6), channel_id=1, source_target_pairs={{0,4},{4,0},{8,12},{12,8},{16,20},{20,16},{24,28},{28,24},{1,5},{5... | collective-permute-start | bytes 3244040 | tf_op jit(solution)/shard_map/ppermute | solution.py:40
  594.1 15.4 %collective-permute-start.35 = (bf16[1,2,1,1,192,384]{5,4,3,2,1,0:T(8,128)(2,1)}, bf16[1,2,1,1,192,384]{5,4,3,2,1,0:T(8,128)(2,1)}, u32[]{:S(2)}, u32[]{:S(2)}) collective-permute-start(bf16[1,2,1,1,192,384]{5,4,3,2,1,0:T(8,128)(2,1)} %add_convert_fusion.13), channel_id=1, source_target_pairs={{0,16},{4,20},{8,24},{12,28},{16,0},{20,4},{24,8},{28,12},{1,17},{... | collective-permute-start | bytes 884744 | tf_op jit(solution)/shard_map/ppermute | solution.py:40
  611.4 5.5 collective-permute-start.36
  621.8 33.9 %collective-permute-start.46 = (bf16[2,2,1,1,384,384]{5,4,3,2,1,0:T(8,128)(2,1)}, bf16[2,2,1,1,384,384]{5,4,3,2,1,0:T(8,128)(2,1)S(1)}, u32[]{:S(2)}, u32[]{:S(2)}) collective-permute-start(bf16[2,2,1,1,384,384]{5,4,3,2,1,0:T(8,128)(2,1)} %add_convert_fusion.3), channel_id=1, source_target_pairs={{0,2},{1,3},{2,0},{3,1},{4,6},{5,7},{6,4},{7,5},{8,10},{9,11},{10,... | collective-permute-start | bytes 3538952 | tf_op jit(solution)/shard_map/ppermute | solution.py:40
  626.6 45.7 %collective-permute-start.40 = (bf16[2,2,1,1,384,384]{5,4,3,2,1,0:T(8,128)(2,1)}, bf16[2,2,1,1,384,384]{5,4,3,2,1,0:T(8,128)(2,1)S(1)}, u32[]{:S(2)}, u32[]{:S(2)}) collective-permute-start(bf16[2,2,1,1,384,384]{5,4,3,2,1,0:T(8,128)(2,1)} %add_convert_fusion.4), channel_id=1, source_target_pairs={{0,2},{1,3},{2,0},{3,1},{4,6},{5,7},{6,4},{7,5},{8,10},{9,11},{10,... | collective-permute-start | bytes 3538952 | tf_op jit(solution)/shard_map/ppermute | solution.py:40
  629.1 23.4 %collective-permute-start.28 = (bf16[1,2,1,1,352,384]{5,4,3,2,1,0:T(8,128)(2,1)S(1)}, bf16[1,2,1,1,352,384]{5,4,3,2,1,0:T(8,128)(2,1)S(1)}, u32[]{:S(2)}, u32[]{:S(2)}) collective-permute-start(bf16[1,2,1,1,352,384]{5,4,3,2,1,0:T(8,128)(2,1)S(1)} %add_convert_fusion.10), channel_id=1, source_target_pairs={{0,16},{4,20},{8,24},{12,28},{16,0},{20,4},{24,8},{28,12},{1,17},{... | collective-permute-start | bytes 1622024 | tf_op jit(solution)/shard_map/ppermute | solution.py:40
  654.1 23.4 %collective-permute-start.29 = (bf16[1,1,1,1,352,384]{5,4,3,2,1,0:T(8,128)(2,1)S(1)}, bf16[1,1,1,1,352,384]{5,4,3,2,1,0:T(8,128)(2,1)}, u32[]{:S(2)}, u32[]{:S(2)}) collective-permute-start(bf16[1,1,1,1,352,384]{5,4,3,2,1,0:T(8,128)(2,1)S(1)} %add_convert_fusion.14), channel_id=1, source_target_pairs={{0,8},{4,12},{8,0},{12,4},{16,24},{20,28},{24,16},{28,20},{1,9},{5... | collective-permute-start | bytes 811016 | tf_op jit(solution)/shard_map/ppermute | solution.py:40
  658.3 43.2 %collective-permute-start.47 = (bf16[1,2,1,1,384,384]{5,4,3,2,1,0:T(8,128)(2,1)}, bf16[1,2,1,1,384,384]{5,4,3,2,1,0:T(8,128)(2,1)}, u32[]{:S(2)}, u32[]{:S(2)}) collective-permute-start(bf16[1,2,1,1,384,384]{5,4,3,2,1,0:T(8,128)(2,1)} %add_convert_fusion.7), channel_id=1, source_target_pairs={{0,16},{4,20},{8,24},{12,28},{16,0},{20,4},{24,8},{28,12},{1,17},{... | collective-permute-start | bytes 1769480 | tf_op jit(solution)/shard_map/ppermute | solution.py:40
  674.9 38.3 %collective-permute-start.41 = (bf16[1,2,1,1,384,384]{5,4,3,2,1,0:T(8,128)(2,1)}, bf16[1,2,1,1,384,384]{5,4,3,2,1,0:T(8,128)(2,1)}, u32[]{:S(2)}, u32[]{:S(2)}) collective-permute-start(bf16[1,2,1,1,384,384]{5,4,3,2,1,0:T(8,128)(2,1)} %add_convert_fusion.8), channel_id=1, source_target_pairs={{0,16},{4,20},{8,24},{12,28},{16,0},{20,4},{24,8},{28,12},{1,17},{... | collective-permute-start | bytes 1769480 | tf_op jit(solution)/shard_map/ppermute | solution.py:40
  703.6 15.8 %collective-permute-start.48 = (bf16[1,1,1,1,384,384]{5,4,3,2,1,0:T(8,128)(2,1)}, bf16[1,1,1,1,384,384]{5,4,3,2,1,0:T(8,128)(2,1)S(1)}, u32[]{:S(2)}, u32[]{:S(2)}) collective-permute-start(bf16[1,1,1,1,384,384]{5,4,3,2,1,0:T(8,128)(2,1)} %add_convert_fusion.11), channel_id=1, source_target_pairs={{0,8},{4,12},{8,0},{12,4},{16,24},{20,28},{24,16},{28,20},{1,9},{5... | collective-permute-start | bytes 884744 | tf_op jit(solution)/shard_map/ppermute | solution.py:40
  714.6 11.0 %collective-permute-start.42 = (bf16[1,1,1,1,384,384]{5,4,3,2,1,0:T(8,128)(2,1)S(1)}, bf16[1,1,1,1,384,384]{5,4,3,2,1,0:T(8,128)(2,1)S(1)}, u32[]{:S(2)}, u32[]{:S(2)}) collective-permute-start(bf16[1,1,1,1,384,384]{5,4,3,2,1,0:T(8,128)(2,1)S(1)} %add_convert_fusion.12), channel_id=1, source_target_pairs={{0,8},{4,12},{8,0},{12,4},{16,24},{20,28},{24,16},{28,20},{1,9},{5... | collective-permute-start | bytes 884744 | tf_op jit(solution)/shard_map/ppermute | solution.py:40
  721.0 6.8 collective-permute-start.49
  737.7 3.6 collective-permute-start.51
  741.3 3.6 collective-permute-start.52
  744.9 3.6 collective-permute-start.53
  748.5 4.5 collective-permute-start.54
  (65 other events, 528.6 us)

commit v2 on v1

v2 whole, which is shorter than its diff:
```python
from functools import partial, reduce

import jax
import jax.numpy as jnp
from jax import lax
from jax.experimental import pallas as pl
from jax.experimental.pallas import tpu as pltpu
from jax.sharding import PartitionSpec as P

D = 768
HEADS = 12
HEAD_DIM = 64
FF = 3072
V = 2026
M = 128
L = 2
UNIT = 384
VPAD = 2304
BOTH = ("dp", "fsdp")


epsilon = 1e-06
step_rate = 10000.0
inertia = 0.5
average_decay = 0.5
clip_bound = 0.01


HOPS = {
    "zhi": ("dp", 4, 8, 0),
    "zlo": ("dp", 2, 8, 1),
    "y": ("dp", 1, 8, 2),
    "x": ("fsdp", 2, 4, 3),
    "core": ("fsdp", 1, 4, None),
}

PIECES = {"T": (160, ((3, 24),))}
for layer in range(L):
    PIECES.update(
        {
            f"Q{layer}": (144, ((3, 24),)),
            f"O{layer}": (48, ((1, 24),)),
            f"D{layer}": (192, ((1, 96),)),
            f"E{layer}": (96, ((2, 24),)),
            f"F{layer}": (96, ((2, 24),)),
        }
    )

GATHER = {
    "t": ("T",),
    "a": ("Q0", "O0"),
    "d": ("D0",),
    "u": ("E0", "F0"),
    "l": ("Q1", "O1", "D1", "E1", "F1"),
}
GATHER_WAY = {
    "t": ("zlo", "zhi", "y", "x"),
    "a": ("zlo", "zhi", "x", "y"),
    "d": ("zlo", "zhi", "y", "x"),
    "u": ("zlo", "zhi", "x", "y"),
}
SCATTER = {
    "l": ("Q1", "O1", "D1", "E1", "F1"),
    "d": ("D0",),
    "u": ("E0", "F0"),
    "a": ("Q0", "O0"),
    "t": ("T",),
}
SCATTER_WAY = {
    "d": ("x", "y", "zhi", "zlo"),
    "u": ("y", "zhi", "zlo", "x"),
    "a": ("y", "x", "zhi", "zlo"),
    "t": ("x", "zhi", "zlo", "y"),
}
FORWARD_ORDER = (
    ("t", "a", "d", "u", "t", "a", "t", "a", "d", "u", "t", "a", "embed", "d", "u", "attention0", "d", "u")
    + ("forward0", "attention1", "forward1", "head")
)
BACKWARD_ORDER = (
    ("forward1", "attention1", "forward0", "attention0", "u", "d", "a", "embed", "t", "u", "d", "t", "a")
    + ("u", "d", "u", "a", "t", "u", "d", "t", "d", "a", "t", "a")
)
LAST = (("l", "u"), ("d", "t", "a"))


def placed(layout):
    places = {}
    for name, pieces in layout.items():
        start = 0
        for piece in pieces:
            places[piece] = (name, start)
            start += PIECES[piece][0]
    return places


def height(pieces):
    return sum(PIECES[piece][0] for piece in pieces)


def swap(tensor, hop):
    axis, flip, size, unused = HOPS[hop]
    return lax.ppermute(tensor, axis, [(i, i ^ flip) for i in range(size)])


def side(hop):
    axis, flip, unused, unused = HOPS[hop]
    return (lax.axis_index(axis) // flip) % 2


def in_order(bit, own, other, axis):
    return jnp.where(
        bit == 0, jnp.concatenate([own, other], axis), jnp.concatenate([other, own], axis)
    )


def pick(tensor, index, axis):
    return lax.dynamic_slice_in_dim(tensor, index, 1, axis)


def column_units(shard):
    rows, width = shard.shape
    return shard.reshape(rows, 2, width // (2 * UNIT), UNIT).transpose(1, 2, 0, 3)


def natural_weight(halves, units, rows):
    chips = halves.shape[1]
    block = halves.reshape(2, chips, units, rows, UNIT)
    return block.transpose(1, 3, 0, 2, 4).reshape(chips * rows, 2 * units * UNIT)


def weight_blocks(grad, units, rows):
    chips = grad.shape[0] // rows
    block = grad.reshape(chips, rows, 2, units, UNIT).transpose(2, 0, 3, 1, 4)
    return block.reshape(2, chips, units * rows, UNIT)


TOKENS = 512
SLOTS = 256
ANY = pl.BlockSpec(memory_space=pl.ANY)
SMEM = pl.BlockSpec(memory_space=pltpu.SMEM)
VMEM = pl.BlockSpec(memory_space=pltpu.VMEM)
low = jnp.bfloat16
full = jnp.float32


def dot(left, right):
    return lax.dot_general(left, right, (((1,), (0,)), ((), ())), preferred_element_type=full)


def dot_right(left, right):
    return lax.dot_general(left, right, (((1,), (1,)), ((), ())), preferred_element_type=full)


def dot_left(left, right):
    return lax.dot_general(left, right, (((0,), (0,)), ((), ())), preferred_element_type=full)


def norm_parts(stream):
    centre = stream - jnp.mean(stream, -1, keepdims=True)
    spread = lax.rsqrt(jnp.mean(centre * centre, -1, keepdims=True) + epsilon)
    return centre * spread, spread


def norm_back(upstream, scaled, spread, gain):
    weighted = upstream * gain
    return spread * (
        weighted
        - jnp.mean(weighted, -1, keepdims=True)
        - scaled * jnp.mean(weighted * scaled, -1, keepdims=True)
    )


def rows_sum(tensor):
    return jnp.sum(tensor, 0, keepdims=True)


def columns(start, size):
    return pl.ds(pl.multiple_of(start, 128), size)


def unit_copies(core, halves, at, units, first, half_units, target, sems):
    copies = []
    for which, source in enumerate(halves):
        half = core if which == 0 else 1 - core
        if len(source.shape) == 4:
            source = source.at[:, half]
        for unit in range(units):
            copies.append(
                pltpu.make_async_copy(
                    source.at[:, pl.ds(at + 48 * unit, 48), :],
                    target.at[:, :, columns((half * half_units + first + unit) * UNIT, UNIT)],
                    sems.at[which * units + unit],
                )
            )
    return copies


def flat(block):
    return block.reshape(block.shape[0] * block.shape[1], block.shape[2])


def head_mask(shape, which):
    lane = lax.broadcasted_iota(jnp.int32, shape, 1)
    return lane < HEAD_DIM if which == 0 else lane >= HEAD_DIM


def embed_kernel(at, core, codes, pos, valid, mine, yours, ids, stream, weight, sems):
    copies = unit_copies(core[0], (mine, yours), at, 3, 0, 3, weight, sems)
    for copy in copies:
        copy.start()
    place = lax.broadcasted_iota(jnp.int32, (TOKENS, SLOTS), 0)
    masked = jnp.max(jnp.where(place == pos[...], valid[...], 0.0), -1, keepdims=True)
    tokens = jnp.where(masked > 0, V - 1, codes[...])
    ids[...] = tokens
    for copy in copies:
        copy.wait()
    acc = jnp.zeros((TOKENS, D), full)
    for tile in range(3):
        word = lax.broadcasted_iota(jnp.int32, (TOKENS, D), 1) + tile * D
        hot = jnp.where(word == tokens, 1.0, 0.0).astype(low)
        acc += dot_right(hot, flat(weight[:, :, tile * D : (tile + 1) * D]))
    stream[...] = acc


def attention_kernel(
    ats, core, stream, vector, *refs
):
    in_pair, out_pair = refs[0:2], refs[2:4]
    triple, lse, mixed, middle, w_in, w_out, sems = refs[4:]
    in_copies = unit_copies(core[0], in_pair, ats[0], 3, 0, 3, w_in, sems.at[pl.ds(0, 6)])
    out_copies = unit_copies(core[0], out_pair, ats[1], 1, 0, 1, w_out, sems.at[pl.ds(6, 2)])
    for copy in in_copies + out_copies:
        copy.start()
    scaled, unused = norm_parts(stream[...])
    normed = (scaled * vector[0:1] + vector[1:2]).astype(low)
    for copy in in_copies:
        copy.wait()
    for part in range(3):
        block = dot(normed, flat(w_in[:, :, part * D : (part + 1) * D]))
        if part == 0:
            block = block + vector[2:3]
        if part == 2:
            block = block + vector[3:4]
        triple[part] = block.astype(low)
    lse[...] = jnp.zeros_like(lse)
    shape = (256, 128)
    lane = lax.broadcasted_iota(jnp.int32, shape, 1)

    def pair(step, carry):
        here = columns(step * 128, 128)
        for image in range(2):
            rows = slice(256 * image, 256 * image + 256)
            queries, key_rows, values = triple[0, rows, here], triple[1, rows, here], triple[2, rows, here]
            results = []
            for which in range(2):
                query = jnp.where(head_mask(shape, which), queries, jnp.zeros_like(queries))
                scores = dot_right(query, key_rows) * HEAD_DIM ** (-0.5)
                peak = jnp.max(scores, -1, keepdims=True)
                raised = jnp.exp(scores - peak)
                total = jnp.sum(raised, -1, keepdims=True)
                probs = (raised * (1.0 / total)).astype(low)
                results.append(dot(probs, values))
                lse[rows] = jnp.where(lane == 2 * step + which, peak + jnp.log(total), lse[rows])
            mixed[rows, here] = jnp.where(head_mask(shape, 0), results[0], results[1]).astype(low)
        return carry

    lax.fori_loop(0, HEADS // 2, pair, 0)
    for copy in out_copies:
        copy.wait()
    middle[...] = stream[...] + dot(mixed[...], flat(w_out[...])) + vector[4:5]


def forward_copies(core, ats, pairs, w_up, w_down, sems):
    first = unit_copies(core, pairs[1], ats[1], 2, 0, 4, w_up, sems.at[pl.ds(0, 4)])
    second = unit_copies(core, pairs[2], ats[2], 2, 2, 4, w_up, sems.at[pl.ds(4, 4)])
    up = first[:2] + second[:2] + first[2:] + second[2:]
    down = []
    for tile in range(4):
        chips = pl.ds(4 * lax.rem(2 * core + tile, 4), 4)
        for which, source in enumerate(pairs[0]):
            half = core if which == 0 else 1 - core
            if len(source.shape) == 4:
                source = source.at[:, half]
            down.append(
                pltpu.make_async_copy(
                    source.at[chips, pl.ds(ats[0], 192), :],
                    w_down.at[chips, :, columns(half * UNIT, UNIT)],
                    sems.at[8 + 2 * tile + which],
                )
            )
    return [up[2 * tile : 2 * tile + 2] + down[2 * tile : 2 * tile + 2] for tile in range(4)]


CURVE = 0.7978845608028654


def forward_kernel(ats, core, middle, vector, *refs):
    pairs = [refs[0:2], refs[2:4], refs[4:6]]
    hidden, result, w_up, w_down, normed, stage, sems, out_sems = refs[6:]
    copies = forward_copies(core[0], ats, pairs, w_up, w_down, sems)
    for group in copies:
        for copy in group:
            copy.start()
    scaled, unused = norm_parts(middle[...])
    normed[...] = (scaled * vector[5:6] + vector[6:7]).astype(low)
    result[...] = middle[...] + vector[7:8]
    sent = []
    for step in range(4):
        tile = lax.rem(2 * core[0] + step, 4)
        for copy in copies[step]:
            copy.wait()
        block = dot(normed[...], flat(w_up[:, :, columns(tile * D, D)])) + vector[pl.ds(8 + tile, 1)]
        if step >= 2:
            sent[step - 2].wait()
        stage[step % 2] = block
        copy = pltpu.make_async_copy(stage.at[step % 2], hidden.at[tile], out_sems.at[step % 2])
        copy.start()
        sent.append(copy)
        bent = jnp.tanh(CURVE * (block + 0.044715 * (block * block * block)))
        active = (0.5 * block * (1.0 + bent)).astype(low)
        result[...] += dot(active, flat(w_down[pl.ds(4 * tile, 4)]))
    for copy in sent[2:]:
        copy.wait()


def head_kernel(
    at,
    core,
    stream,
    final,
    codes,
    pos_column,
    pos_row,
    scale,
    valid,
    bias,
    mine,
    yours,
    upstream,
    chosen_out,
    grad_logits_out,
    bias_grad,
    final_grad,
    loss,
    weight,
    logits,
    sems,
):
    copies = unit_copies(core[0], (mine, yours), at, 3, 0, 3, weight, sems)
    for copy in copies:
        copy.start()
    scaled, spread = norm_parts(stream[...])
    normed = (scaled * final[0:1] + final[1:2]).astype(low)
    picker = lax.broadcasted_iota(jnp.int32, (SLOTS, TOKENS), 1) == pos_column[...]
    target = jnp.sum(jnp.where(picker, codes[...], 0), -1, keepdims=True)
    chosen = dot(picker.astype(full).astype(low), normed).astype(low)
    chosen_out[...] = chosen
    for copy in copies:
        copy.wait()
    peak = jnp.full((SLOTS, 1), -jnp.inf, full)
    picked = jnp.zeros((SLOTS, 1), full)
    for tile in range(3):
        here = slice(tile * D, tile * D + D)
        block = dot(chosen, flat(weight[:, :, here])) + bias[:, here]
        logits[:, here] = block
        peak = jnp.maximum(peak, jnp.max(block, -1, keepdims=True))
        word = lax.broadcasted_iota(jnp.int32, (SLOTS, D), 1) + tile * D
        picked += jnp.sum(jnp.where(word == target, block, 0.0), -1, keepdims=True)
    total = jnp.zeros((SLOTS, 1), full)
    for tile in range(3):
        total += jnp.sum(jnp.exp(logits[:, tile * D : tile * D + D] - peak), -1, keepdims=True)
    log_total = peak + jnp.log(total)
    loss[...] = jnp.broadcast_to(rows_sum(valid[...] * (log_total - picked)), (1, 128))
    grad_chosen = jnp.zeros((SLOTS, D), full)
    for tile in range(3):
        here = slice(tile * D, tile * D + D)
        word = lax.broadcasted_iota(jnp.int32, (SLOTS, D), 1) + tile * D
        chance = jnp.exp(logits[:, here] - log_total)
        block = ((chance - jnp.where(word == target, 1.0, 0.0)) * scale[...]).astype(low)
        grad_logits_out[:, here] = block
        bias_grad[:, here] = rows_sum(block.astype(full))
        grad_chosen += dot_right(block, flat(weight[:, :, here]))
    back = lax.broadcasted_iota(jnp.int32, (TOKENS, SLOTS), 0) == pos_row[...]
    back = back.astype(full).astype(low)
    grad_normed = jnp.zeros((TOKENS, D), full)
    for unused in range(3):
        piece = grad_chosen.astype(low)
        grad_normed += dot(back, piece)
        grad_chosen -= piece.astype(full)
    final_grad[0:1] = rows_sum(grad_normed * scaled)
    final_grad[1:2] = rows_sum(grad_normed)
    upstream[...] = norm_back(grad_normed, scaled, spread, final[0:1])


def leave(source, target, half, at, sem):
    return pltpu.make_async_copy(source, target.at[:, half, pl.ds(at, 48), :], sem)


def forward_back_kernel(ats, outs, carried, core, upstream, middle, vector, hidden, *refs):
    pairs = [refs[0:2], refs[2:4], refs[4:6]]
    refs = refs[6 + carried :]
    grad_middle, vector_grad = refs[0:2]
    targets = refs[2:-11]
    w_up, w_down, normed_t, branch, hidden_tile, down_stage, up_stage, acc = refs[-11:-3]
    sems, hidden_sems, out_sems = refs[-3:]
    own = core[0]
    tiles = [lax.rem(2 * own + step, 4) for step in range(4)]
    fetch = [
        pltpu.make_async_copy(hidden.at[tiles[step]], hidden_tile.at[step % 2], hidden_sems.at[step % 2])
        for step in range(4)
    ]
    fetch[0].start()
    copies = forward_copies(own, ats, pairs, w_up, w_down, sems)
    for group in copies:
        for copy in group:
            copy.start()
    scaled, spread = norm_parts(middle[...])
    normed_t[...] = (scaled * vector[5:6] + vector[6:7]).T.astype(low)
    branch[...] = upstream[...].astype(low)
    vector_grad[...] = jnp.zeros_like(vector_grad)
    vector_grad[7:8] = rows_sum(branch[...].astype(full))
    acc[...] = jnp.zeros_like(acc)
    every = slice(None)
    flights = []

    def land(step):
        for copy in flights[step]:
            copy.wait()

    for step in range(4):
        tile, slot = tiles[step], step % 2
        if step < 3:
            fetch[step + 1].start()
        for copy in copies[step]:
            copy.wait()
        fetch[step].wait()
        block = hidden_tile[slot]
        square = block * block
        bent = jnp.tanh(CURVE * (block + 0.044715 * (square * block)))
        active = (0.5 * block * (1.0 + bent)).astype(low)
        slope = 0.5 * (1.0 + bent) + 0.5 * block * (1.0 - bent * bent) * (
            CURVE * (1.0 + (3.0 * 0.044715) * square)
        )
        back = dot_right(branch[...], flat(w_down[pl.ds(4 * tile, 4)]))
        grad_hidden = (slope * back).astype(low)
        vector_grad[pl.ds(8 + tile, 1)] = rows_sum(grad_hidden.astype(full))
        if step >= 2:
            land(step - 2)
        grad_down = dot(active.T, branch[...]).astype(low)
        down_stage[slot] = grad_down.reshape(4, 192, D)
        flight = []
        for half in range(2):
            place = targets[outs[0][0]].at[pl.ds(4 * tile, 4), half, pl.ds(outs[0][1], 192), :]
            source = down_stage.at[slot, :, :, pl.ds(half * UNIT, UNIT)]
            flight.append(pltpu.make_async_copy(source, place, out_sems.at[slot, half]))
        grad_up = dot(normed_t[...], grad_hidden).astype(low)
        up_stage[slot] = grad_up.reshape(16, 48, D)
        half = own if step < 2 else 1 - own
        for unit in range(2):
            source = up_stage.at[slot, :, :, pl.ds(unit * UNIT, UNIT)]
            at = outs[1 + slot][1] + 48 * unit
            flight.append(leave(source, targets[outs[1 + slot][0]], half, at, out_sems.at[slot, 2 + unit]))
        for copy in flight:
            copy.start()
        flights.append(flight)
        acc[...] += dot_right(grad_hidden, flat(w_up[:, :, columns(tile * D, D)]))
    grad_normed = acc[...]
    scaled, spread = norm_parts(middle[...])
    vector_grad[5:6] = rows_sum(grad_normed * scaled)
    vector_grad[6:7] = rows_sum(grad_normed)
    grad_middle[...] = upstream[...] + norm_back(grad_normed, scaled, spread, vector[5:6])
    land(2)
    land(3)


def attention_back_kernel(
    ats, outs, carried, core, grad_middle, stream, vector, triple, lse, mixed, *refs
):
    in_pair, out_pair = refs[0:2], refs[2:4]
    refs = refs[4 + carried :]
    upstream, vector_grad = refs[0:2]
    targets = refs[2:-7]
    w_in, w_out, grad_mixed, grad_triple, stage, sems, out_sems = refs[-7:]
    target, at = targets[outs[0][0]], outs[0][1]
    out_target, out_at = targets[outs[1][0]], outs[1][1]
    leaving = []
    own = core[0]
    out_copies = unit_copies(own, out_pair, ats[1], 1, 0, 1, w_out, sems.at[pl.ds(6, 2)])
    in_copies = unit_copies(own, in_pair, ats[0], 3, 0, 3, w_in, sems.at[pl.ds(0, 6)])
    for copy in out_copies + in_copies:
        copy.start()
    every = slice(None)
    grad_out_low = grad_middle[...].astype(low)
    vector_grad[...] = jnp.zeros_like(vector_grad)
    vector_grad[4:5] = rows_sum(grad_out_low.astype(full))
    stage[3] = dot(mixed[...].T, grad_out_low).astype(low).reshape(16, 48, D)
    for half in range(2):
        source = stage.at[3, :, :, pl.ds(half * UNIT, UNIT)]
        leaving.append(leave(source, out_target, half, out_at, out_sems.at[6 + half]))
        leaving[-1].start()
    for copy in out_copies:
        copy.wait()
    grad_mixed[...] = dot_right(grad_out_low, flat(w_out[...])).astype(low)
    shape = (256, 128)
    lane = lax.broadcasted_iota(jnp.int32, shape, 1)

    def pair(step, carry):
        here = columns(step * 128, 128)
        for image in range(2):
            rows = slice(256 * image, 256 * image + 256)
            queries, key_rows, values = triple[0, rows, here], triple[1, rows, here], triple[2, rows, here]
            grads = grad_mixed[rows, here]
            outs = []
            for which in range(2):
                mask = head_mask(shape, which)
                none = jnp.zeros_like(queries)
                scores = dot_right(jnp.where(mask, queries, none), key_rows) * HEAD_DIM ** (-0.5)
                total = jnp.sum(jnp.where(lane == 2 * step + which, lse[rows], 0.0), -1, keepdims=True)
                probs = jnp.exp(scores - total)
                grad_values = dot_left(probs.astype(low), grads)
                grad_probs = dot_right(jnp.where(mask, grads, none), values)
                inner = jnp.sum(probs * grad_probs, -1, keepdims=True)
                grad_scores = (probs * (grad_probs - inner)).astype(low)
                grad_queries = dot(grad_scores, key_rows) * HEAD_DIM ** (-0.5)
                grad_keys = dot_left(grad_scores, queries) * HEAD_DIM ** (-0.5)
                outs.append((grad_queries, grad_keys, grad_values))
            first = head_mask(shape, 0)
            for part in range(3):
                grad_triple[part, rows, here] = jnp.where(first, outs[0][part], outs[1][part]).astype(low)
        return carry

    lax.fori_loop(0, HEADS // 2, pair, 0)
    scaled, spread = norm_parts(stream[...])
    normed_t = (scaled * vector[0:1] + vector[1:2]).T.astype(low)
    for copy in in_copies:
        copy.wait()
    grad_normed = jnp.zeros((TOKENS, D), full)
    for part in range(3):
        block = grad_triple[part]
        if part == 0:
            vector_grad[2:3] = rows_sum(block.astype(full))
        if part == 2:
            vector_grad[3:4] = rows_sum(block.astype(full))
        stage[part] = dot(normed_t, block).astype(low).reshape(16, 48, D)
        for side_unit in range(2):
            unit = 2 * part + side_unit
            source = stage.at[part, :, :, pl.ds(side_unit * UNIT, UNIT)]
            leaving.append(leave(source, target, unit // 3, at + 48 * (unit % 3), out_sems.at[unit]))
            leaving[-1].start()
        grad_normed += dot_right(block, flat(w_in[:, :, part * D : (part + 1) * D]))
    vector_grad[0:1] = rows_sum(grad_normed * scaled)
    vector_grad[1:2] = rows_sum(grad_normed)
    upstream[...] = grad_middle[...] + norm_back(grad_normed, scaled, spread, vector[0:1])
    for copy in leaving:
        copy.wait()


def embed_back_kernel(at, carried, upstream, ids, chosen, grad_logits, small, *refs):
    target, stage, sems = refs[carried:]
    leaving = [pltpu.make_async_copy(small, target.at[:, :, pl.ds(at + 144, 16), :], sems.at[6])]
    leaving[0].start()
    stream_t = upstream[...].T.astype(low)
    chosen_t = chosen[...].astype(full).T.astype(low)
    for tile in range(3):
        word = lax.broadcasted_iota(jnp.int32, (TOKENS, D), 1) + tile * D
        hot = jnp.where(word == ids[...], 1.0, 0.0).astype(low)
        block = dot(stream_t, hot) + dot(chosen_t, grad_logits[:, tile * D : tile * D + D])
        stage[tile] = block.astype(low).reshape(16, 48, D)
        for side_unit in range(2):
            unit = 2 * tile + side_unit
            source = stage.at[tile, :, :, pl.ds(side_unit * UNIT, UNIT)]
            leaving.append(leave(source, target, unit // 3, at + 48 * (unit % 3), sems.at[unit]))
            leaving[-1].start()
    for copy in leaving:
        copy.wait()


def shape_of(*dims, kind=full):
    return jax.ShapeDtypeStruct(dims, kind)


class Line:
    def __init__(self, token):
        self.token = token

    def call(self, kernel, operands, in_specs, outs, out_specs, scratch, grid=None, prefetch=0, aliases=None, cost=0):
        def ordered(*refs):
            return kernel(*refs[:prefetch], *refs[prefetch + 1 :])

        in_specs = [ANY] + in_specs
        if grid is None:
            how = dict(in_specs=in_specs, out_specs=out_specs, scratch_shapes=scratch)
        else:
            spec = pltpu.PrefetchScalarGridSpec(
                num_scalar_prefetch=prefetch,
                grid=grid,
                in_specs=in_specs,
                out_specs=out_specs,
                scratch_shapes=scratch,
            )
            how = dict(grid_spec=spec)
        results = pl.pallas_call(
            ordered,
            out_shape=outs,
            compiler_params=pltpu.CompilerParams(vmem_limit_bytes=56 * 2**20),
            cost_estimate=pl.CostEstimate(flops=1000 + int(cost * 1.15e9), bytes_accessed=1000, transcendentals=0),
            input_output_aliases={source + 1: target for source, target in (aliases or {}).items()},
            **how,
        )(*operands[:prefetch], self.token, *operands[prefetch:])
        self.token = results[0]
        return results


DMA = pltpu.SemaphoreType.DMA
MERGE_COST, JOIN_COST = 3, 3


def embed(line, core, codes, pos, valid, pair, at):
    return line.call(
        partial(embed_kernel, at),
        (core, codes, pos, valid, *pair),
        [SMEM, VMEM, VMEM, VMEM, ANY, ANY],
        (shape_of(TOKENS, 1, kind=jnp.int32), shape_of(TOKENS, D)),
        (VMEM, VMEM),
        [pltpu.VMEM((16, 48, VPAD), low), DMA((6,))],
        cost=6,
    )


def attention(line, core, stream, vector, pairs, ats):
    return line.call(
        partial(attention_kernel, ats),
        (core, stream, vector, *pairs[0], *pairs[1]),
        [SMEM, VMEM, VMEM] + [ANY] * 4,
        (
            shape_of(3, TOKENS, D, kind=low),
            shape_of(TOKENS, 128),
            shape_of(TOKENS, D, kind=low),
            shape_of(TOKENS, D),
        ),
        (VMEM,) * 4,
        [pltpu.VMEM((16, 48, 3 * D), low), pltpu.VMEM((16, 48, D), low), DMA((8,))],
        cost=15,
    )


def feed_forward(line, core, middle, vector, pairs, ats):
    return line.call(
        partial(forward_kernel, ats),
        (core, middle, vector, *pairs[0], *pairs[1], *pairs[2]),
        [SMEM, VMEM, VMEM] + [ANY] * 6,
        (shape_of(4, TOKENS, D), shape_of(TOKENS, D)),
        (ANY, VMEM),
        [
            pltpu.VMEM((16, 48, FF), low),
            pltpu.VMEM((16, 192, D), low),
            pltpu.VMEM((TOKENS, D), low),
            pltpu.VMEM((2, TOKENS, D), full),
            DMA((16,)),
            DMA((2,)),
        ],
        cost=12,
    )


def head(line, core, stream, final, codes, pos_column, pos_row, scale, valid, bias, pair, at):
    return line.call(
        partial(head_kernel, at),
        (core, stream, final, codes, pos_column, pos_row, scale, valid, bias, *pair),
        [SMEM] + [VMEM] * 8 + [ANY, ANY],
        (
            shape_of(TOKENS, D),
            shape_of(SLOTS, D, kind=low),
            shape_of(SLOTS, VPAD, kind=low),
            shape_of(1, VPAD),
            shape_of(2, D),
            shape_of(1, 128),
        ),
        (VMEM,) * 6,
        [pltpu.VMEM((16, 48, VPAD), low), pltpu.VMEM((SLOTS, VPAD), full), DMA((6,))],
        cost=10,
    )


class Grads:
    def __init__(self):
        self.places, self.arrays = placed(SCATTER), {}

    def results(self, pieces, before, first):
        names = sorted({self.places[piece][0] for piece in pieces})
        operands, shapes, aliases = [], [], {}
        for name in names:
            if name in self.arrays:
                aliases[before + len(operands)] = first + len(shapes)
                operands.append(self.arrays[name])
            shapes.append(shape_of(16, 2, height(SCATTER[name]), UNIT, kind=low))
        spots = tuple((names.index(self.places[piece][0]), self.places[piece][1]) for piece in pieces)
        return names, operands, shapes, aliases, spots


def feed_forward_back(line, grads, layer, core, upstream, middle, vector, hidden, pairs, ats):
    names, more, shapes, aliases, spots = grads.results((f"D{layer}", f"E{layer}", f"F{layer}"), 11, 2)
    results = line.call(
        partial(forward_back_kernel, ats, spots, len(more)),
        (core, upstream, middle, vector, hidden, *pairs[0], *pairs[1], *pairs[2], *more),
        [SMEM, VMEM, VMEM, VMEM] + [ANY] * (7 + len(more)),
        (shape_of(TOKENS, D), shape_of(12, D), *shapes),
        (VMEM, VMEM) + (ANY,) * len(shapes),
        [
            pltpu.VMEM((16, 48, FF), low),
            pltpu.VMEM((16, 192, D), low),
            pltpu.VMEM((D, TOKENS), low),
            pltpu.VMEM((TOKENS, D), low),
            pltpu.VMEM((2, TOKENS, D), full),
            pltpu.VMEM((2, 4, 192, D), low),
            pltpu.VMEM((2, 16, 48, D), low),
            pltpu.VMEM((TOKENS, D), full),
            DMA((16,)),
            DMA((2,)),
            DMA((2, 4)),
        ],
        aliases=aliases,
        cost=22,
    )
    grads.arrays.update(zip(names, results[2:]))
    return results[:2]


def attention_back(line, grads, layer, core, grad_middle, stream, vector, triple, lse, mixed, pairs, ats):
    names, more, shapes, aliases, spots = grads.results((f"Q{layer}", f"O{layer}"), 11, 2)
    results = line.call(
        partial(attention_back_kernel, ats, spots, len(more)),
        (core, grad_middle, stream, vector, triple, lse, mixed, *pairs[0], *pairs[1], *more),
        [SMEM] + [VMEM] * 6 + [ANY] * (4 + len(more)),
        (shape_of(TOKENS, D), shape_of(12, D), *shapes),
        (VMEM, VMEM) + (ANY,) * len(shapes),
        [
            pltpu.VMEM((16, 48, 3 * D), low),
            pltpu.VMEM((16, 48, D), low),
            pltpu.VMEM((TOKENS, D), low),
            pltpu.VMEM((3, TOKENS, D), low),
            pltpu.VMEM((4, 16, 48, D), low),
            DMA((8,)),
            DMA((8,)),
        ],
        aliases=aliases,
        cost=24,
    )
    grads.arrays.update(zip(names, results[2:]))
    return results[:2]


def embed_back(line, grads, upstream, ids, chosen, grad_logits, small):
    names, more, shapes, aliases, spots = grads.results(("T",), 5, 0)
    results = line.call(
        partial(embed_back_kernel, spots[0][1], len(more)),
        (upstream, ids, chosen, grad_logits, small, *more),
        [VMEM] * 4 + [ANY] * (1 + len(more)),
        tuple(shapes),
        (ANY,) * len(shapes),
        [pltpu.VMEM((3, 16, 48, D), low), DMA((8,))],
        aliases=aliases,
        cost=15,
    )
    grads.arrays.update(zip(names, results))


def join(line, bits, axis, own, other):
    dims = list(own.shape)
    dims[axis] = 2
    cut = next((i for i in range(4) if own.shape[i] == 2), None)
    steps = 1 if cut is None else 2

    def kernel(bits_ref, own_ref, other_ref, out, stage, in_sems, out_sems):
        loads, stores = [], []
        for step in range(steps):
            for which, source in enumerate((own_ref, other_ref)):
                slot = 2 * step + which
                part = [slice(None)] * 4
                if cut is not None:
                    part[cut] = pl.ds(step, 1)
                loads.append(pltpu.make_async_copy(source.at[tuple(part)], stage.at[slot], in_sems.at[slot]))
                place = bits_ref[axis] if which == 0 else 1 - bits_ref[axis]
                part[axis] = pl.ds(place, 1)
                stores.append(pltpu.make_async_copy(stage.at[slot], out.at[tuple(part)], out_sems.at[slot]))
        for copy in loads:
            copy.start()
        for load, store in zip(loads, stores):
            load.wait()
            store.start()
        for copy in stores:
            copy.wait()

    block = [1 if i == cut else size for i, size in enumerate(own.shape)]
    scratch = [pltpu.VMEM((2 * steps, *block), low), DMA((2 * steps,)), DMA((2 * steps,))]
    operands = (bits, own, other)
    return line.call(kernel, operands, [SMEM, ANY, ANY], (shape_of(*dims, kind=low),), (ANY,), scratch, cost=JOIN_COST)[0]


def merge(line, bits, parts, gone, axis, kind=None):
    rows = parts[-1].shape[-2]
    open_axes = [i for i in range(4) if i not in gone and i != axis]
    dims = [2 if i in open_axes else 1 for i in range(4)]
    kind = kind or (full if axis is None else low)
    cut = open_axes[0] if open_axes else None
    block = [1 if i == cut else size for i, size in enumerate(dims)]

    def spec(shape):
        def index(step, bits_ref):
            place = []
            for i in range(4):
                if i == cut:
                    place.append(step)
                elif shape[i] == 1 or i in open_axes:
                    place.append(0)
                else:
                    place.append(1 - bits_ref[i] if i == axis else bits_ref[i])
            if len(shape) == 7:
                place.append(bits_ref[4])
            return (*place, 0, 0)

        return pl.BlockSpec((*block, *(None,) * (len(shape) - 6), rows, UNIT), index)

    def kernel(bits_ref, *refs):
        total = refs[0][...].astype(full)
        for ref in refs[1:-1]:
            total += ref[...].astype(full)
        refs[-1][...] = total.astype(kind)

    return line.call(
        kernel,
        (bits, *parts),
        [spec(part.shape) for part in parts],
        (shape_of(*dims, rows, UNIT, kind=kind),),
        (spec((*dims, rows, UNIT)),),
        [],
        grid=(1 if cut is None else 2,),
        prefetch=1,
        cost=MERGE_COST,
    )[0]


def update(weight, moment, average, grad, factor):
    clipped = grad * factor
    moment_next = inertia * moment + clipped
    weight_next = weight - step_rate * (clipped + inertia * moment_next)
    return (weight_next, moment_next, average_decay * average + (1.0 - average_decay) * weight_next)


def pack_small(vecs, final_norm, counts):
    own = jnp.concatenate(
        [vecs[0], vecs[1], final_norm[0], final_norm[1], counts.astype(full)]
    ).astype(low)
    own = jnp.pad(own, (0, 2 * UNIT - own.shape[0])).reshape(2, UNIT)
    return jnp.pad(own, ((0, 14), (0, 0)))


def body(hops, *arguments):
    codes, mask_pos, mask_count, table, w_qkv, w_out, w_up, w_down = arguments[:8]
    layer_vecs, final_norm, head_bias = arguments[8:11]
    moments, averages = arguments[11:19], arguments[19:27]
    images, seq_len = codes.shape
    core = side("core") if hops else jnp.zeros((), jnp.int32)
    own = core.astype(jnp.int32).reshape(1)
    line = Line(own)
    places = placed(GATHER)
    table_t = jnp.pad(table.T, ((0, 0), (0, VPAD - V)))
    shards = {"T": table_t}
    for l in range(L):
        shards[f"Q{l}"], shards[f"O{l}"], shards[f"D{l}"] = w_qkv[l], w_out[l], w_down[l]
        shards[f"U{l}"] = w_up[l]

    def split_up(make):
        out = {}
        for name, shard in shards.items():
            if name[0] == "U":
                block = make(shard, 4, PIECES["E0"][1][0][1])
                half = block.shape[-2] // 2
                out["E" + name[1]], out["F" + name[1]] = block[..., :half, :], block[..., half:, :]
            else:
                out[name] = make(shard, *PIECES[name][1][0])
        return out

    if hops:
        bits = jnp.stack([side(hop) for hop in ("zhi", "zlo", "y", "x", "core")]).astype(jnp.int32)
        local = split_up(lambda shard, units, rows: column_units(shard).reshape(2, -1, UNIT).astype(low))
        pieces = [piece for name in GATHER for piece in GATHER[name]]
        halves = jnp.concatenate([local[piece] for piece in pieces], 1)
        mine_half = pick(halves, core, 0)[0]
        other_half = swap(pick(halves, 1 - core, 0)[0], "core")
        whole, start = {}, 0
        for piece in pieces:
            units, rows = PIECES[piece][1][0]
            mine = mine_half[start : start + units * rows].reshape(units, 1, rows, UNIT)
            yours = other_half[start : start + units * rows].reshape(units, 1, rows, UNIT)
            whole[piece] = in_order(core, mine, yours, 1).reshape(-1, UNIT)
            start += units * rows
        whole["T"] = jnp.concatenate([whole["T"], pack_small(layer_vecs, final_norm, mask_count)])
        flying, done, pairs = {}, {}, {}
        for name in GATHER:
            chunk = jnp.concatenate([whole[piece] for piece in GATHER[name]])
            if name not in GATHER_WAY:
                chunk = lax.all_gather(chunk, BOTH, axis=0)
                pairs[name] = [chunk.reshape(16, 2, *chunk.shape[1:])] * 2
                continue
            chunk = chunk[None, None, None, None]
            flying[name], done[name] = (chunk, swap(chunk, GATHER_WAY[name][0])), 0

        def next_hop(name):
            way = GATHER_WAY[name]
            chunk = join(line, bits, HOPS[way[done[name]]][3], *flying[name])
            done[name] += 1
            if done[name] < len(way):
                flying[name] = chunk, swap(chunk, way[done[name]])
            else:
                pairs[name] = [part.reshape(16, -1, UNIT) for part in (chunk, swap(chunk, "core"))]
    else:

        def everywhere(shard):
            return lax.all_gather(shard.astype(low), BOTH, axis=0, tiled=True)

        blocks = split_up(lambda shard, units, rows: weight_blocks(everywhere(shard), units, 2 * rows))
        pairs = {}
        for name in GATHER:
            chunk = jnp.concatenate([blocks[piece] for piece in GATHER[name]], 2)
            pairs[name] = [chunk[0], chunk[1]]
        vectors = [everywhere(layer_vecs[l]).astype(full).reshape(12, D) for l in range(L)]
        final_float = everywhere(final_norm.T).T.astype(full)
        mask_total = lax.psum(jnp.sum(mask_count.astype(full)), BOTH)

    slots = jnp.arange(M, dtype=jnp.int32)
    valid = (slots[None, :] < mask_count[:, None]).astype(full)
    spots = mask_pos + seq_len * jnp.arange(images, dtype=jnp.int32)[:, None]
    codes_row, codes_column = codes.reshape(1, TOKENS), codes.reshape(TOKENS, 1)
    pos_row, pos_column = spots.reshape(1, SLOTS), spots.reshape(SLOTS, 1)
    valid_row, valid_column = valid.reshape(1, SLOTS), valid.reshape(SLOTS, 1)
    bias = jnp.pad(head_bias, (0, VPAD - V), constant_values=-1e30).reshape(1, VPAD)

    def sources(*names):
        return [pairs[places[name][0]] for name in names], tuple(places[name][1] for name in names)

    kept = [None] * L
    for step in FORWARD_ORDER:
        if step in GATHER_WAY:
            if hops:
                next_hop(step)
        elif step == "embed":
            (pair,), (at,) = sources("T")
            ids, stream = embed(line, own, codes_column, pos_row, valid_row, pair, at)
            if hops:
                small = [part[:, at + 144 : at + 146].reshape(16, 1, 2 * UNIT) for part in pair]
                small = in_order(core, small[0], small[1], 1).reshape(32, 2 * UNIT).astype(full)
                vectors = [small[:, 288 * l : 288 * l + 288].reshape(12, D) for l in range(L)]
                final_float = small[:, 576:624].reshape(32, 2, 24).transpose(1, 0, 2).reshape(2, D)
                mask_total = jnp.sum(small[:, 624 : 624 + images])
        elif step == "head":
            scale = valid_column * (1.0 / mask_total)
            (pair,), (at,) = sources("T")
            upstream, chosen, grad_logits, bias_grad, final_grad, loss = head(
                line, own, stream, final_float, codes_row, pos_column, pos_row, scale, valid_column, bias, pair, at
            )
        elif step[:-1] == "attention":
            l = int(step[-1])
            two, ats = sources(f"Q{l}", f"O{l}")
            triple, lse, mixed, middle = attention(line, own, stream, vectors[l], two, ats)
            kept[l] = stream, triple, lse, mixed, middle
        else:
            l = int(step[-1])
            three, ats = sources(f"D{l}", f"E{l}", f"F{l}")
            hidden, stream = feed_forward(line, own, kept[l][4], vectors[l], three, ats)
            kept[l] = kept[l] + (hidden,)

    grads = Grads()
    vector_grads = [0.0] * L
    parts, gone, totals = {}, {}, {}

    def small_blocks():
        small = [vector_grads[0].reshape(-1), vector_grads[1].reshape(-1), final_grad[0], final_grad[1]]
        if not hops:
            return small, jnp.zeros((16, 2, 16, UNIT), low)
        small.append(bias_grad[0, :2048])
        small = jnp.concatenate([grad.reshape(32, -1) for grad in small], 1)
        small = jnp.pad(small, ((0, 0), (0, 2 * UNIT - 688))).astype(low)
        small = small.reshape(16, 2, 2, UNIT)
        return small, jnp.pad(small, ((0, 0), (0, 0), (0, 14), (0, 0)))

    def ready(names):
        for name in names:
            grad = grads.arrays[name]
            if name in SCATTER_WAY:
                shape = (2, 2, 2, 2) + grad.shape[1:]
                arrived = swap(pick(grad, 1 - core, 1)[:, 0], "core")
                parts[name], gone[name] = [grad.reshape(shape), arrived.reshape(shape[:4] + shape[5:])], []
            else:
                grad = grad.reshape(32, -1, UNIT)
                total = lax.psum_scatter(grad, BOTH, scatter_dimension=0, tiled=False)
                parts[name], totals[name] = None, total.astype(full)

    complete = {name: [p for p in SCATTER[name]] for name in SCATTER}

    def finished(pieces):
        for piece in pieces:
            complete[grads.places[piece][0]].remove(piece)
        names = [name for name in SCATTER if name in grads.arrays and not complete[name] and name not in parts]
        if hops:
            ready(names)

    for step in BACKWARD_ORDER:
        if step in SCATTER_WAY:
            if not hops:
                continue
            way = SCATTER_WAY[step]
            if len(gone[step]) == len(way):
                totals[step] = merge(line, bits, parts[step], gone[step], None)[0, 0, 0, 0]
                continue
            hop = way[len(gone[step])]
            axis = HOPS[hop][3]
            parts[step].append(swap(merge(line, bits, parts[step], gone[step], axis), hop))
            gone[step].append(axis)
        elif step == "embed":
            small_grads, block = small_blocks()
            embed_back(line, grads, upstream, ids, chosen, grad_logits, block)
            finished(("T",))
        elif step[:-1] == "attention":
            l = int(step[-1])
            stream, triple, lse, mixed = kept[l][:4]
            two, ats = sources(f"Q{l}", f"O{l}")
            upstream, early = attention_back(
                line, grads, l, own, grad_middle, stream, vectors[l], triple, lse, mixed, two, ats
            )
            vector_grads[l] += early
            finished((f"Q{l}", f"O{l}"))
        else:
            l = int(step[-1])
            three, ats = sources(f"D{l}", f"E{l}", f"F{l}")
            grad_middle, late = feed_forward_back(
                line, grads, l, own, upstream, kept[l][4], vectors[l], kept[l][5], three, ats
            )
            vector_grads[l] += late
            finished((f"D{l}", f"E{l}", f"F{l}"))

    shares = {}
    if hops:
        for names in LAST:
            mine, leaving, where = [], [], []
            for name in names:
                start = 0
                for piece in SCATTER[name]:
                    units, rows = PIECES[piece][1][0]
                    block = totals[name][start : start + 2 * units * rows].reshape(units, 2, rows, UNIT)
                    mine.append(pick(block, core, 1).reshape(-1, UNIT))
                    leaving.append(pick(block, 1 - core, 1).reshape(-1, UNIT))
                    where.append((piece, units, rows))
                    start += PIECES[piece][0]
            mine, arrived = jnp.concatenate(mine), swap(jnp.concatenate(leaving), "core")
            both = in_order(core, mine[None], arrived[None], 0)
            start = 0
            for piece, units, rows in where:
                block = both[:, start : start + units * rows].reshape(2, units, rows, UNIT)
                shares[piece] = block
                start += units * rows
        for l in range(L):
            shares[f"U{l}"] = jnp.concatenate([shares[f"E{l}"], shares[f"F{l}"]], 1)
        for piece in list(shares):
            block = shares[piece]
            shares[piece] = block.transpose(2, 0, 1, 3).reshape(block.shape[2], -1)
        at = grads.places["T"][1] + 144
        small_sum = totals[grads.places["T"][0]][at : at + 2].reshape(-1)
    else:
        head_grad, loss_sum = lax.psum((bias_grad[0, :V], loss[0, 0]), BOTH)
        small_sum = [lax.psum_scatter(g, BOTH, scatter_dimension=0, tiled=True) for g in small_grads]
        small_sum = jnp.concatenate(small_sum)
        for piece, (name, start) in grads.places.items():
            size = 144 if piece == "T" else PIECES[piece][0]
            shares[piece] = grads.arrays[name][:, :, start : start + size].transpose(1, 0, 2, 3)
        for l in range(L):
            shares[f"U{l}"] = jnp.concatenate([shares[f"E{l}"], shares[f"F{l}"]], 2)
        for piece, block in shares.items():
            units, rows = (4, 24) if piece[0] == "U" else PIECES[piece][1][0]
            weight = natural_weight(block, units, 2 * rows).astype(full)
            shares[piece] = lax.psum_scatter(weight, BOTH, scatter_dimension=0, tiled=True)
    width, narrow = layer_vecs.shape[1], final_norm.shape[1]
    grads_own = [shares["T"][:, :V].T]
    grads_own += [jnp.stack([shares[f"{kind}{l}"] for l in range(L)]) for kind in "QOUD"]
    grads_own += [
        small_sum[: 2 * width].reshape(L, width),
        small_sum[2 * width : 2 * width + 2 * narrow].reshape(2, narrow),
    ]
    squares = reduce(jnp.add, [jnp.sum(share * share) for share in grads_own])
    if hops:
        bias_share = small_sum[624:688]
        squares = squares + jnp.sum(bias_share * bias_share)
        tail = jnp.concatenate([bias_share, squares[None], loss[0, :1], jnp.zeros(62)])
        tail = tail.reshape(1, 1, 1, 1, 1, 128)
        for hop in ("core", "x", "y", "zlo", "zhi"):
            axis = HOPS[hop][3]
            tail = in_order(side(hop), tail, swap(tail, hop), 4 if axis is None else axis)
        tail = tail.reshape(32, 128)
        head_grad = tail[:, :64].reshape(-1)[:V]
        squares, loss_sum = jnp.sum(tail[:, 64]), jnp.sum(tail[:, 65])
    else:
        squares = lax.psum(squares, BOTH) + jnp.sum(head_grad * head_grad)
    grad_norm = jnp.sqrt(squares)
    factor = jnp.minimum(1.0, clip_bound / (grad_norm + epsilon))
    results = [
        update(weight, moment, average, grad, factor)
        for weight, moment, average, grad in zip(arguments[3:11], moments, averages, grads_own + [head_grad])
    ]
    return (
        (loss_sum, mask_total, grad_norm)
        + tuple(result[0] for result in results)
        + tuple(result[1] for result in results)
        + tuple(result[2] for result in results)
    )


def solution(mesh):
    return jax.shard_map(
        partial(body, mesh.shape["dp"] == 8 and mesh.shape["fsdp"] == 4),
        mesh=mesh,
        in_specs=(
            P(("dp", "fsdp"), None),
            P(("dp", "fsdp"), None),
            P(("dp", "fsdp")),
            P(None, ("dp", "fsdp")),
            P(None, ("dp", "fsdp"), None),
            P(None, ("dp", "fsdp"), None),
            P(None, ("dp", "fsdp"), None),
            P(None, ("dp", "fsdp"), None),
            P(None, ("dp", "fsdp")),
            P(None, ("dp", "fsdp")),
            P(),
            P(None, ("dp", "fsdp")),
            P(None, ("dp", "fsdp"), None),
            P(None, ("dp", "fsdp"), None),
            P(None, ("dp", "fsdp"), None),
            P(None, ("dp", "fsdp"), None),
            P(None, ("dp", "fsdp")),
            P(None, ("dp", "fsdp")),
            P(),
            P(None, ("dp", "fsdp")),
            P(None, ("dp", "fsdp"), None),
            P(None, ("dp", "fsdp"), None),
            P(None, ("dp", "fsdp"), None),
            P(None, ("dp", "fsdp"), None),
            P(None, ("dp", "fsdp")),
            P(None, ("dp", "fsdp")),
            P(),
        ),
        out_specs=(
            P(),
            P(),
            P(),
            P(None, ("dp", "fsdp")),
            P(None, ("dp", "fsdp"), None),
            P(None, ("dp", "fsdp"), None),
            P(None, ("dp", "fsdp"), None),
            P(None, ("dp", "fsdp"), None),
            P(None, ("dp", "fsdp")),
            P(None, ("dp", "fsdp")),
            P(),
            P(None, ("dp", "fsdp")),
            P(None, ("dp", "fsdp"), None),
            P(None, ("dp", "fsdp"), None),
            P(None, ("dp", "fsdp"), None),
            P(None, ("dp", "fsdp"), None),
            P(None, ("dp", "fsdp")),
            P(None, ("dp", "fsdp")),
            P(),
            P(None, ("dp", "fsdp")),
            P(None, ("dp", "fsdp"), None),
            P(None, ("dp", "fsdp"), None),
            P(None, ("dp", "fsdp"), None),
            P(None, ("dp", "fsdp"), None),
            P(None, ("dp", "fsdp")),
            P(None, ("dp", "fsdp")),
            P(),
        ),
        check_vma=False,
    )
```

time: 773 us -> 635 us (0.82)
  waiting for transfers between devices: 393 us -> 178 us
  Pallas kernels: 178 us -> 279 us
  other arithmetic: 109 us -> 23.4 us
  local copies, waits for them, and re-layouts: 23 us -> 62 us
  between operations: 10.5 us -> 24.4 us
  starting transfers between devices: 51.6 us -> 59.5 us
    ppermute x55 -> x48, waiting for transfers between devices: 393 us -> 178 us  [swap(): return lax.ppermute(tensor, axis, [(i, i ^ flip) for i in range(size)])]
    pallas_call x11 -> x47, Pallas kernels: 178 us -> 279 us  [call(): pl.pallas_call(ordered, out_shape=outs, compiler_params=pltpu.CompilerPar...]
    convert_element_type x16 -> x0, other arithmetic: 41.7 us -> none  [scatter_chips(): arrived = swap(leaving.astype(jnp.bfloat16), hop)]
    select_n x34 -> x18, other arithmetic: 33.9 us -> 2.12 us  [in_order(): jnp.where(bit == 0, jnp.concatenate([own, other], axis), jnp.concatenate(...]
    unnamed x124 -> x203, local copies, waits for them, and re-layouts: 4.25 us -> 31.9 us
    squeeze x0 -> x5, local copies, waits for them, and re-layouts: none -> 9.11 us  [the longest x4 9.05 us: ready(): arrived = swap(pick(grad, 1 - core, 1)[:, 0], 'core')]
    ppermute x55 -> x48, starting transfers between devices: 51.6 us -> 59.4 us  [swap(): return lax.ppermute(tensor, axis, [(i, i ^ flip) for i in range(size)])]
  transfers between devices with their start and end apart: 55 -> 50, of which waited for: 36 -> 27; matrix products, arithmetic and copies ran while one was open for 14% -> 5% of each run, Pallas kernels for 6% -> 31%
where the time goes in v2:
time: 635 us; the launch traced here: 626 us
  Pallas kernels  279 us (44%)
  waiting for transfers between devices  178 us (28%)
  local copies, waits for them, and re-layouts  62 us (10%)
  starting transfers between devices  59.5 us (9%)
  between operations  24.4 us (4%)
  other arithmetic  23.4 us (4%)
    pallas_call x47, Pallas kernels, call(): pl.pallas_call(ordered, out_shape=outs, compiler_params=pltpu.CompilerPar...  279 us
    ppermute x48, waiting for transfers between devices, swap(): return lax.ppermute(tensor, axis, [(i, i ^ flip) for i in range(size)])  178 us
    ppermute x48, starting transfers between devices, swap(): return lax.ppermute(tensor, axis, [(i, i ^ flip) for i in range(size)])  59.4 us
    unnamed x203, local copies, waits for them, and re-layouts  31.9 us
  transfers between devices with their start and end apart: 50, of which 27 were waited for; matrix products, arithmetic and copies ran while one was open for 5% of the time, Pallas kernels for 31%

profile of v2, /device:TPU:0, one launch (start us, length us, event | category | flops | bytes accessed | tf_op | source)
XLA Modules:
  0.0 625.9 jit_solution(3463608247556774851)
XLA Ops:
  14.8 3.0 collective-permute-start.4
  20.3 9.3 %collective-permute-done.1.refs_3_ = bf16[1,1,1,1,160,384]{5,4,3,2,1,0:T(8,128)(2,1)S(1)} collective-permute-done((bf16[1,1,1,1,160,384]{5,4,3,2,1,0:T(8,128)(2,1)S(1)}, bf16[1,1,1,1,160,384]{5,4,3,2,1,0:T(8,128)(2,1)S(1)}, u32[]{:S(2)}, u32[]{:S(2)}) %collective-permute-start.1) | collective-permute-done | bytes 122912 | tf_op jit(solution)/shard_map/ppermute | solution.py:102
  32.6 3.9 collective-permute-start.5
  40.7 3.3 collective-permute-start.6
  50.1 8.5 %collective-permute-done.5.refs_3_ = bf16[1,2,1,1,160,384]{5,4,3,2,1,0:T(8,128)(2,1)S(1)} collective-permute-done((bf16[1,2,1,1,160,384]{5,4,3,2,1,0:T(8,128)(2,1)}, bf16[1,2,1,1,160,384]{5,4,3,2,1,0:T(8,128)(2,1)S(1)}, u32[]{:S(2)}, u32[]{:S(2)}) %collective-permute-start.5) | collective-permute-done | bytes 245792 | tf_op jit(solution)/shard_map/ppermute | solution.py:102
  63.5 3.0 collective-permute-done.6.refs_3_
  71.4 7.6 %collective-permute-done.7.refs_3_ = bf16[2,2,1,1,160,384]{5,4,3,2,1,0:T(8,128)(2,1)S(1)} collective-permute-done((bf16[2,2,1,1,160,384]{5,4,3,2,1,0:T(8,128)(2,1)}, bf16[2,2,1,1,160,384]{5,4,3,2,1,0:T(8,128)(2,1)S(1)}, u32[]{:S(2)}, u32[]{:S(2)}) %collective-permute-start.7) | collective-permute-done | bytes 491552 | tf_op jit(solution)/shard_map/ppermute | solution.py:102
  84.1 2.9 collective-permute-start.10
  94.2 14.3 %collective-permute-done.9.refs_3_ = bf16[1,2,1,1,192,384]{5,4,3,2,1,0:T(8,128)(2,1)S(1)} collective-permute-done((bf16[1,2,1,1,192,384]{5,4,3,2,1,0:T(8,128)(2,1)S(1)}, bf16[1,2,1,1,192,384]{5,4,3,2,1,0:T(8,128)(2,1)S(1)}, u32[]{:S(2)}, u32[]{:S(2)}) %collective-permute-start.9) | collective-permute-done | bytes 294944 | tf_op jit(solution)/shard_map/ppermute | solution.py:102
  111.7 12.6 %collective-permute-done.10.refs_3_ = bf16[1,2,1,1,192,384]{5,4,3,2,1,0:T(8,128)(2,1)S(1)} collective-permute-done((bf16[1,2,1,1,192,384]{5,4,3,2,1,0:T(8,128)(2,1)S(1)}, bf16[1,2,1,1,192,384]{5,4,3,2,1,0:T(8,128)(2,1)S(1)}, u32[]{:S(2)}, u32[]{:S(2)}) %collective-permute-start.10) | collective-permute-done | bytes 294944 | tf_op jit(solution)/shard_map/ppermute | solution.py:102
  128.5 3.1 shard_map.476.refs_0_
  132.8 3.2 shard_map.477.refs_0_
  142.1 6.2 shard_map.478
  150.3 5.4 collective-permute-done.14.refs_3_
  163.3 14.8 %shard_map.481 = (bf16[3,512,768]{2,1,0:T(8,128)(2,1)}, f32[512,128]{1,0:T(8,128)}, bf16[512,768]{1,0:T(8,128)(2,1)}, f32[512,768]{1,0:T(8,128)}) custom-call(bf16[2,2,1,2,192,384]{5,4,3,2,1,0:T(8,128)(2,1)} %shard_map.480.refs_0_.refs_2_, s32[1]{0:T(128)} %bitcast.4.refs_0_.refs_1_, f32[512,768]{1,0:T(8,128)} %get-tuple-element.61.refs_2_.refs_3_, ...), custom_call_target="tpu_custom_call" | custom-call | flops 17250000896 | bytes 1000 | tf_op jit(solution)/shard_map/pallas_call | solution.py:602
  178.2 8.3 %collective-permute-done.17.refs_3_ = bf16[2,2,2,1,192,384]{5,4,3,2,1,0:T(8,128)(2,1)S(1)} collective-permute-done((bf16[2,2,2,1,192,384]{5,4,3,2,1,0:T(8,128)(2,1)}, bf16[2,2,2,1,192,384]{5,4,3,2,1,0:T(8,128)(2,1)S(1)}, u32[]{:S(2)}, u32[]{:S(2)}) %collective-permute-start.17) | collective-permute-done | bytes 1179680 | tf_op jit(solution)/shard_map/ppermute | solution.py:102
  187.5 3.2 shard_map.482.refs_0_
  191.8 3.4 shard_map.483.refs_0_
  203.3 12.0 %shard_map.484 = (f32[4,512,768]{2,1,0:T(8,128)}, f32[512,768]{1,0:T(8,128)}) custom-call(bf16[2,2,2,2,192,384]{5,4,3,2,1,0:T(8,128)(2,1)} %shard_map.483.refs_0_, s32[1]{0:T(128)} %bitcast.4.refs_0_.refs_1_, f32[512,768]{1,0:T(8,128)} %get-tuple-element.63.refs_2_.refs_3_, f32[12,768]{1,0:T(8,128)} %reshape.1367.refs_3_.refs_4_, ...), custom_call_target="tpu_custom_call" | custom-call | flops 13800000512 | bytes 1000 | tf_op jit(solution)/shard_map/pallas_call | solution.py:602
  215.3 14.9 %shard_map.485 = (bf16[3,512,768]{2,1,0:T(8,128)(2,1)}, f32[512,128]{1,0:T(8,128)}, bf16[512,768]{1,0:T(8,128)(2,1)}, f32[512,768]{1,0:T(8,128)}) custom-call(f32[4,512,768]{2,1,0:T(8,128)} %get-tuple-element.64.refs_0_.refs_5_, s32[1]{0:T(128)} %bitcast.4.refs_0_.refs_1_, f32[512,768]{1,0:T(8,128)} %get-tuple-element.65.refs_2_.refs_3_, ...), custom_call_target="tpu_custom_call" | custom-call | flops 17250000896 | bytes 1000 | tf_op jit(solution)/shard_map/pallas_call | solution.py:602
  230.2 12.0 %shard_map.486 = (f32[4,512,768]{2,1,0:T(8,128)}, f32[512,768]{1,0:T(8,128)}) custom-call(bf16[3,512,768]{2,1,0:T(8,128)(2,1)} %get-tuple-element.66.refs_0_.refs_5_, s32[1]{0:T(128)} %bitcast.4.refs_0_.refs_1_, f32[512,768]{1,0:T(8,128)} %get-tuple-element.67.refs_2_.refs_3_, f32[12,768]{1,0:T(8,128)} %reshape.1374.refs_3_.refs_4_, ...), custom_call_target="tpu_custom_call" | custom-call | flops 13800000512 | bytes 1000 | tf_op jit(solution)/shard_map/pallas_call | solution.py:602
  242.2 9.8 %shard_map.487 = (f32[512,768]{1,0:T(8,128)}, bf16[256,768]{1,0:T(8,128)(2,1)}, bf16[256,2304]{1,0:T(8,128)(2,1)}, f32[1,2304]{1,0:T(1,128)}, f32[2,768]{1,0:T(2,128)}, /*index=5*/f32[1,128]{1,0:T(1,128)}) custom-call(f32[4,512,768]{2,1,0:T(8,128)} %get-tuple-element.68.refs_0_.refs_5_, s32[1]{0:T(128)} %bitcast.4.refs_0_.refs_1_, ...), custom_call_target="tpu_custom_call" | custom-call | flops 11500001280 | bytes 1000 | tf_op jit(solution)/shard_map/pallas_call | solution.py:602
  252.0 22.4 %shard_map.488 = (f32[512,768]{1,0:T(8,128)}, f32[12,768]{1,0:T(8,128)}, bf16[16,2,576,384]{3,2,1,0:T(8,128)(2,1)}) custom-call(f32[512,768]{1,0:T(8,128)} %get-tuple-element.70.refs_0_.refs_2_, s32[1]{0:T(128)} %bitcast.4.refs_0_.refs_1_, f32[512,768]{1,0:T(8,128)} %get-tuple-element.70.refs_0_.refs_2_, f32[512,768]{1,0:T(8,128)} %get-tuple-element.67.refs_2_.refs_3_, ...), custom_call_target="tpu_custom_call" | custom-call | flops 25300000768 | bytes 1000 | tf_op jit(solution)/shard_map/pallas_call | solution.py:602
  274.4 24.4 %shard_map.489 = (f32[512,768]{1,0:T(8,128)}, f32[12,768]{1,0:T(8,128)}, bf16[16,2,576,384]{3,2,1,0:T(8,128)(2,1)}) custom-call(f32[512,768]{1,0:T(8,128)} %get-tuple-element.71.refs_0_.refs_2_, s32[1]{0:T(128)} %bitcast.4.refs_0_.refs_1_, f32[512,768]{1,0:T(8,128)} %get-tuple-element.71.refs_0_.refs_2_, ...), custom_call_target="tpu_custom_call", output_to_operand_aliasing={{2}: (12, {})} | custom-call | flops 27600001024 | bytes 1000 | tf_op jit(solution)/shard_map/pallas_call | solution.py:602
  298.8 22.2 %shard_map.490 = (f32[512,768]{1,0:T(8,128)}, f32[12,768]{1,0:T(8,128)}, bf16[16,2,192,384]{3,2,1,0:T(8,128)(2,1)}, bf16[16,2,192,384]{3,2,1,0:T(8,128)(2,1)}) custom-call(f32[512,768]{1,0:T(8,128)} %get-tuple-element.75.refs_0_.refs_2_, s32[1]{0:T(128)} %bitcast.4.refs_0_.refs_1_, f32[512,768]{1,0:T(8,128)} %get-tuple-element.75.refs_0_.refs_2_, ...), custom_call_target="tpu_custom_call" | custom-call | flops 25300000768 | bytes 1000 | tf_op jit(solution)/shard_map/pallas_call | solution.py:602
  321.0 3.6 dynamic-slice_bitcast_fusion.2
  325.9 25.0 %shard_map.491 = (f32[512,768]{1,0:T(8,128)}, f32[12,768]{1,0:T(8,128)}, bf16[16,2,192,384]{3,2,1,0:T(8,128)(2,1)}) custom-call(f32[512,768]{1,0:T(8,128)} %get-tuple-element.76.refs_0_.refs_2_, s32[1]{0:T(128)} %bitcast.4.refs_0_.refs_1_, f32[512,768]{1,0:T(8,128)} %get-tuple-element.76.refs_0_.refs_2_, f32[512,768]{1,0:T(8,128)} %get-tuple-element.61.refs_2_.refs_3_, ...), custom_call_target="tpu_custom_call" | custom-call | flops 27600001024 | bytes 1000 | tf_op jit(solution)/shard_map/pallas_call | solution.py:602
  350.9 3.4 dynamic-slice_bitcast_fusion
  356.1 3.3 shard_map.492.refs_1_
  359.4 3.3 shard_map.493.refs_1_
  362.7 3.3 shard_map.494.refs_0_
  366.0 15.1 %shard_map.495.refs_1_ = bf16[16,2,160,384]{3,2,1,0:T(8,128)(2,1)} custom-call(bf16[2,2,1,2,192,384]{5,4,3,2,1,0:T(8,128)(2,1)} %shard_map.494.refs_0_, f32[512,768]{1,0:T(8,128)} %get-tuple-element.79.refs_1_, s32[512,1]{1,0:T(8,128)} %get-tuple-element.60.refs_0_.refs_2_, bf16[256,768]{1,0:T(8,128)(2,1)} %get-tuple-element.83.refs_3_, ...), custom_call_target="tpu_custom_call" | custom-call | flops 17250000896 | bytes 1000 | tf_op jit(solution)/shard_map/pallas_call | solution.py:602
  388.1 3.1 shard_map.496.refs_1_
  393.5 31.5 %collective-permute-done.25.refs_4_ = bf16[2,2,1,2,192,384]{5,4,3,2,1,0:T(8,128)(2,1)} collective-permute-done((bf16[2,2,1,2,192,384]{5,4,3,2,1,0:T(8,128)(2,1)}, bf16[2,2,1,2,192,384]{5,4,3,2,1,0:T(8,128)(2,1)}, u32[]{:S(2)}, u32[]{:S(2)}) %collective-permute-start.25) | collective-permute-done | bytes 1179680 | tf_op jit(solution)/shard_map/ppermute | solution.py:102
  425.0 2.9 shard_map.497.refs_1_
  430.7 3.0 shard_map.498.refs_1_
  435.2 17.4 %collective-permute-done.27.refs_4_ = bf16[2,2,2,1,160,384]{5,4,3,2,1,0:T(8,128)(2,1)S(1)} collective-permute-done((bf16[2,2,2,1,160,384]{5,4,3,2,1,0:T(8,128)(2,1)}, bf16[2,2,2,1,160,384]{5,4,3,2,1,0:T(8,128)(2,1)S(1)}, u32[]{:S(2)}, u32[]{:S(2)}) %collective-permute-start.27) | collective-permute-done | bytes 983072 | tf_op jit(solution)/shard_map/ppermute | solution.py:102
  453.6 3.0 shard_map.499.refs_1_
  456.6 2.9 collective-permute-start.33
  459.5 3.3 collective-permute-done.28.refs_4_
  463.9 3.2 shard_map.500.refs_1_
  467.7 18.5 %collective-permute-done.29.refs_5_ = bf16[1,2,1,2,192,384]{5,4,3,2,1,0:T(8,128)(2,1)S(1)} collective-permute-done((bf16[1,2,1,2,192,384]{5,4,3,2,1,0:T(8,128)(2,1)}, bf16[1,2,1,2,192,384]{5,4,3,2,1,0:T(8,128)(2,1)S(1)}, u32[]{:S(2)}, u32[]{:S(2)}) %collective-permute-start.29) | collective-permute-done | bytes 589856 | tf_op jit(solution)/shard_map/ppermute | solution.py:102
  487.1 2.8 shard_map.501.refs_1_
  490.7 2.8 shard_map.502.refs_1_
  493.5 3.3 collective-permute-start.35
  496.8 17.7 %collective-permute-done.31.refs_6_ = bf16[1,1,1,2,192,384]{5,4,3,2,1,0:T(8,128)(2,1)S(1)} collective-permute-done((bf16[1,1,1,2,192,384]{5,4,3,2,1,0:T(8,128)(2,1)}, bf16[1,1,1,2,192,384]{5,4,3,2,1,0:T(8,128)(2,1)S(1)}, u32[]{:S(2)}, u32[]{:S(2)}) %collective-permute-start.31) | collective-permute-done | bytes 294944 | tf_op jit(solution)/shard_map/ppermute | solution.py:102
  519.5 2.8 shard_map.504.refs_1_
  525.8 6.3 %collective-permute-start.36 = (bf16[1,1,2,1,160,384]{5,4,3,2,1,0:T(8,128)(2,1)}, bf16[1,1,2,1,160,384]{5,4,3,2,1,0:T(8,128)(2,1)S(1)}, u32[]{:S(2)}, u32[]{:S(2)}) collective-permute-start(bf16[1,1,2,1,160,384]{5,4,3,2,1,0:T(8,128)(2,1)} %shard_map.505.refs_1_), channel_id=1, source_target_pairs={{0,8},{4,12},{8,0},{12,4},{16,24},{20,28},{24,16},{28,20},{1,9},{5... | collective-permute-start | bytes 737288 | tf_op jit(solution)/shard_map/ppermute | solution.py:102
  (490 shorter events, 186.6 us)
Async XLA Ops:
  7.2 208.0 %all-gather.3.cloned.1.call-start = ((), (), s32[]{:S(2)}) async-start(), calls=%async_computation.2 | async-start | bytes 14598144 | tf_op jit(solution)/shard_map/all_gather | solution.py:903
  10.6 2.0 collective-permute-start
  13.8 553.1 %reduce-scatter.2.cloned.1.call-start = ((), (), s32[]{:S(2)}) async-start(), calls=%async_computation.1 | async-start | bytes 14598144 | tf_op jit(solution)/shard_map/reduce_scatter | solution.py:996
  14.8 32.2 %collective-permute-start.4 = (bf16[1,1,1,1,192,384]{5,4,3,2,1,0:T(8,128)(2,1)S(1)}, bf16[1,1,1,1,192,384]{5,4,3,2,1,0:T(8,128)(2,1)S(1)}, u32[]{:S(2)}, u32[]{:S(2)}) collective-permute-start(bf16[1,1,1,1,192,384]{5,4,3,2,1,0:T(8,128)(2,1)S(1)} %maximum_bitcast_fusion.4.refs_2_), channel_id=1, source_target_pairs={{0,8},{4,12},{8,0},{12,4},{16,24},{20,28},{24,16},{28,20},{1,9},{5... | collective-permute-start | bytes 442376 | tf_op jit(solution)/shard_map/ppermute | solution.py:102
  17.9 26.2 %collective-permute-start.3 = (bf16[1,1,1,1,192,384]{5,4,3,2,1,0:T(8,128)(2,1)S(1)}, bf16[1,1,1,1,192,384]{5,4,3,2,1,0:T(8,128)(2,1)S(1)}, u32[]{:S(2)}, u32[]{:S(2)}) collective-permute-start(bf16[1,1,1,1,192,384]{5,4,3,2,1,0:T(8,128)(2,1)S(1)} %bitcast.381), channel_id=1, source_target_pairs={{0,8},{4,12},{8,0},{12,4},{16,24},{20,28},{24,16},{28,20},{1,9},{5... | collective-permute-start | bytes 442376 | tf_op jit(solution)/shard_map/ppermute | solution.py:102
  18.0 11.6 %collective-permute-start.1 = (bf16[1,1,1,1,160,384]{5,4,3,2,1,0:T(8,128)(2,1)S(1)}, bf16[1,1,1,1,160,384]{5,4,3,2,1,0:T(8,128)(2,1)S(1)}, u32[]{:S(2)}, u32[]{:S(2)}) collective-permute-start(bf16[1,1,1,1,160,384]{5,4,3,2,1,0:T(8,128)(2,1)S(1)} %fusion.4.refs_2_), channel_id=1, source_target_pairs={{0,8},{4,12},{8,0},{12,4},{16,24},{20,28},{24,16},{28,20},{1,9},{5... | collective-permute-start | bytes 368648 | tf_op jit(solution)/shard_map/ppermute | solution.py:102
  20.2 17.5 %collective-permute-start.2 = (bf16[1,1,1,1,192,384]{5,4,3,2,1,0:T(8,128)(2,1)S(1)}, bf16[1,1,1,1,192,384]{5,4,3,2,1,0:T(8,128)(2,1)S(1)}, u32[]{:S(2)}, u32[]{:S(2)}) collective-permute-start(bf16[1,1,1,1,192,384]{5,4,3,2,1,0:T(8,128)(2,1)S(1)} %maximum_bitcast_fusion.3.refs_2_), channel_id=1, source_target_pairs={{0,8},{4,12},{8,0},{12,4},{16,24},{20,28},{24,16},{28,20},{1,9},{5... | collective-permute-start | bytes 442376 | tf_op jit(solution)/shard_map/ppermute | solution.py:102
  32.6 26.0 %collective-permute-start.5 = (bf16[1,2,1,1,160,384]{5,4,3,2,1,0:T(8,128)(2,1)}, bf16[1,2,1,1,160,384]{5,4,3,2,1,0:T(8,128)(2,1)S(1)}, u32[]{:S(2)}, u32[]{:S(2)}) collective-permute-start(bf16[1,2,1,1,160,384]{5,4,3,2,1,0:T(8,128)(2,1)} %shard_map.466.refs_0_.refs_2_), channel_id=1, source_target_pairs={{0,16},{4,20},{8,24},{12,28},{16,0},{20,4},{24,8},{28,12},{1,17},{... | collective-permute-start | bytes 737288 | tf_op jit(solution)/shard_map/ppermute | solution.py:102
  40.7 25.8 %collective-permute-start.6 = (bf16[1,2,1,1,192,384]{5,4,3,2,1,0:T(8,128)(2,1)}, bf16[1,2,1,1,192,384]{5,4,3,2,1,0:T(8,128)(2,1)S(1)}, u32[]{:S(2)}, u32[]{:S(2)}) collective-permute-start(bf16[1,2,1,1,192,384]{5,4,3,2,1,0:T(8,128)(2,1)} %shard_map.467.refs_0_.refs_2_), channel_id=1, source_target_pairs={{0,16},{4,20},{8,24},{12,28},{16,0},{20,4},{24,8},{28,12},{1,17},{... | collective-permute-start | bytes 884744 | tf_op jit(solution)/shard_map/ppermute | solution.py:102
  61.8 17.2 %collective-permute-start.7 = (bf16[2,2,1,1,160,384]{5,4,3,2,1,0:T(8,128)(2,1)}, bf16[2,2,1,1,160,384]{5,4,3,2,1,0:T(8,128)(2,1)S(1)}, u32[]{:S(2)}, u32[]{:S(2)}) collective-permute-start(bf16[2,2,1,1,160,384]{5,4,3,2,1,0:T(8,128)(2,1)} %shard_map.470.refs_0_.refs_2_), channel_id=1, source_target_pairs={{0,4},{4,0},{8,12},{12,8},{16,20},{20,16},{24,28},{28,24},{1,5},{5... | collective-permute-start | bytes 1474568 | tf_op jit(solution)/shard_map/ppermute | solution.py:102
  69.8 19.2 %collective-permute-start.8 = (bf16[2,2,1,1,192,384]{5,4,3,2,1,0:T(8,128)(2,1)}, bf16[2,2,1,1,192,384]{5,4,3,2,1,0:T(8,128)(2,1)S(1)}, u32[]{:S(2)}, u32[]{:S(2)}) collective-permute-start(bf16[2,2,1,1,192,384]{5,4,3,2,1,0:T(8,128)(2,1)} %shard_map.471.refs_0_.refs_2_), channel_id=1, source_target_pairs={{0,2},{1,3},{2,0},{3,1},{4,6},{5,7},{6,4},{7,5},{8,10},{9,11},{10,... | collective-permute-start | bytes 1769480 | tf_op jit(solution)/shard_map/ppermute | solution.py:102
  82.6 45.0 %collective-permute-start.11 = (bf16[2,2,2,1,160,384]{5,4,3,2,1,0:T(8,128)(2,1)}, bf16[2,2,2,1,160,384]{5,4,3,2,1,0:T(8,128)(2,1)S(1)}, u32[]{:S(2)}, u32[]{:S(2)}) collective-permute-start(bf16[2,2,2,1,160,384]{5,4,3,2,1,0:T(8,128)(2,1)} %shard_map.472.refs_0_.refs_2_), channel_id=1, source_target_pairs={{0,2},{1,3},{2,0},{3,1},{4,6},{5,7},{6,4},{7,5},{8,10},{9,11},{10,... | collective-permute-start | bytes 2949128 | tf_op jit(solution)/shard_map/ppermute | solution.py:102
  84.1 24.4 %collective-permute-start.9 = (bf16[1,2,1,1,192,384]{5,4,3,2,1,0:T(8,128)(2,1)S(1)}, bf16[1,2,1,1,192,384]{5,4,3,2,1,0:T(8,128)(2,1)S(1)}, u32[]{:S(2)}, u32[]{:S(2)}) collective-permute-start(bf16[1,2,1,1,192,384]{5,4,3,2,1,0:T(8,128)(2,1)S(1)} %copy-done.72), channel_id=1, source_target_pairs={{0,16},{4,20},{8,24},{12,28},{16,0},{20,4},{24,8},{28,12},{1,17},{... | collective-permute-start | bytes 884744 | tf_op jit(solution)/shard_map/ppermute | solution.py:102
  84.1 40.2 %collective-permute-start.10 = (bf16[1,2,1,1,192,384]{5,4,3,2,1,0:T(8,128)(2,1)S(1)}, bf16[1,2,1,1,192,384]{5,4,3,2,1,0:T(8,128)(2,1)S(1)}, u32[]{:S(2)}, u32[]{:S(2)}) collective-permute-start(bf16[1,2,1,1,192,384]{5,4,3,2,1,0:T(8,128)(2,1)S(1)} %copy-done.73), channel_id=1, source_target_pairs={{0,16},{4,20},{8,24},{12,28},{16,0},{20,4},{24,8},{28,12},{1,17},{... | collective-permute-start | bytes 884744 | tf_op jit(solution)/shard_map/ppermute | solution.py:102
  92.6 39.1 %collective-permute-start.12 = (bf16[2,2,1,2,192,384]{5,4,3,2,1,0:T(8,128)(2,1)}, bf16[2,2,1,2,192,384]{5,4,3,2,1,0:T(8,128)(2,1)S(1)}, u32[]{:S(2)}, u32[]{:S(2)}) collective-permute-start(bf16[2,2,1,2,192,384]{5,4,3,2,1,0:T(8,128)(2,1)} %shard_map.473.refs_0_.refs_2_), channel_id=1, source_target_pairs={{0,4},{4,0},{8,12},{12,8},{16,20},{20,16},{24,28},{28,24},{1,5},{5... | collective-permute-start | bytes 3538952 | tf_op jit(solution)/shard_map/ppermute | solution.py:102
  131.6 9.2 %collective-permute-start.13 = (bf16[2,2,2,2,160,384]{5,4,3,2,1,0:T(8,128)(2,1)}, bf16[2,2,2,2,160,384]{5,4,3,2,1,0:T(8,128)(2,1)S(1)}, u32[]{:S(2)}, u32[]{:S(2)}) collective-permute-start(bf16[2,2,2,2,160,384]{5,4,3,2,1,0:T(8,128)(2,1)} %shard_map.476.refs_0_), channel_id=1, source_target_pairs={{0,1},{1,0},{2,3},{3,2},{4,5},{5,4},{6,7},{7,6},{8,9},{9,8},{10,11... | collective-permute-start | bytes 5898248 | tf_op jit(solution)/shard_map/ppermute | solution.py:102
  135.9 27.4 %collective-permute-start.16 = (bf16[2,2,2,2,192,384]{5,4,3,2,1,0:T(8,128)(2,1)}, bf16[2,2,2,2,192,384]{5,4,3,2,1,0:T(8,128)(2,1)}, u32[]{:S(2)}, u32[]{:S(2)}) collective-permute-start(bf16[2,2,2,2,192,384]{5,4,3,2,1,0:T(8,128)(2,1)} %shard_map.477.refs_0_), channel_id=1, source_target_pairs={{0,1},{1,0},{2,3},{3,2},{4,5},{5,4},{6,7},{7,6},{8,9},{9,8},{10,11... | collective-permute-start | bytes 7077896 | tf_op jit(solution)/shard_map/ppermute | solution.py:102
  138.6 17.1 %collective-permute-start.14 = (bf16[2,2,1,1,192,384]{5,4,3,2,1,0:T(8,128)(2,1)S(1)}, bf16[2,2,1,1,192,384]{5,4,3,2,1,0:T(8,128)(2,1)}, u32[]{:S(2)}, u32[]{:S(2)}) collective-permute-start(bf16[2,2,1,1,192,384]{5,4,3,2,1,0:T(8,128)(2,1)S(1)} %copy-done.66), channel_id=1, source_target_pairs={{0,4},{4,0},{8,12},{12,8},{16,20},{20,16},{24,28},{28,24},{1,5},{5... | collective-permute-start | bytes 1769480 | tf_op jit(solution)/shard_map/ppermute | solution.py:102
  139.9 19.1 %collective-permute-start.15 = (bf16[2,2,1,1,192,384]{5,4,3,2,1,0:T(8,128)(2,1)S(1)}, bf16[2,2,1,1,192,384]{5,4,3,2,1,0:T(8,128)(2,1)}, u32[]{:S(2)}, u32[]{:S(2)}) collective-permute-start(bf16[2,2,1,1,192,384]{5,4,3,2,1,0:T(8,128)(2,1)S(1)} %copy-done.65), channel_id=1, source_target_pairs={{0,2},{1,3},{2,0},{3,1},{4,6},{5,7},{6,4},{7,5},{8,10},{9,11},{10,... | collective-permute-start | bytes 1769480 | tf_op jit(solution)/shard_map/ppermute | solution.py:102
  158.5 28.0 %collective-permute-start.17 = (bf16[2,2,2,1,192,384]{5,4,3,2,1,0:T(8,128)(2,1)}, bf16[2,2,2,1,192,384]{5,4,3,2,1,0:T(8,128)(2,1)S(1)}, u32[]{:S(2)}, u32[]{:S(2)}) collective-permute-start(bf16[2,2,2,1,192,384]{5,4,3,2,1,0:T(8,128)(2,1)} %shard_map.479.refs_0_.refs_2_), channel_id=1, source_target_pairs={{0,2},{1,3},{2,0},{3,1},{4,6},{5,7},{6,4},{7,5},{8,10},{9,11},{10,... | collective-permute-start | bytes 3538952 | tf_op jit(solution)/shard_map/ppermute | solution.py:102
  161.7 29.0 %collective-permute-start.18 = (bf16[2,2,1,2,192,384]{5,4,3,2,1,0:T(8,128)(2,1)}, bf16[2,2,1,2,192,384]{5,4,3,2,1,0:T(8,128)(2,1)S(1)}, u32[]{:S(2)}, u32[]{:S(2)}) collective-permute-start(bf16[2,2,1,2,192,384]{5,4,3,2,1,0:T(8,128)(2,1)} %shard_map.480.refs_0_.refs_2_), channel_id=1, source_target_pairs={{0,4},{4,0},{8,12},{12,8},{16,20},{20,16},{24,28},{28,24},{1,5},{5... | collective-permute-start | bytes 3538952 | tf_op jit(solution)/shard_map/ppermute | solution.py:102
  195.2 7.4 %collective-permute-start.20 = (bf16[2,2,2,2,192,384]{5,4,3,2,1,0:T(8,128)(2,1)}, bf16[2,2,2,2,192,384]{5,4,3,2,1,0:T(8,128)(2,1)}, u32[]{:S(2)}, u32[]{:S(2)}) collective-permute-start(bf16[2,2,2,2,192,384]{5,4,3,2,1,0:T(8,128)(2,1)} %shard_map.483.refs_0_), channel_id=1, source_target_pairs={{0,1},{1,0},{2,3},{3,2},{4,5},{5,4},{6,7},{7,6},{8,9},{9,8},{10,11... | collective-permute-start | bytes 7077896 | tf_op jit(solution)/shard_map/ppermute | solution.py:102
  195.3 8.0 %collective-permute-start.19 = (bf16[2,2,2,2,192,384]{5,4,3,2,1,0:T(8,128)(2,1)S(1)}, bf16[2,2,2,2,192,384]{5,4,3,2,1,0:T(8,128)(2,1)}, u32[]{:S(2)}, u32[]{:S(2)}) collective-permute-start(bf16[2,2,2,2,192,384]{5,4,3,2,1,0:T(8,128)(2,1)S(1)} %copy-done.54), channel_id=1, source_target_pairs={{0,1},{1,0},{2,3},{3,2},{4,5},{5,4},{6,7},{7,6},{8,9},{9,8},{10,11... | collective-permute-start | bytes 7077896 | tf_op jit(solution)/shard_map/ppermute | solution.py:102
  324.6 31.5 %collective-permute-start.21 = (bf16[16,192,384]{2,1,0:T(8,128)(2,1)}, bf16[16,192,384]{2,1,0:T(8,128)(2,1)}, u32[]{:S(2)}, u32[]{:S(2)}) collective-permute-start(bf16[16,192,384]{2,1,0:T(8,128)(2,1)} %dynamic-slice_bitcast_fusion.2), channel_id=1, source_target_pairs={{0,1},{1,0},{2,3},{3,2},{4,5},{5,4},{6,7},{7,6},{8,9},{9,8},{10,11... | collective-permute-start | bytes 7077896 | tf_op jit(solution)/shard_map/ppermute | solution.py:102
  325.7 33.7 %collective-permute-start.22 = (bf16[16,192,384]{2,1,0:T(8,128)(2,1)S(1)}, bf16[16,192,384]{2,1,0:T(8,128)(2,1)}, u32[]{:S(2)}, u32[]{:S(2)}) collective-permute-start(bf16[16,192,384]{2,1,0:T(8,128)(2,1)S(1)} %dynamic-slice_bitcast_fusion.1), channel_id=1, source_target_pairs={{0,1},{1,0},{2,3},{3,2},{4,5},{5,4},{6,7},{7,6},{8,9},{9,8},{10,11... | collective-permute-start | bytes 7077896 | tf_op jit(solution)/shard_map/ppermute | solution.py:102
  354.3 8.4 %collective-permute-start.23 = (bf16[16,192,384]{2,1,0:T(8,128)(2,1)}, bf16[16,192,384]{2,1,0:T(8,128)(2,1)}, u32[]{:S(2)}, u32[]{:S(2)}) collective-permute-start(bf16[16,192,384]{2,1,0:T(8,128)(2,1)} %dynamic-slice_bitcast_fusion), channel_id=1, source_target_pairs={{0,1},{1,0},{2,3},{3,2},{4,5},{5,4},{6,7},{7,6},{8,9},{9,8},{10,11... | collective-permute-start | bytes 7077896 | tf_op jit(solution)/shard_map/ppermute | solution.py:102
  382.8 4.0 collective-permute-start.24
  383.3 41.8 %collective-permute-start.25 = (bf16[2,2,1,2,192,384]{5,4,3,2,1,0:T(8,128)(2,1)}, bf16[2,2,1,2,192,384]{5,4,3,2,1,0:T(8,128)(2,1)}, u32[]{:S(2)}, u32[]{:S(2)}) collective-permute-start(bf16[2,2,1,2,192,384]{5,4,3,2,1,0:T(8,128)(2,1)} %shard_map.492.refs_1_), channel_id=1, source_target_pairs={{0,4},{4,0},{8,12},{12,8},{16,20},{20,16},{24,28},{28,24},{1,5},{5... | collective-permute-start | bytes 3538952 | tf_op jit(solution)/shard_map/ppermute | solution.py:102
  384.6 46.1 %collective-permute-start.26 = (bf16[2,2,2,1,192,384]{5,4,3,2,1,0:T(8,128)(2,1)}, bf16[2,2,2,1,192,384]{5,4,3,2,1,0:T(8,128)(2,1)}, u32[]{:S(2)}, u32[]{:S(2)}) collective-permute-start(bf16[2,2,2,1,192,384]{5,4,3,2,1,0:T(8,128)(2,1)} %shard_map.493.refs_1_), channel_id=1, source_target_pairs={{0,2},{1,3},{2,0},{3,1},{4,6},{5,7},{6,4},{7,5},{8,10},{9,11},{10,... | collective-permute-start | bytes 3538952 | tf_op jit(solution)/shard_map/ppermute | solution.py:102
  391.2 61.4 %collective-permute-start.27 = (bf16[2,2,2,1,160,384]{5,4,3,2,1,0:T(8,128)(2,1)}, bf16[2,2,2,1,160,384]{5,4,3,2,1,0:T(8,128)(2,1)S(1)}, u32[]{:S(2)}, u32[]{:S(2)}) collective-permute-start(bf16[2,2,2,1,160,384]{5,4,3,2,1,0:T(8,128)(2,1)} %shard_map.496.refs_1_), channel_id=1, source_target_pairs={{0,2},{1,3},{2,0},{3,1},{4,6},{5,7},{6,4},{7,5},{8,10},{9,11},{10,... | collective-permute-start | bytes 2949128 | tf_op jit(solution)/shard_map/ppermute | solution.py:102
  392.0 70.8 %collective-permute-start.28 = (bf16[2,2,1,2,192,384]{5,4,3,2,1,0:T(8,128)(2,1)}, bf16[2,2,1,2,192,384]{5,4,3,2,1,0:T(8,128)(2,1)S(1)}, u32[]{:S(2)}, u32[]{:S(2)}) collective-permute-start(bf16[2,2,1,2,192,384]{5,4,3,2,1,0:T(8,128)(2,1)} %shard_map.494.refs_0_), channel_id=1, source_target_pairs={{0,4},{4,0},{8,12},{12,8},{16,20},{20,16},{24,28},{28,24},{1,5},{5... | collective-permute-start | bytes 3538952 | tf_op jit(solution)/shard_map/ppermute | solution.py:102
  428.0 58.3 %collective-permute-start.29 = (bf16[1,2,1,2,192,384]{5,4,3,2,1,0:T(8,128)(2,1)}, bf16[1,2,1,2,192,384]{5,4,3,2,1,0:T(8,128)(2,1)S(1)}, u32[]{:S(2)}, u32[]{:S(2)}) collective-permute-start(bf16[1,2,1,2,192,384]{5,4,3,2,1,0:T(8,128)(2,1)} %shard_map.497.refs_1_), channel_id=1, source_target_pairs={{0,16},{4,20},{8,24},{12,28},{16,0},{20,4},{24,8},{28,12},{1,17},{... | collective-permute-start | bytes 1769480 | tf_op jit(solution)/shard_map/ppermute | solution.py:102
  433.7 56.2 %collective-permute-start.30 = (bf16[2,2,1,1,192,384]{5,4,3,2,1,0:T(8,128)(2,1)}, bf16[2,2,1,1,192,384]{5,4,3,2,1,0:T(8,128)(2,1)S(1)}, u32[]{:S(2)}, u32[]{:S(2)}) collective-permute-start(bf16[2,2,1,1,192,384]{5,4,3,2,1,0:T(8,128)(2,1)} %shard_map.498.refs_1_), channel_id=1, source_target_pairs={{0,4},{4,0},{8,12},{12,8},{16,20},{20,16},{24,28},{28,24},{1,5},{5... | collective-permute-start | bytes 1769480 | tf_op jit(solution)/shard_map/ppermute | solution.py:102
  456.6 65.7 %collective-permute-start.33 = (bf16[1,2,2,1,160,384]{5,4,3,2,1,0:T(8,128)(2,1)}, bf16[1,2,2,1,160,384]{5,4,3,2,1,0:T(8,128)(2,1)S(1)}, u32[]{:S(2)}, u32[]{:S(2)}) collective-permute-start(bf16[1,2,2,1,160,384]{5,4,3,2,1,0:T(8,128)(2,1)} %shard_map.499.refs_1_), channel_id=1, source_target_pairs={{0,16},{4,20},{8,24},{12,28},{16,0},{20,4},{24,8},{28,12},{1,17},{... | collective-permute-start | bytes 1474568 | tf_op jit(solution)/shard_map/ppermute | solution.py:102
  467.0 51.7 %collective-permute-start.32 = (bf16[2,2,1,1,192,384]{5,4,3,2,1,0:T(8,128)(2,1)}, bf16[2,2,1,1,192,384]{5,4,3,2,1,0:T(8,128)(2,1)S(1)}, u32[]{:S(2)}, u32[]{:S(2)}) collective-permute-start(bf16[2,2,1,1,192,384]{5,4,3,2,1,0:T(8,128)(2,1)} %shard_map.500.refs_1_), channel_id=1, source_target_pairs={{0,2},{1,3},{2,0},{3,1},{4,6},{5,7},{6,4},{7,5},{8,10},{9,11},{10,... | collective-permute-start | bytes 1769480 | tf_op jit(solution)/shard_map/ppermute | solution.py:102
  489.8 24.6 %collective-permute-start.31 = (bf16[1,1,1,2,192,384]{5,4,3,2,1,0:T(8,128)(2,1)}, bf16[1,1,1,2,192,384]{5,4,3,2,1,0:T(8,128)(2,1)S(1)}, u32[]{:S(2)}, u32[]{:S(2)}) collective-permute-start(bf16[1,1,1,2,192,384]{5,4,3,2,1,0:T(8,128)(2,1)} %shard_map.501.refs_1_), channel_id=1, source_target_pairs={{0,8},{4,12},{8,0},{12,4},{16,24},{20,28},{24,16},{28,20},{1,9},{5... | collective-permute-start | bytes 884744 | tf_op jit(solution)/shard_map/ppermute | solution.py:102
  493.5 42.0 %collective-permute-start.35 = (bf16[1,2,1,1,192,384]{5,4,3,2,1,0:T(8,128)(2,1)}, bf16[1,2,1,1,192,384]{5,4,3,2,1,0:T(8,128)(2,1)S(1)}, u32[]{:S(2)}, u32[]{:S(2)}) collective-permute-start(bf16[1,2,1,1,192,384]{5,4,3,2,1,0:T(8,128)(2,1)} %shard_map.502.refs_1_), channel_id=1, source_target_pairs={{0,16},{4,20},{8,24},{12,28},{16,0},{20,4},{24,8},{28,12},{1,17},{... | collective-permute-start | bytes 884744 | tf_op jit(solution)/shard_map/ppermute | solution.py:102
  517.8 14.3 %collective-permute-start.34 = (bf16[1,1,1,1,192,384]{5,4,3,2,1,0:T(8,128)(2,1)}, bf16[1,1,1,1,192,384]{5,4,3,2,1,0:T(8,128)(2,1)S(1)}, u32[]{:S(2)}, u32[]{:S(2)}) collective-permute-start(bf16[1,1,1,1,192,384]{5,4,3,2,1,0:T(8,128)(2,1)} %shard_map.503.refs_1_), channel_id=1, source_target_pairs={{0,2},{1,3},{2,0},{3,1},{4,6},{5,7},{6,4},{7,5},{8,10},{9,11},{10,... | collective-permute-start | bytes 442376 | tf_op jit(solution)/shard_map/ppermute | solution.py:102
  522.3 27.2 %collective-permute-start.38 = (bf16[1,2,1,1,192,384]{5,4,3,2,1,0:T(8,128)(2,1)}, bf16[1,2,1,1,192,384]{5,4,3,2,1,0:T(8,128)(2,1)S(1)}, u32[]{:S(2)}, u32[]{:S(2)}) collective-permute-start(bf16[1,2,1,1,192,384]{5,4,3,2,1,0:T(8,128)(2,1)} %shard_map.504.refs_1_), channel_id=1, source_target_pairs={{0,16},{4,20},{8,24},{12,28},{16,0},{20,4},{24,8},{28,12},{1,17},{... | collective-permute-start | bytes 884744 | tf_op jit(solution)/shard_map/ppermute | solution.py:102
  525.8 15.4 %collective-permute-start.36 = (bf16[1,1,2,1,160,384]{5,4,3,2,1,0:T(8,128)(2,1)}, bf16[1,1,2,1,160,384]{5,4,3,2,1,0:T(8,128)(2,1)S(1)}, u32[]{:S(2)}, u32[]{:S(2)}) collective-permute-start(bf16[1,1,2,1,160,384]{5,4,3,2,1,0:T(8,128)(2,1)} %shard_map.505.refs_1_), channel_id=1, source_target_pairs={{0,8},{4,12},{8,0},{12,4},{16,24},{20,28},{24,16},{28,20},{1,9},{5... | collective-permute-start | bytes 737288 | tf_op jit(solution)/shard_map/ppermute | solution.py:102
  538.8 6.3 %collective-permute-start.37 = (bf16[1,1,1,1,192,384]{5,4,3,2,1,0:T(8,128)(2,1)}, bf16[1,1,1,1,192,384]{5,4,3,2,1,0:T(8,128)(2,1)S(1)}, u32[]{:S(2)}, u32[]{:S(2)}) collective-permute-start(bf16[1,1,1,1,192,384]{5,4,3,2,1,0:T(8,128)(2,1)} %shard_map.507.refs_1_), channel_id=1, source_target_pairs={{0,8},{4,12},{8,0},{12,4},{16,24},{20,28},{24,16},{28,20},{1,9},{5... | collective-permute-start | bytes 442376 | tf_op jit(solution)/shard_map/ppermute | solution.py:102
  544.4 8.5 %collective-permute-start.39 = (bf16[1,1,1,1,160,384]{5,4,3,2,1,0:T(8,128)(2,1)}, bf16[1,1,1,1,160,384]{5,4,3,2,1,0:T(8,128)(2,1)S(1)}, u32[]{:S(2)}, u32[]{:S(2)}) collective-permute-start(bf16[1,1,1,1,160,384]{5,4,3,2,1,0:T(8,128)(2,1)} %shard_map.508.refs_1_), channel_id=1, source_target_pairs={{0,4},{4,0},{8,12},{12,8},{16,20},{20,16},{24,28},{28,24},{1,5},{5... | collective-permute-start | bytes 368648 | tf_op jit(solution)/shard_map/ppermute | solution.py:102
  552.9 5.7 collective-permute-start.40
  573.4 2.2 collective-permute-start.42
  590.8 3.6 collective-permute-start.44
  594.4 3.6 collective-permute-start.45
  598.0 3.6 collective-permute-start.46
  601.6 4.5 collective-permute-start.47
  (91 other events, 385.5 us)
Sparse Core Ops, SparseCore 0:
  13.9 151.9 all-gather.2
  299.0 217.5 reduce-scatter.1

commit v3 on v2

--- a/solution.py
+++ b/solution.py
@@ -60,27 +60,31 @@
     "u": ("zlo", "zhi", "x", "y"),
 }
 SCATTER = {
-    "l": ("Q1", "O1", "D1", "E1", "F1"),
+    "c": ("D1", "E1", "F1"),
+    "b": ("Q1", "O1"),
     "d": ("D0",),
     "u": ("E0", "F0"),
     "a": ("Q0", "O0"),
     "t": ("T",),
 }
 SCATTER_WAY = {
+    "b": ("x", "y", "zhi", "zlo"),
     "d": ("x", "y", "zhi", "zlo"),
-    "u": ("y", "zhi", "zlo", "x"),
+    "u": ("y", "x", "zhi", "zlo"),
     "a": ("y", "x", "zhi", "zlo"),
-    "t": ("x", "zhi", "zlo", "y"),
+    "t": ("x", "y", "zhi", "zlo"),
 }
 FORWARD_ORDER = (
-    ("t", "a", "d", "u", "t", "a", "t", "a", "d", "u", "t", "a", "embed", "d", "u", "attention0", "d", "u")
+    ("l", "t", "a", "d", "u", "t", "a", "t", "a", "d", "u", "t", "a", "embed", "d", "u", "attention0", "d", "u")
     + ("forward0", "attention1", "forward1", "head")
 )
 BACKWARD_ORDER = (
-    ("forward1", "attention1", "forward0", "attention0", "u", "d", "a", "embed", "t", "u", "d", "t", "a")
-    + ("u", "d", "u", "a", "t", "u", "d", "t", "d", "a", "t", "a")
+    ("forward1", "attention1", "forward0", "b", "attention0", "b", "u", "d", "a", "embed", "u", "d", "t")
+    + ("b", "a", "t", "u", "d", "b", "u", "a", "t", "d", "b", "u", "t", "d", "a", "t", "a")
 )
-LAST = (("l", "u"), ("d", "t", "a"))
+LONG = {5: 14, 10: 14, 11: 14}
+SETTLED = 15
+LAST = (("c", "b"), ("u", "d", "t", "a"))
 
 
 def placed(layout):
@@ -100,6 +104,14 @@
 def swap(tensor, hop):
     axis, flip, size, unused = HOPS[hop]
     return lax.ppermute(tensor, axis, [(i, i ^ flip) for i in range(size)])
+
+
+def swap_both(tensor, hops):
+    flips = [HOPS[hop] for hop in hops]
+    if flips[0][0] == flips[1][0]:
+        axis, flip, size = flips[0][0], flips[0][1] ^ flips[1][1], flips[0][2]
+        return lax.ppermute(tensor, axis, [(i, i ^ flip) for i in range(size)])
+    return swap(swap(tensor, hops[0]), hops[1])
 
 
 def side(hop):
@@ -415,7 +427,7 @@
         for copy in group:
             copy.start()
     scaled, spread = norm_parts(middle[...])
-    normed_t[...] = (scaled * vector[5:6] + vector[6:7]).T.astype(low)
+    normed_t[...] = (scaled * vector[5:6] + vector[6:7]).astype(low).T
     branch[...] = upstream[...].astype(low)
     vector_grad[...] = jnp.zeros_like(vector_grad)
     vector_grad[7:8] = rows_sum(branch[...].astype(full))
@@ -447,17 +459,19 @@
         if step >= 2:
             land(step - 2)
         grad_down = dot(active.T, branch[...]).astype(low)
-        down_stage[slot] = grad_down.reshape(4, 192, D)
+        for half in range(2):
+            down_stage[slot, half] = grad_down[:, half * UNIT : half * UNIT + UNIT].reshape(4, 192, UNIT)
         flight = []
         for half in range(2):
             place = targets[outs[0][0]].at[pl.ds(4 * tile, 4), half, pl.ds(outs[0][1], 192), :]
-            source = down_stage.at[slot, :, :, pl.ds(half * UNIT, UNIT)]
+            source = down_stage.at[slot, half]
             flight.append(pltpu.make_async_copy(source, place, out_sems.at[slot, half]))
         grad_up = dot(normed_t[...], grad_hidden).astype(low)
-        up_stage[slot] = grad_up.reshape(16, 48, D)
+        for unit in range(2):
+            up_stage[slot, unit] = grad_up[:, unit * UNIT : unit * UNIT + UNIT].reshape(16, 48, UNIT)
         half = own if step < 2 else 1 - own
         for unit in range(2):
-            source = up_stage.at[slot, :, :, pl.ds(unit * UNIT, UNIT)]
+            source = up_stage.at[slot, unit]
             at = outs[1 + slot][1] + 48 * unit
             flight.append(leave(source, targets[outs[1 + slot][0]], half, at, out_sems.at[slot, 2 + unit]))
         for copy in flight:
@@ -493,9 +507,10 @@
     grad_out_low = grad_middle[...].astype(low)
     vector_grad[...] = jnp.zeros_like(vector_grad)
     vector_grad[4:5] = rows_sum(grad_out_low.astype(full))
-    stage[3] = dot(mixed[...].T, grad_out_low).astype(low).reshape(16, 48, D)
+    grad_out = dot(mixed[...].T, grad_out_low).astype(low)
     for half in range(2):
-        source = stage.at[3, :, :, pl.ds(half * UNIT, UNIT)]
+        stage[3, half] = grad_out[:, half * UNIT : half * UNIT + UNIT].reshape(16, 48, UNIT)
+        source = stage.at[3, half]
         leaving.append(leave(source, out_target, half, out_at, out_sems.at[6 + half]))
         leaving[-1].start()
     for copy in out_copies:
@@ -531,7 +546,7 @@
 
     lax.fori_loop(0, HEADS // 2, pair, 0)
     scaled, spread = norm_parts(stream[...])
-    normed_t = (scaled * vector[0:1] + vector[1:2]).T.astype(low)
+    normed_t = (scaled * vector[0:1] + vector[1:2]).astype(low).T
     for copy in in_copies:
         copy.wait()
     grad_normed = jnp.zeros((TOKENS, D), full)
@@ -541,10 +556,11 @@
             vector_grad[2:3] = rows_sum(block.astype(full))
         if part == 2:
             vector_grad[3:4] = rows_sum(block.astype(full))
-        stage[part] = dot(normed_t, block).astype(low).reshape(16, 48, D)
+        grad_in = dot(normed_t, block).astype(low)
         for side_unit in range(2):
             unit = 2 * part + side_unit
-            source = stage.at[part, :, :, pl.ds(side_unit * UNIT, UNIT)]
+            stage[part, side_unit] = grad_in[:, side_unit * UNIT : side_unit * UNIT + UNIT].reshape(16, 48, UNIT)
+            source = stage.at[part, side_unit]
             leaving.append(leave(source, target, unit // 3, at + 48 * (unit % 3), out_sems.at[unit]))
             leaving[-1].start()
         grad_normed += dot_right(block, flat(w_in[:, :, part * D : (part + 1) * D]))
@@ -559,16 +575,17 @@
     target, stage, sems = refs[carried:]
     leaving = [pltpu.make_async_copy(small, target.at[:, :, pl.ds(at + 144, 16), :], sems.at[6])]
     leaving[0].start()
-    stream_t = upstream[...].T.astype(low)
-    chosen_t = chosen[...].astype(full).T.astype(low)
+    stream_t = upstream[...].astype(low).T
+    chosen_t = chosen[...].T
     for tile in range(3):
         word = lax.broadcasted_iota(jnp.int32, (TOKENS, D), 1) + tile * D
         hot = jnp.where(word == ids[...], 1.0, 0.0).astype(low)
         block = dot(stream_t, hot) + dot(chosen_t, grad_logits[:, tile * D : tile * D + D])
-        stage[tile] = block.astype(low).reshape(16, 48, D)
         for side_unit in range(2):
             unit = 2 * tile + side_unit
-            source = stage.at[tile, :, :, pl.ds(side_unit * UNIT, UNIT)]
+            part = block[:, side_unit * UNIT : side_unit * UNIT + UNIT].astype(low)
+            stage[tile, side_unit] = part.reshape(16, 48, UNIT)
+            source = stage.at[tile, side_unit]
             leaving.append(leave(source, target, unit // 3, at + 48 * (unit % 3), sems.at[unit]))
             leaving[-1].start()
     for copy in leaving:
@@ -581,13 +598,18 @@
 
 class Line:
     def __init__(self, token):
-        self.token = token
+        self.tokens = [token]
+
+    def wait(self, array):
+        self.tokens.append(array)
 
     def call(self, kernel, operands, in_specs, outs, out_specs, scratch, grid=None, prefetch=0, aliases=None, cost=0):
+        tokens, extra = self.tokens, len(self.tokens)
+
         def ordered(*refs):
-            return kernel(*refs[:prefetch], *refs[prefetch + 1 :])
-
-        in_specs = [ANY] + in_specs
+            return kernel(*refs[:prefetch], *refs[prefetch + extra :])
+
+        in_specs = [ANY] * extra + in_specs
         if grid is None:
             how = dict(in_specs=in_specs, out_specs=out_specs, scratch_shapes=scratch)
         else:
@@ -602,17 +624,18 @@
         results = pl.pallas_call(
             ordered,
             out_shape=outs,
-            compiler_params=pltpu.CompilerParams(vmem_limit_bytes=56 * 2**20),
+            compiler_params=pltpu.CompilerParams(vmem_limit_bytes=63 * 2**20),
             cost_estimate=pl.CostEstimate(flops=1000 + int(cost * 1.15e9), bytes_accessed=1000, transcendentals=0),
-            input_output_aliases={source + 1: target for source, target in (aliases or {}).items()},
+            input_output_aliases={source + extra: target for source, target in (aliases or {}).items()},
             **how,
-        )(*operands[:prefetch], self.token, *operands[prefetch:])
-        self.token = results[0]
+        )(*operands[:prefetch], *tokens, *operands[prefetch:])
+        if not aliases or aliases.get(0) != 0:
+            self.tokens = [results[0]]
         return results
 
 
 DMA = pltpu.SemaphoreType.DMA
-MERGE_COST, JOIN_COST = 3, 3
+JOIN_COST = 3
 
 
 def embed(line, core, codes, pos, valid, pair, at):
@@ -712,15 +735,15 @@
             pltpu.VMEM((D, TOKENS), low),
             pltpu.VMEM((TOKENS, D), low),
             pltpu.VMEM((2, TOKENS, D), full),
-            pltpu.VMEM((2, 4, 192, D), low),
-            pltpu.VMEM((2, 16, 48, D), low),
+            pltpu.VMEM((2, 2, 4, 192, UNIT), low),
+            pltpu.VMEM((2, 2, 16, 48, UNIT), low),
             pltpu.VMEM((TOKENS, D), full),
             DMA((16,)),
             DMA((2,)),
             DMA((2, 4)),
         ],
         aliases=aliases,
-        cost=22,
+        cost=1,
     )
     grads.arrays.update(zip(names, results[2:]))
     return results[:2]
@@ -739,12 +762,12 @@
             pltpu.VMEM((16, 48, D), low),
             pltpu.VMEM((TOKENS, D), low),
             pltpu.VMEM((3, TOKENS, D), low),
-            pltpu.VMEM((4, 16, 48, D), low),
+            pltpu.VMEM((4, 2, 16, 48, UNIT), low),
             DMA((8,)),
             DMA((8,)),
         ],
         aliases=aliases,
-        cost=24,
+        cost=1,
     )
     grads.arrays.update(zip(names, results[2:]))
     return results[:2]
@@ -758,11 +781,19 @@
         [VMEM] * 4 + [ANY] * (1 + len(more)),
         tuple(shapes),
         (ANY,) * len(shapes),
-        [pltpu.VMEM((3, 16, 48, D), low), DMA((8,))],
+        [pltpu.VMEM((3, 2, 16, 48, UNIT), low), DMA((8,))],
         aliases=aliases,
-        cost=15,
+        cost=1,
     )
     grads.arrays.update(zip(names, results))
+
+
+def pass_on(line, array):
+    def kernel(unused, out):
+        pass
+
+    shape = (shape_of(*array.shape, kind=array.dtype),)
+    return line.call(kernel, (array,), [ANY], shape, (ANY,), [], aliases={0: 0})[0]
 
 
 def join(line, bits, axis, own, other):
@@ -797,11 +828,11 @@
     return line.call(kernel, operands, [SMEM, ANY, ANY], (shape_of(*dims, kind=low),), (ANY,), scratch, cost=JOIN_COST)[0]
 
 
-def merge(line, bits, parts, gone, axis, kind=None):
+def merge(line, bits, parts, gone, axis, cost=2):
     rows = parts[-1].shape[-2]
     open_axes = [i for i in range(4) if i not in gone and i != axis]
     dims = [2 if i in open_axes else 1 for i in range(4)]
-    kind = kind or (full if axis is None else low)
+    kind = full if axis is None else low
     cut = open_axes[0] if open_axes else None
     block = [1 if i == cut else size for i, size in enumerate(dims)]
 
@@ -836,7 +867,7 @@
         [],
         grid=(1 if cut is None else 2,),
         prefetch=1,
-        cost=MERGE_COST,
+        cost=cost,
     )[0]
 
 
@@ -900,8 +931,7 @@
         for name in GATHER:
             chunk = jnp.concatenate([whole[piece] for piece in GATHER[name]])
             if name not in GATHER_WAY:
-                chunk = lax.all_gather(chunk, BOTH, axis=0)
-                pairs[name] = [chunk.reshape(16, 2, *chunk.shape[1:])] * 2
+                whole[name] = chunk
                 continue
             chunk = chunk[None, None, None, None]
             flying[name], done[name] = (chunk, swap(chunk, GATHER_WAY[name][0])), 0
@@ -941,9 +971,12 @@
 
     kept = [None] * L
     for step in FORWARD_ORDER:
-        if step in GATHER_WAY:
-            if hops:
+        if step in GATHER:
+            if hops and step in GATHER_WAY:
                 next_hop(step)
+            elif hops:
+                chunk = lax.all_gather(pass_on(line, whole[step]), BOTH, axis=0)
+                pairs[step] = [chunk.reshape(16, 2, *chunk.shape[1:])] * 2
         elif step == "embed":
             (pair,), (at,) = sources("T")
             ids, stream = embed(line, own, codes_column, pos_row, valid_row, pair, at)
@@ -972,7 +1005,7 @@
 
     grads = Grads()
     vector_grads = [0.0] * L
-    parts, gone, totals = {}, {}, {}
+    parts, gone, totals, settled = {}, {}, {}, None
 
     def small_blocks():
         small = [vector_grads[0].reshape(-1), vector_grads[1].reshape(-1), final_grad[0], final_grad[1]]
@@ -995,6 +1028,7 @@
                 grad = grad.reshape(32, -1, UNIT)
                 total = lax.psum_scatter(grad, BOTH, scatter_dimension=0, tiled=False)
                 parts[name], totals[name] = None, total.astype(full)
+                return total
 
     complete = {name: [p for p in SCATTER[name]] for name in SCATTER}
 
@@ -1002,10 +1036,9 @@
         for piece in pieces:
             complete[grads.places[piece][0]].remove(piece)
         names = [name for name in SCATTER if name in grads.arrays and not complete[name] and name not in parts]
-        if hops:
-            ready(names)
-
-    for step in BACKWARD_ORDER:
+        return ready(names) if hops else None
+
+    for at, step in enumerate(BACKWARD_ORDER):
         if step in SCATTER_WAY:
             if not hops:
                 continue
@@ -1015,7 +1048,10 @@
                 continue
             hop = way[len(gone[step])]
             axis = HOPS[hop][3]
-            parts[step].append(swap(merge(line, bits, parts[step], gone[step], axis), hop))
+            cost = LONG.get(at, 2)
+            if at == SETTLED:
+                line.wait(settled)
+            parts[step].append(swap(merge(line, bits, parts[step], gone[step], axis, cost), hop))
             gone[step].append(axis)
         elif step == "embed":
             small_grads, block = small_blocks()
@@ -1037,7 +1073,8 @@
                 line, grads, l, own, upstream, kept[l][4], vectors[l], kept[l][5], three, ats
             )
             vector_grads[l] += late
-            finished((f"D{l}", f"E{l}", f"F{l}"))
+            total = finished((f"D{l}", f"E{l}", f"F{l}"))
+            settled = settled if total is None else total
 
     shares = {}
     if hops:
@@ -1064,8 +1101,7 @@
         for piece in list(shares):
             block = shares[piece]
             shares[piece] = block.transpose(2, 0, 1, 3).reshape(block.shape[2], -1)
-        at = grads.places["T"][1] + 144
-        small_sum = totals[grads.places["T"][0]][at : at + 2].reshape(-1)
+        small_sum = totals[grads.places["T"][0]][144:146].reshape(-1)
     else:
         head_grad, loss_sum = lax.psum((bias_grad[0, :V], loss[0, 0]), BOTH)
         small_sum = [lax.psum_scatter(g, BOTH, scatter_dimension=0, tiled=True) for g in small_grads]
@@ -1086,19 +1122,27 @@
         small_sum[: 2 * width].reshape(L, width),
         small_sum[2 * width : 2 * width + 2 * narrow].reshape(2, narrow),
     ]
-    squares = reduce(jnp.add, [jnp.sum(share * share) for share in grads_own])
     if hops:
+        squares = reduce(jnp.add, [jnp.sum(totals[name] * totals[name]) for name in SCATTER])
         bias_share = small_sum[624:688]
-        squares = squares + jnp.sum(bias_share * bias_share)
         tail = jnp.concatenate([bias_share, squares[None], loss[0, :1], jnp.zeros(62)])
         tail = tail.reshape(1, 1, 1, 1, 1, 128)
-        for hop in ("core", "x", "y", "zlo", "zhi"):
-            axis = HOPS[hop][3]
-            tail = in_order(side(hop), tail, swap(tail, hop), 4 if axis is None else axis)
+        for group in (("core",), ("x", "y"), ("zhi", "zlo")):
+            if len(group) == 1:
+                tail = jnp.concatenate([tail, swap(tail, group[0])], 4)
+                continue
+            axis, flips = [HOPS[hop][3] for hop in group], [swap(tail, hop) for hop in group]
+            across = swap_both(tail, group)
+            tail = jnp.concatenate(
+                [jnp.concatenate([tail, flips[1]], axis[1]), jnp.concatenate([flips[0], across], axis[1])], axis[0]
+            )
+        for hop, axis in (("core", 4), ("x", 3), ("y", 2), ("zlo", 1), ("zhi", 0)):
+            tail = jnp.where(side(hop) == 0, tail, jnp.flip(tail, axis))
         tail = tail.reshape(32, 128)
         head_grad = tail[:, :64].reshape(-1)[:V]
         squares, loss_sum = jnp.sum(tail[:, 64]), jnp.sum(tail[:, 65])
     else:
+        squares = reduce(jnp.add, [jnp.sum(share * share) for share in grads_own])
         squares = lax.psum(squares, BOTH) + jnp.sum(head_grad * head_grad)
     grad_norm = jnp.sqrt(squares)
     factor = jnp.minimum(1.0, clip_bound / (grad_norm + epsilon))

time: 635 us -> 596 us (0.939)
  waiting for transfers between devices: 178 us -> 126 us
  Pallas kernels: 279 us -> 288 us
    ppermute x48 -> x54, waiting for transfers between devices: 178 us -> 123 us  [swap(): return lax.ppermute(tensor, axis, [(i, i ^ flip) for i in range(size)])]
    unnamed x203 -> x164, local copies, waits for them, and re-layouts: 31.9 us -> 19.1 us
    pallas_call x47 -> x53, Pallas kernels: 279 us -> 288 us  [call(): pl.pallas_call(ordered, out_shape=outs, compiler_params=pltpu.CompilerPar...]
    squeeze x4 -> x5, local copies, waits for them, and re-layouts: 9.05 us -> 15.2 us  [ready(): arrived = swap(pick(grad, 1 - core, 1)[:, 0], 'core')]
    ppermute x48 -> x54, starting transfers between devices: 59.4 us -> 61.4 us  [swap(): return lax.ppermute(tensor, axis, [(i, i ^ flip) for i in range(size)])]
  transfers between devices with their start and end apart: 50 -> 57, of which waited for: 27 -> 21; matrix products, arithmetic and copies ran while one was open for 5% -> 10% of each run, Pallas kernels for 31% -> 39%
where the time goes in v3:
time: 596 us; the launch traced here: 587 us
  Pallas kernels  288 us (48%)
  waiting for transfers between devices  126 us (21%)
  starting transfers between devices  63.5 us (11%)
  local copies, waits for them, and re-layouts  59.3 us (10%)
  other arithmetic  26.9 us (5%)
  between operations  22.9 us (4%)
    pallas_call x53, Pallas kernels, call(): pl.pallas_call(ordered, out_shape=outs, compiler_params=pltpu.CompilerPar...  288 us
    ppermute x54, waiting for transfers between devices, swap(): return lax.ppermute(tensor, axis, [(i, i ^ flip) for i in range(size)])  123 us
    ppermute x54, starting transfers between devices, swap(): return lax.ppermute(tensor, axis, [(i, i ^ flip) for i in range(size)])  61.4 us
    unnamed x164, local copies, waits for them, and re-layouts  19.1 us
    squeeze x5, local copies, waits for them, and re-layouts, ready(): arrived = swap(pick(grad, 1 - core, 1)[:, 0], 'core')  15.2 us
  transfers between devices with their start and end apart: 57, of which 21 were waited for; matrix products, arithmetic and copies ran while one was open for 10% of the time, Pallas kernels for 39%

profile of v3, /device:TPU:0, one launch (start us, length us, event | category | flops | bytes accessed | tf_op | source)
XLA Modules:
  0.0 586.5 jit_solution(6782168477804863233)
XLA Ops:
  15.5 3.0 collective-permute-start.4
  21.7 8.5 %collective-permute-done.1.refs_3_ = bf16[1,1,1,1,160,384]{5,4,3,2,1,0:T(8,128)(2,1)S(1)} collective-permute-done((bf16[1,1,1,1,160,384]{5,4,3,2,1,0:T(8,128)(2,1)S(1)}, bf16[1,1,1,1,160,384]{5,4,3,2,1,0:T(8,128)(2,1)S(1)}, u32[]{:S(2)}, u32[]{:S(2)}) %collective-permute-start.1) | collective-permute-done | bytes 122912 | tf_op jit(solution)/shard_map/ppermute | solution.py:106
  33.2 3.9 collective-permute-start.5
  40.8 3.2 collective-permute-start.6
  48.7 10.5 %collective-permute-done.5.refs_3_ = bf16[1,2,1,1,160,384]{5,4,3,2,1,0:T(8,128)(2,1)S(1)} collective-permute-done((bf16[1,2,1,1,160,384]{5,4,3,2,1,0:T(8,128)(2,1)}, bf16[1,2,1,1,160,384]{5,4,3,2,1,0:T(8,128)(2,1)S(1)}, u32[]{:S(2)}, u32[]{:S(2)}) %collective-permute-start.5) | collective-permute-done | bytes 245792 | tf_op jit(solution)/shard_map/ppermute | solution.py:106
  64.2 3.1 collective-permute-done.6.refs_3_
  72.0 7.8 %collective-permute-done.7.refs_3_ = bf16[2,2,1,1,160,384]{5,4,3,2,1,0:T(8,128)(2,1)} collective-permute-done((bf16[2,2,1,1,160,384]{5,4,3,2,1,0:T(8,128)(2,1)}, bf16[2,2,1,1,160,384]{5,4,3,2,1,0:T(8,128)(2,1)}, u32[]{:S(2)}, u32[]{:S(2)}) %collective-permute-start.7) | collective-permute-done | bytes 491552 | tf_op jit(solution)/shard_map/ppermute | solution.py:106
  84.1 2.9 collective-permute-start.10
  94.8 14.5 %collective-permute-done.9.refs_3_ = bf16[1,2,1,1,192,384]{5,4,3,2,1,0:T(8,128)(2,1)} collective-permute-done((bf16[1,2,1,1,192,384]{5,4,3,2,1,0:T(8,128)(2,1)S(1)}, bf16[1,2,1,1,192,384]{5,4,3,2,1,0:T(8,128)(2,1)}, u32[]{:S(2)}, u32[]{:S(2)}) %collective-permute-start.9) | collective-permute-done | bytes 294944 | tf_op jit(solution)/shard_map/ppermute | solution.py:106
  112.0 13.1 %collective-permute-done.10.refs_3_ = bf16[1,2,1,1,192,384]{5,4,3,2,1,0:T(8,128)(2,1)} collective-permute-done((bf16[1,2,1,1,192,384]{5,4,3,2,1,0:T(8,128)(2,1)}, bf16[1,2,1,1,192,384]{5,4,3,2,1,0:T(8,128)(2,1)}, u32[]{:S(2)}, u32[]{:S(2)}) %collective-permute-start.10) | collective-permute-done | bytes 294944 | tf_op jit(solution)/shard_map/ppermute | solution.py:106
  127.7 3.1 shard_map.476.refs_0_
  130.9 3.3 shard_map.477.refs_0_
  138.8 6.2 %shard_map.478 = (s32[512,1]{1,0:T(8,128)}, f32[512,768]{1,0:T(8,128)}) custom-call(bf16[2,2,2,2,192,384]{5,4,3,2,1,0:T(8,128)(2,1)} %shard_map.477.refs_0_, s32[1]{0:T(128)} %bitcast.4.refs_0_.refs_1_, s32[512,1]{1,0:T(8,128)} %bitcast.355, s32[1,256]{1,0:T(1,128)} %bitcast.379, f32[1,256]{1,0:T(1,128)} %bitcast.384, bf16[16,160,384]{2,1,0:T(8,128)(2,1)} %bitcast.388, ...), custom_call_target="tpu_custom_call" | custom-call | flops 6900000768 | bytes 1000 | tf_op jit(solution)/shard_map/pallas_call | solution.py:624
  147.1 9.2 %collective-permute-done.14.refs_3_ = bf16[2,2,1,1,192,384]{5,4,3,2,1,0:T(8,128)(2,1)} collective-permute-done((bf16[2,2,1,1,192,384]{5,4,3,2,1,0:T(8,128)(2,1)}, bf16[2,2,1,1,192,384]{5,4,3,2,1,0:T(8,128)(2,1)}, u32[]{:S(2)}, u32[]{:S(2)}) %collective-permute-start.14) | collective-permute-done | bytes 589856 | tf_op jit(solution)/shard_map/ppermute | solution.py:106
  164.0 14.7 %shard_map.481 = (bf16[3,512,768]{2,1,0:T(8,128)(2,1)}, f32[512,128]{1,0:T(8,128)}, bf16[512,768]{1,0:T(8,128)(2,1)}, f32[512,768]{1,0:T(8,128)}) custom-call(bf16[2,2,1,2,192,384]{5,4,3,2,1,0:T(8,128)(2,1)} %shard_map.480.refs_0_.refs_2_, s32[1]{0:T(128)} %bitcast.4.refs_0_.refs_1_, f32[512,768]{1,0:T(8,128)} %get-tuple-element.61.refs_2_.refs_3_, ...), custom_call_target="tpu_custom_call" | custom-call | flops 17250000896 | bytes 1000 | tf_op jit(solution)/shard_map/pallas_call | solution.py:624
  178.8 8.5 %collective-permute-done.17.refs_3_ = bf16[2,2,2,1,192,384]{5,4,3,2,1,0:T(8,128)(2,1)} collective-permute-done((bf16[2,2,2,1,192,384]{5,4,3,2,1,0:T(8,128)(2,1)}, bf16[2,2,2,1,192,384]{5,4,3,2,1,0:T(8,128)(2,1)}, u32[]{:S(2)}, u32[]{:S(2)}) %collective-permute-start.17) | collective-permute-done | bytes 1179680 | tf_op jit(solution)/shard_map/ppermute | solution.py:106
  187.2 3.2 shard_map.482.refs_0_
  190.5 3.2 shard_map.483.refs_0_
  202.0 11.9 %shard_map.484 = (f32[4,512,768]{2,1,0:T(8,128)}, f32[512,768]{1,0:T(8,128)}) custom-call(bf16[2,2,2,2,192,384]{5,4,3,2,1,0:T(8,128)(2,1)} %shard_map.483.refs_0_, s32[1]{0:T(128)} %bitcast.4.refs_0_.refs_1_, f32[512,768]{1,0:T(8,128)} %get-tuple-element.63.refs_2_.refs_3_, f32[12,768]{1,0:T(8,128)} %reshape.664.refs_3_.refs_4_, ...), custom_call_target="tpu_custom_call" | custom-call | flops 13800000512 | bytes 1000 | tf_op jit(solution)/shard_map/pallas_call | solution.py:624
  214.0 14.9 %shard_map.486 = (bf16[3,512,768]{2,1,0:T(8,128)(2,1)}, f32[512,128]{1,0:T(8,128)}, bf16[512,768]{1,0:T(8,128)(2,1)}, f32[512,768]{1,0:T(8,128)}) custom-call(f32[4,512,768]{2,1,0:T(8,128)} %get-tuple-element.64.refs_0_.refs_5_, s32[1]{0:T(128)} %bitcast.4.refs_0_.refs_1_, f32[512,768]{1,0:T(8,128)} %get-tuple-element.65.refs_2_.refs_3_, ...), custom_call_target="tpu_custom_call" | custom-call | flops 17250000896 | bytes 1000 | tf_op jit(solution)/shard_map/pallas_call | solution.py:624
  229.0 12.0 %shard_map.487 = (f32[4,512,768]{2,1,0:T(8,128)}, f32[512,768]{1,0:T(8,128)}) custom-call(bf16[3,512,768]{2,1,0:T(8,128)(2,1)} %get-tuple-element.66.refs_0_.refs_5_, s32[1]{0:T(128)} %bitcast.4.refs_0_.refs_1_, f32[512,768]{1,0:T(8,128)} %get-tuple-element.67.refs_2_.refs_3_, f32[12,768]{1,0:T(8,128)} %reshape.671.refs_3_.refs_4_, ...), custom_call_target="tpu_custom_call" | custom-call | flops 13800000512 | bytes 1000 | tf_op jit(solution)/shard_map/pallas_call | solution.py:624
  241.0 9.8 %shard_map.488 = (f32[512,768]{1,0:T(8,128)}, bf16[256,768]{1,0:T(8,128)(2,1)}, bf16[256,2304]{1,0:T(8,128)(2,1)}, f32[1,2304]{1,0:T(1,128)}, f32[2,768]{1,0:T(2,128)}, /*index=5*/f32[1,128]{1,0:T(1,128)}) custom-call(f32[4,512,768]{2,1,0:T(8,128)} %get-tuple-element.68.refs_0_.refs_5_, s32[1]{0:T(128)} %bitcast.4.refs_0_.refs_1_, ...), custom_call_target="tpu_custom_call" | custom-call | flops 11500001280 | bytes 1000 | tf_op jit(solution)/shard_map/pallas_call | solution.py:624
  250.8 20.9 %shard_map.489 = (f32[512,768]{1,0:T(8,128)}, f32[12,768]{1,0:T(8,128)}, bf16[16,2,384,384]{3,2,1,0:T(8,128)(2,1)}) custom-call(f32[512,768]{1,0:T(8,128)} %get-tuple-element.70.refs_0_.refs_2_, s32[1]{0:T(128)} %bitcast.4.refs_0_.refs_1_, f32[512,768]{1,0:T(8,128)} %get-tuple-element.70.refs_0_.refs_2_, f32[512,768]{1,0:T(8,128)} %get-tuple-element.67.refs_2_.refs_3_, ...), custom_call_target="tpu_custom_call" | custom-call | flops 1150001024 | bytes 1000 | tf_op jit(solution)/shard_map/pallas_call | solution.py:624
  271.7 23.3 %shard_map.490 = (f32[512,768]{1,0:T(8,128)}, f32[12,768]{1,0:T(8,128)}, bf16[16,2,192,384]{3,2,1,0:T(8,128)(2,1)}) custom-call(f32[512,768]{1,0:T(8,128)} %get-tuple-element.71.refs_0_.refs_2_, s32[1]{0:T(128)} %bitcast.4.refs_0_.refs_1_, f32[512,768]{1,0:T(8,128)} %get-tuple-element.71.refs_0_.refs_2_, f32[512,768]{1,0:T(8,128)} %get-tuple-element.65.refs_2_.refs_3_, ...), custom_call_target="tpu_custom_call" | custom-call | flops 1150001024 | bytes 1000 | tf_op jit(solution)/shard_map/pallas_call | solution.py:624
  295.0 3.5 dynamic-slice_bitcast_fusion.3
  298.6 20.8 %shard_map.491 = (f32[512,768]{1,0:T(8,128)}, f32[12,768]{1,0:T(8,128)}, bf16[16,2,192,384]{3,2,1,0:T(8,128)(2,1)}, bf16[16,2,192,384]{3,2,1,0:T(8,128)(2,1)}) custom-call(f32[512,768]{1,0:T(8,128)} %get-tuple-element.74.refs_0_.refs_2_, s32[1]{0:T(128)} %bitcast.4.refs_0_.refs_1_, f32[512,768]{1,0:T(8,128)} %get-tuple-element.74.refs_0_.refs_2_, ...), custom_call_target="tpu_custom_call" | custom-call | flops 1150001024 | bytes 1000 | tf_op jit(solution)/shard_map/pallas_call | solution.py:624
  319.5 3.3 shard_map.492.refs_0_
  324.1 3.5 dynamic-slice_bitcast_fusion.2
  329.8 23.5 %shard_map.493 = (f32[512,768]{1,0:T(8,128)}, f32[12,768]{1,0:T(8,128)}, bf16[16,2,192,384]{3,2,1,0:T(8,128)(2,1)}) custom-call(bf16[2,2,2,1,192,384]{5,4,3,2,1,0:T(8,128)(2,1)} %shard_map.492.refs_0_, s32[1]{0:T(128)} %bitcast.4.refs_0_.refs_1_, f32[512,768]{1,0:T(8,128)} %get-tuple-element.75.refs_1_.refs_2_, ...), custom_call_target="tpu_custom_call" | custom-call | flops 1150001024 | bytes 1000 | tf_op jit(solution)/shard_map/pallas_call | solution.py:624
  353.3 3.4 dynamic-slice_bitcast_fusion
  357.3 6.8 %collective-permute-done.22.refs_4_ = bf16[2,2,2,1,192,384]{5,4,3,2,1,0:T(8,128)(2,1)} collective-permute-done((bf16[2,2,2,1,192,384]{5,4,3,2,1,0:T(8,128)(2,1)}, bf16[2,2,2,1,192,384]{5,4,3,2,1,0:T(8,128)(2,1)}, u32[]{:S(2)}, u32[]{:S(2)}) %collective-permute-start.22) | collective-permute-done | bytes 1179680 | tf_op jit(solution)/shard_map/ppermute | solution.py:106
  364.1 2.9 shard_map.494.refs_1_
  367.1 3.4 shard_map.495.refs_1_
  374.1 3.3 shard_map.496.refs_1_
  378.3 3.2 shard_map.497.refs_0_
  383.1 15.0 %shard_map.498.refs_1_ = bf16[16,2,160,384]{3,2,1,0:T(8,128)(2,1)} custom-call(bf16[2,2,1,2,192,384]{5,4,3,2,1,0:T(8,128)(2,1)} %shard_map.497.refs_0_, f32[512,768]{1,0:T(8,128)} %get-tuple-element.79.refs_1_, s32[512,1]{1,0:T(8,128)} %get-tuple-element.60.refs_0_.refs_2_, bf16[256,768]{1,0:T(8,128)(2,1)} %get-tuple-element.83.refs_3_, ...), custom_call_target="tpu_custom_call" | custom-call | flops 1150001024 | bytes 1000 | tf_op jit(solution)/shard_map/pallas_call | solution.py:624
  398.2 3.0 dynamic-slice_bitcast_fusion.4
  401.2 6.9 %collective-permute-done.26.refs_4_ = bf16[2,2,1,2,192,384]{5,4,3,2,1,0:T(8,128)(2,1)} collective-permute-done((bf16[2,2,1,2,192,384]{5,4,3,2,1,0:T(8,128)(2,1)}, bf16[2,2,1,2,192,384]{5,4,3,2,1,0:T(8,128)(2,1)}, u32[]{:S(2)}, u32[]{:S(2)}) %collective-permute-start.26) | collective-permute-done | bytes 1179680 | tf_op jit(solution)/shard_map/ppermute | solution.py:106
  408.1 3.0 shard_map.499.refs_1_
  411.1 2.9 shard_map.500.refs_1_
  414.0 3.1 shard_map.501.refs_1_
  426.4 4.1 collective-permute-start.34
  430.5 17.7 %collective-permute-done.30.refs_4_ = bf16[2,2,1,2,192,384]{5,4,3,2,1,0:T(8,128)(2,1)} collective-permute-done((bf16[2,2,1,2,192,384]{5,4,3,2,1,0:T(8,128)(2,1)}, bf16[2,2,1,2,192,384]{5,4,3,2,1,0:T(8,128)(2,1)}, u32[]{:S(2)}, u32[]{:S(2)}) %collective-permute-start.30) | collective-permute-done | bytes 1179680 | tf_op jit(solution)/shard_map/ppermute | solution.py:106
  448.2 2.9 shard_map.503.refs_1_
  452.0 3.0 shard_map.504.refs_1_
  459.4 3.9 collective-permute-start.35
  463.3 3.0 shard_map.506.refs_1_
  477.7 3.3 collective-permute-done.35.refs_6_
  (465 shorter events, 199.1 us)
Async XLA Ops:
  7.2 206.8 %all-gather.3.cloned.1.call-start = ((), (), s32[]{:S(2)}) async-start(), calls=%async_computation.2 | async-start | bytes 14598144 | tf_op jit(solution)/shard_map/all_gather | solution.py:978
  14.4 437.6 %reduce-scatter.2.cloned.1.call-start = ((), (), s32[]{:S(2)}) async-start(), calls=%async_computation.1 | async-start | bytes 9732096 | tf_op jit(solution)/shard_map/reduce_scatter | solution.py:1029
  15.5 30.9 %collective-permute-start.4 = (bf16[1,1,1,1,192,384]{5,4,3,2,1,0:T(8,128)(2,1)S(1)}, bf16[1,1,1,1,192,384]{5,4,3,2,1,0:T(8,128)(2,1)}, u32[]{:S(2)}, u32[]{:S(2)}) collective-permute-start(bf16[1,1,1,1,192,384]{5,4,3,2,1,0:T(8,128)(2,1)S(1)} %maximum_bitcast_fusion.3.refs_2_), channel_id=1, source_target_pairs={{0,8},{4,12},{8,0},{12,4},{16,24},{20,28},{24,16},{28,20},{1,9},{5... | collective-permute-start | bytes 442376 | tf_op jit(solution)/shard_map/ppermute | solution.py:106
  18.5 25.5 %collective-permute-start.3 = (bf16[1,1,1,1,192,384]{5,4,3,2,1,0:T(8,128)(2,1)S(1)}, bf16[1,1,1,1,192,384]{5,4,3,2,1,0:T(8,128)(2,1)}, u32[]{:S(2)}, u32[]{:S(2)}) collective-permute-start(bf16[1,1,1,1,192,384]{5,4,3,2,1,0:T(8,128)(2,1)S(1)} %bitcast.373), channel_id=1, source_target_pairs={{0,8},{4,12},{8,0},{12,4},{16,24},{20,28},{24,16},{28,20},{1,9},{5... | collective-permute-start | bytes 442376 | tf_op jit(solution)/shard_map/ppermute | solution.py:106
  18.7 11.6 %collective-permute-start.1 = (bf16[1,1,1,1,160,384]{5,4,3,2,1,0:T(8,128)(2,1)S(1)}, bf16[1,1,1,1,160,384]{5,4,3,2,1,0:T(8,128)(2,1)S(1)}, u32[]{:S(2)}, u32[]{:S(2)}) collective-permute-start(bf16[1,1,1,1,160,384]{5,4,3,2,1,0:T(8,128)(2,1)S(1)} %fusion.3.refs_2_), channel_id=1, source_target_pairs={{0,8},{4,12},{8,0},{12,4},{16,24},{20,28},{24,16},{28,20},{1,9},{5... | collective-permute-start | bytes 368648 | tf_op jit(solution)/shard_map/ppermute | solution.py:106
  21.6 16.8 %collective-permute-start.2 = (bf16[1,1,1,1,192,384]{5,4,3,2,1,0:T(8,128)(2,1)S(1)}, bf16[1,1,1,1,192,384]{5,4,3,2,1,0:T(8,128)(2,1)}, u32[]{:S(2)}, u32[]{:S(2)}) collective-permute-start(bf16[1,1,1,1,192,384]{5,4,3,2,1,0:T(8,128)(2,1)S(1)} %maximum_bitcast_fusion.2.refs_2_), channel_id=1, source_target_pairs={{0,8},{4,12},{8,0},{12,4},{16,24},{20,28},{24,16},{28,20},{1,9},{5... | collective-permute-start | bytes 442376 | tf_op jit(solution)/shard_map/ppermute | solution.py:106
  33.2 26.0 %collective-permute-start.5 = (bf16[1,2,1,1,160,384]{5,4,3,2,1,0:T(8,128)(2,1)}, bf16[1,2,1,1,160,384]{5,4,3,2,1,0:T(8,128)(2,1)S(1)}, u32[]{:S(2)}, u32[]{:S(2)}) collective-permute-start(bf16[1,2,1,1,160,384]{5,4,3,2,1,0:T(8,128)(2,1)} %shard_map.466.refs_0_.refs_2_), channel_id=1, source_target_pairs={{0,16},{4,20},{8,24},{12,28},{16,0},{20,4},{24,8},{28,12},{1,17},{... | collective-permute-start | bytes 737288 | tf_op jit(solution)/shard_map/ppermute | solution.py:106
  40.8 26.5 %collective-permute-start.6 = (bf16[1,2,1,1,192,384]{5,4,3,2,1,0:T(8,128)(2,1)}, bf16[1,2,1,1,192,384]{5,4,3,2,1,0:T(8,128)(2,1)S(1)}, u32[]{:S(2)}, u32[]{:S(2)}) collective-permute-start(bf16[1,2,1,1,192,384]{5,4,3,2,1,0:T(8,128)(2,1)} %shard_map.467.refs_0_.refs_2_), channel_id=1, source_target_pairs={{0,16},{4,20},{8,24},{12,28},{16,0},{20,4},{24,8},{28,12},{1,17},{... | collective-permute-start | bytes 884744 | tf_op jit(solution)/shard_map/ppermute | solution.py:106
  62.5 17.3 %collective-permute-start.7 = (bf16[2,2,1,1,160,384]{5,4,3,2,1,0:T(8,128)(2,1)}, bf16[2,2,1,1,160,384]{5,4,3,2,1,0:T(8,128)(2,1)}, u32[]{:S(2)}, u32[]{:S(2)}) collective-permute-start(bf16[2,2,1,1,160,384]{5,4,3,2,1,0:T(8,128)(2,1)} %shard_map.470.refs_0_.refs_2_), channel_id=1, source_target_pairs={{0,4},{4,0},{8,12},{12,8},{16,20},{20,16},{24,28},{28,24},{1,5},{5... | collective-permute-start | bytes 1474568 | tf_op jit(solution)/shard_map/ppermute | solution.py:106
  70.5 19.2 %collective-permute-start.8 = (bf16[2,2,1,1,192,384]{5,4,3,2,1,0:T(8,128)(2,1)}, bf16[2,2,1,1,192,384]{5,4,3,2,1,0:T(8,128)(2,1)S(1)}, u32[]{:S(2)}, u32[]{:S(2)}) collective-permute-start(bf16[2,2,1,1,192,384]{5,4,3,2,1,0:T(8,128)(2,1)} %shard_map.471.refs_0_.refs_2_), channel_id=1, source_target_pairs={{0,2},{1,3},{2,0},{3,1},{4,6},{5,7},{6,4},{7,5},{8,10},{9,11},{10,... | collective-permute-start | bytes 1769480 | tf_op jit(solution)/shard_map/ppermute | solution.py:106
  82.6 45.1 %collective-permute-start.11 = (bf16[2,2,2,1,160,384]{5,4,3,2,1,0:T(8,128)(2,1)}, bf16[2,2,2,1,160,384]{5,4,3,2,1,0:T(8,128)(2,1)}, u32[]{:S(2)}, u32[]{:S(2)}) collective-permute-start(bf16[2,2,2,1,160,384]{5,4,3,2,1,0:T(8,128)(2,1)} %shard_map.472.refs_0_.refs_2_), channel_id=1, source_target_pairs={{0,2},{1,3},{2,0},{3,1},{4,6},{5,7},{6,4},{7,5},{8,10},{9,11},{10,... | collective-permute-start | bytes 2949128 | tf_op jit(solution)/shard_map/ppermute | solution.py:106
  84.1 25.3 %collective-permute-start.9 = (bf16[1,2,1,1,192,384]{5,4,3,2,1,0:T(8,128)(2,1)S(1)}, bf16[1,2,1,1,192,384]{5,4,3,2,1,0:T(8,128)(2,1)}, u32[]{:S(2)}, u32[]{:S(2)}) collective-permute-start(bf16[1,2,1,1,192,384]{5,4,3,2,1,0:T(8,128)(2,1)S(1)} %copy-done.62), channel_id=1, source_target_pairs={{0,16},{4,20},{8,24},{12,28},{16,0},{20,4},{24,8},{28,12},{1,17},{... | collective-permute-start | bytes 884744 | tf_op jit(solution)/shard_map/ppermute | solution.py:106
  84.1 41.1 %collective-permute-start.10 = (bf16[1,2,1,1,192,384]{5,4,3,2,1,0:T(8,128)(2,1)}, bf16[1,2,1,1,192,384]{5,4,3,2,1,0:T(8,128)(2,1)}, u32[]{:S(2)}, u32[]{:S(2)}) collective-permute-start(bf16[1,2,1,1,192,384]{5,4,3,2,1,0:T(8,128)(2,1)} %shard_map.469.refs_0_.refs_2_), channel_id=1, source_target_pairs={{0,16},{4,20},{8,24},{12,28},{16,0},{20,4},{24,8},{28,12},{1,17},{... | collective-permute-start | bytes 884744 | tf_op jit(solution)/shard_map/ppermute | solution.py:106
  93.3 37.6 %collective-permute-start.12 = (bf16[2,2,1,2,192,384]{5,4,3,2,1,0:T(8,128)(2,1)}, bf16[2,2,1,2,192,384]{5,4,3,2,1,0:T(8,128)(2,1)}, u32[]{:S(2)}, u32[]{:S(2)}) collective-permute-start(bf16[2,2,1,2,192,384]{5,4,3,2,1,0:T(8,128)(2,1)} %shard_map.473.refs_0_.refs_2_), channel_id=1, source_target_pairs={{0,4},{4,0},{8,12},{12,8},{16,20},{20,16},{24,28},{28,24},{1,5},{5... | collective-permute-start | bytes 3538952 | tf_op jit(solution)/shard_map/ppermute | solution.py:106
  130.8 8.0 %collective-permute-start.13 = (bf16[2,2,2,2,160,384]{5,4,3,2,1,0:T(8,128)(2,1)}, bf16[2,2,2,2,160,384]{5,4,3,2,1,0:T(8,128)(2,1)}, u32[]{:S(2)}, u32[]{:S(2)}) collective-permute-start(bf16[2,2,2,2,160,384]{5,4,3,2,1,0:T(8,128)(2,1)} %shard_map.476.refs_0_), channel_id=1, source_target_pairs={{0,1},{1,0},{2,3},{3,2},{4,5},{5,4},{6,7},{7,6},{8,9},{9,8},{10,11... | collective-permute-start | bytes 5898248 | tf_op jit(solution)/shard_map/ppermute | solution.py:106
  134.2 29.8 %collective-permute-start.16 = (bf16[2,2,2,2,192,384]{5,4,3,2,1,0:T(8,128)(2,1)}, bf16[2,2,2,2,192,384]{5,4,3,2,1,0:T(8,128)(2,1)}, u32[]{:S(2)}, u32[]{:S(2)}) collective-permute-start(bf16[2,2,2,2,192,384]{5,4,3,2,1,0:T(8,128)(2,1)} %shard_map.477.refs_0_), channel_id=1, source_target_pairs={{0,1},{1,0},{2,3},{3,2},{4,5},{5,4},{6,7},{7,6},{8,9},{9,8},{10,11... | collective-permute-start | bytes 7077896 | tf_op jit(solution)/shard_map/ppermute | solution.py:106
  136.8 19.6 %collective-permute-start.14 = (bf16[2,2,1,1,192,384]{5,4,3,2,1,0:T(8,128)(2,1)}, bf16[2,2,1,1,192,384]{5,4,3,2,1,0:T(8,128)(2,1)}, u32[]{:S(2)}, u32[]{:S(2)}) collective-permute-start(bf16[2,2,1,1,192,384]{5,4,3,2,1,0:T(8,128)(2,1)} %shard_map.474.refs_0_.refs_2_), channel_id=1, source_target_pairs={{0,4},{4,0},{8,12},{12,8},{16,20},{20,16},{24,28},{28,24},{1,5},{5... | collective-permute-start | bytes 1769480 | tf_op jit(solution)/shard_map/ppermute | solution.py:106
  137.9 21.6 %collective-permute-start.15 = (bf16[2,2,1,1,192,384]{5,4,3,2,1,0:T(8,128)(2,1)S(1)}, bf16[2,2,1,1,192,384]{5,4,3,2,1,0:T(8,128)(2,1)}, u32[]{:S(2)}, u32[]{:S(2)}) collective-permute-start(bf16[2,2,1,1,192,384]{5,4,3,2,1,0:T(8,128)(2,1)S(1)} %copy-done.60), channel_id=1, source_target_pairs={{0,2},{1,3},{2,0},{3,1},{4,6},{5,7},{6,4},{7,5},{8,10},{9,11},{10,... | collective-permute-start | bytes 1769480 | tf_op jit(solution)/shard_map/ppermute | solution.py:106
  159.1 28.1 %collective-permute-start.17 = (bf16[2,2,2,1,192,384]{5,4,3,2,1,0:T(8,128)(2,1)}, bf16[2,2,2,1,192,384]{5,4,3,2,1,0:T(8,128)(2,1)}, u32[]{:S(2)}, u32[]{:S(2)}) collective-permute-start(bf16[2,2,2,1,192,384]{5,4,3,2,1,0:T(8,128)(2,1)} %shard_map.479.refs_0_.refs_2_), channel_id=1, source_target_pairs={{0,2},{1,3},{2,0},{3,1},{4,6},{5,7},{6,4},{7,5},{8,10},{9,11},{10,... | collective-permute-start | bytes 3538952 | tf_op jit(solution)/shard_map/ppermute | solution.py:106
  162.2 28.3 %collective-permute-start.18 = (bf16[2,2,1,2,192,384]{5,4,3,2,1,0:T(8,128)(2,1)}, bf16[2,2,1,2,192,384]{5,4,3,2,1,0:T(8,128)(2,1)}, u32[]{:S(2)}, u32[]{:S(2)}) collective-permute-start(bf16[2,2,1,2,192,384]{5,4,3,2,1,0:T(8,128)(2,1)} %shard_map.480.refs_0_.refs_2_), channel_id=1, source_target_pairs={{0,4},{4,0},{8,12},{12,8},{16,20},{20,16},{24,28},{28,24},{1,5},{5... | collective-permute-start | bytes 3538952 | tf_op jit(solution)/shard_map/ppermute | solution.py:106
  193.8 8.2 %collective-permute-start.19 = (bf16[2,2,2,2,192,384]{5,4,3,2,1,0:T(8,128)(2,1)}, bf16[2,2,2,2,192,384]{5,4,3,2,1,0:T(8,128)(2,1)}, u32[]{:S(2)}, u32[]{:S(2)}) collective-permute-start(bf16[2,2,2,2,192,384]{5,4,3,2,1,0:T(8,128)(2,1)} %shard_map.482.refs_0_), channel_id=1, source_target_pairs={{0,1},{1,0},{2,3},{3,2},{4,5},{5,4},{6,7},{7,6},{8,9},{9,8},{10,11... | collective-permute-start | bytes 7077896 | tf_op jit(solution)/shard_map/ppermute | solution.py:106
  298.5 20.9 %collective-permute-start.21 = (bf16[16,192,384]{2,1,0:T(8,128)(2,1)}, bf16[16,192,384]{2,1,0:T(8,128)(2,1)}, u32[]{:S(2)}, u32[]{:S(2)}) collective-permute-start(bf16[16,192,384]{2,1,0:T(8,128)(2,1)} %dynamic-slice_bitcast_fusion.3), channel_id=1, source_target_pairs={{0,1},{1,0},{2,3},{3,2},{4,5},{5,4},{6,7},{7,6},{8,9},{9,8},{10,11... | collective-permute-start | bytes 7077896 | tf_op jit(solution)/shard_map/ppermute | solution.py:106
  322.7 41.3 %collective-permute-start.22 = (bf16[2,2,2,1,192,384]{5,4,3,2,1,0:T(8,128)(2,1)}, bf16[2,2,2,1,192,384]{5,4,3,2,1,0:T(8,128)(2,1)}, u32[]{:S(2)}, u32[]{:S(2)}) collective-permute-start(bf16[2,2,2,1,192,384]{5,4,3,2,1,0:T(8,128)(2,1)} %shard_map.492.refs_0_), channel_id=1, source_target_pairs={{0,2},{1,3},{2,0},{3,1},{4,6},{5,7},{6,4},{7,5},{8,10},{9,11},{10,... | collective-permute-start | bytes 3538952 | tf_op jit(solution)/shard_map/ppermute | solution.py:106
  327.5 39.5 %collective-permute-start.23 = (bf16[16,192,384]{2,1,0:T(8,128)(2,1)}, bf16[16,192,384]{2,1,0:T(8,128)(2,1)}, u32[]{:S(2)}, u32[]{:S(2)}) collective-permute-start(bf16[16,192,384]{2,1,0:T(8,128)(2,1)} %dynamic-slice_bitcast_fusion.2), channel_id=1, source_target_pairs={{0,1},{1,0},{2,3},{3,2},{4,5},{5,4},{6,7},{7,6},{8,9},{9,8},{10,11... | collective-permute-start | bytes 7077896 | tf_op jit(solution)/shard_map/ppermute | solution.py:106
  329.8 44.3 %collective-permute-start.24 = (bf16[16,192,384]{2,1,0:T(8,128)(2,1)}, bf16[16,192,384]{2,1,0:T(8,128)(2,1)}, u32[]{:S(2)}, u32[]{:S(2)}) collective-permute-start(bf16[16,192,384]{2,1,0:T(8,128)(2,1)} %dynamic-slice_bitcast_fusion.1), channel_id=1, source_target_pairs={{0,1},{1,0},{2,3},{3,2},{4,5},{5,4},{6,7},{7,6},{8,9},{9,8},{10,11... | collective-permute-start | bytes 7077896 | tf_op jit(solution)/shard_map/ppermute | solution.py:106
  356.7 21.5 %collective-permute-start.25 = (bf16[16,192,384]{2,1,0:T(8,128)(2,1)}, bf16[16,192,384]{2,1,0:T(8,128)(2,1)}, u32[]{:S(2)}, u32[]{:S(2)}) collective-permute-start(bf16[16,192,384]{2,1,0:T(8,128)(2,1)} %dynamic-slice_bitcast_fusion), channel_id=1, source_target_pairs={{0,1},{1,0},{2,3},{3,2},{4,5},{5,4},{6,7},{7,6},{8,9},{9,8},{10,11... | collective-permute-start | bytes 7077896 | tf_op jit(solution)/shard_map/ppermute | solution.py:106
  370.5 37.6 %collective-permute-start.26 = (bf16[2,2,1,2,192,384]{5,4,3,2,1,0:T(8,128)(2,1)}, bf16[2,2,1,2,192,384]{5,4,3,2,1,0:T(8,128)(2,1)}, u32[]{:S(2)}, u32[]{:S(2)}) collective-permute-start(bf16[2,2,1,2,192,384]{5,4,3,2,1,0:T(8,128)(2,1)} %shard_map.495.refs_1_), channel_id=1, source_target_pairs={{0,4},{4,0},{8,12},{12,8},{16,20},{20,16},{24,28},{28,24},{1,5},{5... | collective-permute-start | bytes 3538952 | tf_op jit(solution)/shard_map/ppermute | solution.py:106
  373.7 49.0 %collective-permute-start.29 = (bf16[2,2,1,1,192,384]{5,4,3,2,1,0:T(8,128)(2,1)}, bf16[2,2,1,1,192,384]{5,4,3,2,1,0:T(8,128)(2,1)S(1)}, u32[]{:S(2)}, u32[]{:S(2)}) collective-permute-start(bf16[2,2,1,1,192,384]{5,4,3,2,1,0:T(8,128)(2,1)} %shard_map.494.refs_1_), channel_id=1, source_target_pairs={{0,4},{4,0},{8,12},{12,8},{16,20},{20,16},{24,28},{28,24},{1,5},{5... | collective-permute-start | bytes 1769480 | tf_op jit(solution)/shard_map/ppermute | solution.py:106
  377.4 33.7 %collective-permute-start.27 = (bf16[2,2,2,1,192,384]{5,4,3,2,1,0:T(8,128)(2,1)}, bf16[2,2,2,1,192,384]{5,4,3,2,1,0:T(8,128)(2,1)}, u32[]{:S(2)}, u32[]{:S(2)}) collective-permute-start(bf16[2,2,2,1,192,384]{5,4,3,2,1,0:T(8,128)(2,1)} %shard_map.496.refs_1_), channel_id=1, source_target_pairs={{0,2},{1,3},{2,0},{3,1},{4,6},{5,7},{6,4},{7,5},{8,10},{9,11},{10,... | collective-permute-start | bytes 3538952 | tf_op jit(solution)/shard_map/ppermute | solution.py:106
  381.5 66.7 %collective-permute-start.30 = (bf16[2,2,1,2,192,384]{5,4,3,2,1,0:T(8,128)(2,1)}, bf16[2,2,1,2,192,384]{5,4,3,2,1,0:T(8,128)(2,1)}, u32[]{:S(2)}, u32[]{:S(2)}) collective-permute-start(bf16[2,2,1,2,192,384]{5,4,3,2,1,0:T(8,128)(2,1)} %shard_map.497.refs_0_), channel_id=1, source_target_pairs={{0,4},{4,0},{8,12},{12,8},{16,20},{20,16},{24,28},{28,24},{1,5},{5... | collective-permute-start | bytes 3538952 | tf_op jit(solution)/shard_map/ppermute | solution.py:106
  401.2 12.8 %collective-permute-start.28 = (bf16[16,160,384]{2,1,0:T(8,128)(2,1)}, bf16[16,160,384]{2,1,0:T(8,128)(2,1)}, u32[]{:S(2)}, u32[]{:S(2)}) collective-permute-start(bf16[16,160,384]{2,1,0:T(8,128)(2,1)} %dynamic-slice_bitcast_fusion.4), channel_id=1, source_target_pairs={{0,1},{1,0},{2,3},{3,2},{4,5},{5,4},{6,7},{7,6},{8,9},{9,8},{10,11... | collective-permute-start | bytes 5898248 | tf_op jit(solution)/shard_map/ppermute | solution.py:106
  417.1 34.9 %collective-permute-start.31 = (bf16[2,2,2,1,160,384]{5,4,3,2,1,0:T(8,128)(2,1)}, bf16[2,2,2,1,160,384]{5,4,3,2,1,0:T(8,128)(2,1)}, u32[]{:S(2)}, u32[]{:S(2)}) collective-permute-start(bf16[2,2,2,1,160,384]{5,4,3,2,1,0:T(8,128)(2,1)} %shard_map.501.refs_1_), channel_id=1, source_target_pairs={{0,2},{1,3},{2,0},{3,1},{4,6},{5,7},{6,4},{7,5},{8,10},{9,11},{10,... | collective-permute-start | bytes 2949128 | tf_op jit(solution)/shard_map/ppermute | solution.py:106
  418.2 38.4 %collective-permute-start.32 = (bf16[2,2,1,1,192,384]{5,4,3,2,1,0:T(8,128)(2,1)}, bf16[2,2,1,1,192,384]{5,4,3,2,1,0:T(8,128)(2,1)}, u32[]{:S(2)}, u32[]{:S(2)}) collective-permute-start(bf16[2,2,1,1,192,384]{5,4,3,2,1,0:T(8,128)(2,1)} %shard_map.499.refs_1_), channel_id=1, source_target_pairs={{0,2},{1,3},{2,0},{3,1},{4,6},{5,7},{6,4},{7,5},{8,10},{9,11},{10,... | collective-permute-start | bytes 1769480 | tf_op jit(solution)/shard_map/ppermute | solution.py:106
  419.2 44.1 %collective-permute-start.33 = (bf16[2,2,1,1,192,384]{5,4,3,2,1,0:T(8,128)(2,1)}, bf16[2,2,1,1,192,384]{5,4,3,2,1,0:T(8,128)(2,1)}, u32[]{:S(2)}, u32[]{:S(2)}) collective-permute-start(bf16[2,2,1,1,192,384]{5,4,3,2,1,0:T(8,128)(2,1)} %shard_map.500.refs_1_), channel_id=1, source_target_pairs={{0,4},{4,0},{8,12},{12,8},{16,20},{20,16},{24,28},{28,24},{1,5},{5... | collective-permute-start | bytes 1769480 | tf_op jit(solution)/shard_map/ppermute | solution.py:106
  426.4 43.2 %collective-permute-start.34 = (bf16[1,2,1,1,192,384]{5,4,3,2,1,0:T(8,128)(2,1)}, bf16[1,2,1,1,192,384]{5,4,3,2,1,0:T(8,128)(2,1)}, u32[]{:S(2)}, u32[]{:S(2)}) collective-permute-start(bf16[1,2,1,1,192,384]{5,4,3,2,1,0:T(8,128)(2,1)} %shard_map.502.refs_1_), channel_id=1, source_target_pairs={{0,16},{4,20},{8,24},{12,28},{16,0},{20,4},{24,8},{28,12},{1,17},{... | collective-permute-start | bytes 884744 | tf_op jit(solution)/shard_map/ppermute | solution.py:106
  451.1 32.5 %collective-permute-start.36 = (bf16[2,2,1,1,192,384]{5,4,3,2,1,0:T(8,128)(2,1)}, bf16[2,2,1,1,192,384]{5,4,3,2,1,0:T(8,128)(2,1)S(1)}, u32[]{:S(2)}, u32[]{:S(2)}) collective-permute-start(bf16[2,2,1,1,192,384]{5,4,3,2,1,0:T(8,128)(2,1)} %shard_map.503.refs_1_), channel_id=1, source_target_pairs={{0,2},{1,3},{2,0},{3,1},{4,6},{5,7},{6,4},{7,5},{8,10},{9,11},{10,... | collective-permute-start | bytes 1769480 | tf_op jit(solution)/shard_map/ppermute | solution.py:106
  455.0 34.6 %collective-permute-start.37 = (bf16[2,2,1,1,160,384]{5,4,3,2,1,0:T(8,128)(2,1)}, bf16[2,2,1,1,160,384]{5,4,3,2,1,0:T(8,128)(2,1)}, u32[]{:S(2)}, u32[]{:S(2)}) collective-permute-start(bf16[2,2,1,1,160,384]{5,4,3,2,1,0:T(8,128)(2,1)} %shard_map.504.refs_1_), channel_id=1, source_target_pairs={{0,4},{4,0},{8,12},{12,8},{16,20},{20,16},{24,28},{28,24},{1,5},{5... | collective-permute-start | bytes 1474568 | tf_op jit(solution)/shard_map/ppermute | solution.py:106
  459.4 21.6 %collective-permute-start.35 = (bf16[1,2,1,1,192,384]{5,4,3,2,1,0:T(8,128)(2,1)}, bf16[1,2,1,1,192,384]{5,4,3,2,1,0:T(8,128)(2,1)}, u32[]{:S(2)}, u32[]{:S(2)}) collective-permute-start(bf16[1,2,1,1,192,384]{5,4,3,2,1,0:T(8,128)(2,1)} %shard_map.505.refs_1_), channel_id=1, source_target_pairs={{0,16},{4,20},{8,24},{12,28},{16,0},{20,4},{24,8},{28,12},{1,17},{... | collective-permute-start | bytes 884744 | tf_op jit(solution)/shard_map/ppermute | solution.py:106
  466.3 26.5 %collective-permute-start.38 = (bf16[1,2,1,1,192,384]{5,4,3,2,1,0:T(8,128)(2,1)}, bf16[1,2,1,1,192,384]{5,4,3,2,1,0:T(8,128)(2,1)}, u32[]{:S(2)}, u32[]{:S(2)}) collective-permute-start(bf16[1,2,1,1,192,384]{5,4,3,2,1,0:T(8,128)(2,1)} %shard_map.506.refs_1_), channel_id=1, source_target_pairs={{0,16},{4,20},{8,24},{12,28},{16,0},{20,4},{24,8},{28,12},{1,17},{... | collective-permute-start | bytes 884744 | tf_op jit(solution)/shard_map/ppermute | solution.py:106
  472.4 25.1 %collective-permute-start.39 = (bf16[1,1,1,1,192,384]{5,4,3,2,1,0:T(8,128)(2,1)}, bf16[1,1,1,1,192,384]{5,4,3,2,1,0:T(8,128)(2,1)}, u32[]{:S(2)}, u32[]{:S(2)}) collective-permute-start(bf16[1,1,1,1,192,384]{5,4,3,2,1,0:T(8,128)(2,1)} %shard_map.507.refs_1_), channel_id=1, source_target_pairs={{0,8},{4,12},{8,0},{12,4},{16,24},{20,28},{24,16},{28,20},{1,9},{5... | collective-permute-start | bytes 442376 | tf_op jit(solution)/shard_map/ppermute | solution.py:106
  483.6 22.1 %collective-permute-start.40 = (bf16[1,1,1,1,192,384]{5,4,3,2,1,0:T(8,128)(2,1)}, bf16[1,1,1,1,192,384]{5,4,3,2,1,0:T(8,128)(2,1)S(1)}, u32[]{:S(2)}, u32[]{:S(2)}) collective-permute-start(bf16[1,1,1,1,192,384]{5,4,3,2,1,0:T(8,128)(2,1)} %shard_map.508.refs_1_), channel_id=1, source_target_pairs={{0,8},{4,12},{8,0},{12,4},{16,24},{20,28},{24,16},{28,20},{1,9},{5... | collective-permute-start | bytes 442376 | tf_op jit(solution)/shard_map/ppermute | solution.py:106
  487.2 33.4 %collective-permute-start.43 = (bf16[1,2,1,1,192,384]{5,4,3,2,1,0:T(8,128)(2,1)}, bf16[1,2,1,1,192,384]{5,4,3,2,1,0:T(8,128)(2,1)S(1)}, u32[]{:S(2)}, u32[]{:S(2)}) collective-permute-start(bf16[1,2,1,1,192,384]{5,4,3,2,1,0:T(8,128)(2,1)} %shard_map.509.refs_1_), channel_id=1, source_target_pairs={{0,16},{4,20},{8,24},{12,28},{16,0},{20,4},{24,8},{28,12},{1,17},{... | collective-permute-start | bytes 884744 | tf_op jit(solution)/shard_map/ppermute | solution.py:106
  492.2 22.5 %collective-permute-start.41 = (bf16[1,2,1,1,160,384]{5,4,3,2,1,0:T(8,128)(2,1)}, bf16[1,2,1,1,160,384]{5,4,3,2,1,0:T(8,128)(2,1)}, u32[]{:S(2)}, u32[]{:S(2)}) collective-permute-start(bf16[1,2,1,1,160,384]{5,4,3,2,1,0:T(8,128)(2,1)} %shard_map.510.refs_1_), channel_id=1, source_target_pairs={{0,16},{4,20},{8,24},{12,28},{16,0},{20,4},{24,8},{28,12},{1,17},{... | collective-permute-start | bytes 737288 | tf_op jit(solution)/shard_map/ppermute | solution.py:106
  495.5 21.8 %collective-permute-start.42 = (bf16[1,1,1,1,192,384]{5,4,3,2,1,0:T(8,128)(2,1)}, bf16[1,1,1,1,192,384]{5,4,3,2,1,0:T(8,128)(2,1)S(1)}, u32[]{:S(2)}, u32[]{:S(2)}) collective-permute-start(bf16[1,1,1,1,192,384]{5,4,3,2,1,0:T(8,128)(2,1)} %shard_map.511.refs_1_), channel_id=1, source_target_pairs={{0,8},{4,12},{8,0},{12,4},{16,24},{20,28},{24,16},{28,20},{1,9},{5... | collective-permute-start | bytes 442376 | tf_op jit(solution)/shard_map/ppermute | solution.py:106
  504.0 59.5 %collective-permute-start.54 = (f32[288,384]{1,0:T(8,128)}, f32[288,384]{1,0:T(8,128)}, u32[]{:S(2)}, u32[]{:S(2)}) collective-permute-start(f32[288,384]{1,0:T(8,128)} %get-tuple-element.182), channel_id=1, source_target_pairs={{0,1},{1,0},{2,3},{3,2},{4,5},{5,4},{6,7},{7,6},{8,9},{9,8},{10,11... | collective-permute-start | bytes 1327112 | tf_op jit(solution)/shard_map/ppermute | solution.py:106
  517.3 11.5 %collective-permute-start.44 = (bf16[1,1,1,1,160,384]{5,4,3,2,1,0:T(8,128)(2,1)}, bf16[1,1,1,1,160,384]{5,4,3,2,1,0:T(8,128)(2,1)S(1)}, u32[]{:S(2)}, u32[]{:S(2)}) collective-permute-start(bf16[1,1,1,1,160,384]{5,4,3,2,1,0:T(8,128)(2,1)} %shard_map.514.refs_1_), channel_id=1, source_target_pairs={{0,8},{4,12},{8,0},{12,4},{16,24},{20,28},{24,16},{28,20},{1,9},{5... | collective-permute-start | bytes 368648 | tf_op jit(solution)/shard_map/ppermute | solution.py:106
  524.7 11.5 %collective-permute-start.45 = (bf16[1,1,1,1,192,384]{5,4,3,2,1,0:T(8,128)(2,1)}, bf16[1,1,1,1,192,384]{5,4,3,2,1,0:T(8,128)(2,1)S(1)}, u32[]{:S(2)}, u32[]{:S(2)}) collective-permute-start(bf16[1,1,1,1,192,384]{5,4,3,2,1,0:T(8,128)(2,1)} %shard_map.516.refs_1_), channel_id=1, source_target_pairs={{0,8},{4,12},{8,0},{12,4},{16,24},{20,28},{24,16},{28,20},{1,9},{5... | collective-permute-start | bytes 442376 | tf_op jit(solution)/shard_map/ppermute | solution.py:106
  557.1 9.7 %collective-permute-start.53 = (f32[360,384]{1,0:T(8,128)}, f32[360,384]{1,0:T(8,128)}, u32[]{:S(2)}, u32[]{:S(2)}) collective-permute-start(f32[360,384]{1,0:T(8,128)} %get-tuple-element.184), channel_id=1, source_target_pairs={{0,1},{1,0},{2,3},{3,2},{4,5},{5,4},{6,7},{7,6},{8,9},{9,8},{10,11... | collective-permute-start | bytes 1658888 | tf_op jit(solution)/shard_map/ppermute | solution.py:106
  (77 other events, 472.4 us)
Sparse Core Ops, SparseCore 0:
  14.5 152.4 all-gather.2
  271.8 160.7 reduce-scatter.1

commit v4 on v3

--- a/solution.py
+++ b/solution.py
@@ -79,10 +79,10 @@
     + ("forward0", "attention1", "forward1", "head")
 )
 BACKWARD_ORDER = (
-    ("forward1", "attention1", "forward0", "b", "attention0", "b", "u", "d", "a", "embed", "u", "d", "t")
+    ("forward1", "attention1", "forward0", "b", "attention0", "u", "d", "b", "a", "embed", "u", "d", "t")
     + ("b", "a", "t", "u", "d", "b", "u", "a", "t", "d", "b", "u", "t", "d", "a", "t", "a")
 )
-LONG = {5: 14, 10: 14, 11: 14}
+LONG = {7: 14, 10: 14, 11: 14}
 SETTLED = 15
 LAST = (("c", "b"), ("u", "d", "t", "a"))
 
@@ -404,15 +404,42 @@
     upstream[...] = norm_back(grad_normed, scaled, spread, final[0:1])
 
 
-def leave(source, target, half, at, sem):
-    return pltpu.make_async_copy(source, target.at[:, half, pl.ds(at, 48), :], sem)
-
-
-def forward_back_kernel(ats, outs, carried, core, upstream, middle, vector, hidden, *refs):
+class Leaving:
+    def __init__(self, own, half, source, target, chips, rows, sem, which=None):
+        self.branch = None
+        if len(target) == 1:
+            self.copies = [pltpu.make_async_copy(source, target[0].at[chips, half, rows, :], sem)]
+        elif which is not None:
+            self.copies = [pltpu.make_async_copy(source, target[which].at[chips, rows, :], sem)]
+        else:
+            self.copies = [pltpu.make_async_copy(source, part.at[chips, rows, :], sem) for part in target]
+            self.branch = own, half
+
+    def start(self):
+        if self.branch is None:
+            self.copies[0].start()
+            return
+        own, half = self.branch
+        pl.when(half == own)(self.copies[0].start)
+        pl.when(half != own)(self.copies[1].start)
+
+    def wait(self):
+        self.copies[0].wait()
+
+
+def split_targets(refs, sizes):
+    targets, start = [], 0
+    for size in sizes:
+        targets.append(refs[start : start + size])
+        start += size
+    return targets
+
+
+def forward_back_kernel(ats, outs, sizes, carried, core, upstream, middle, vector, hidden, *refs):
     pairs = [refs[0:2], refs[2:4], refs[4:6]]
     refs = refs[6 + carried :]
     grad_middle, vector_grad = refs[0:2]
-    targets = refs[2:-11]
+    targets = split_targets(refs[2:-11], sizes)
     w_up, w_down, normed_t, branch, hidden_tile, down_stage, up_stage, acc = refs[-11:-3]
     sems, hidden_sems, out_sems = refs[-3:]
     own = core[0]
@@ -463,17 +490,17 @@
             down_stage[slot, half] = grad_down[:, half * UNIT : half * UNIT + UNIT].reshape(4, 192, UNIT)
         flight = []
         for half in range(2):
-            place = targets[outs[0][0]].at[pl.ds(4 * tile, 4), half, pl.ds(outs[0][1], 192), :]
-            source = down_stage.at[slot, half]
-            flight.append(pltpu.make_async_copy(source, place, out_sems.at[slot, half]))
+            rows, target = pl.ds(outs[0][1], 192), targets[outs[0][0]]
+            source, sem = down_stage.at[slot, half], out_sems.at[slot, half]
+            flight.append(Leaving(own, half, source, target, pl.ds(4 * tile, 4), rows, sem))
         grad_up = dot(normed_t[...], grad_hidden).astype(low)
         for unit in range(2):
             up_stage[slot, unit] = grad_up[:, unit * UNIT : unit * UNIT + UNIT].reshape(16, 48, UNIT)
         half = own if step < 2 else 1 - own
         for unit in range(2):
-            source = up_stage.at[slot, unit]
-            at = outs[1 + slot][1] + 48 * unit
-            flight.append(leave(source, targets[outs[1 + slot][0]], half, at, out_sems.at[slot, 2 + unit]))
+            rows, target = pl.ds(outs[1 + slot][1] + 48 * unit, 48), targets[outs[1 + slot][0]]
+            source, sem = up_stage.at[slot, unit], out_sems.at[slot, 2 + unit]
+            flight.append(Leaving(own, half, source, target, every, rows, sem, step // 2))
         for copy in flight:
             copy.start()
         flights.append(flight)
@@ -488,12 +515,12 @@
 
 
 def attention_back_kernel(
-    ats, outs, carried, core, grad_middle, stream, vector, triple, lse, mixed, *refs
+    ats, outs, sizes, carried, core, grad_middle, stream, vector, triple, lse, mixed, *refs
 ):
     in_pair, out_pair = refs[0:2], refs[2:4]
     refs = refs[4 + carried :]
     upstream, vector_grad = refs[0:2]
-    targets = refs[2:-7]
+    targets = split_targets(refs[2:-7], sizes)
     w_in, w_out, grad_mixed, grad_triple, stage, sems, out_sems = refs[-7:]
     target, at = targets[outs[0][0]], outs[0][1]
     out_target, out_at = targets[outs[1][0]], outs[1][1]
@@ -511,7 +538,7 @@
     for half in range(2):
         stage[3, half] = grad_out[:, half * UNIT : half * UNIT + UNIT].reshape(16, 48, UNIT)
         source = stage.at[3, half]
-        leaving.append(leave(source, out_target, half, out_at, out_sems.at[6 + half]))
+        leaving.append(Leaving(own, half, source, out_target, every, pl.ds(out_at, 48), out_sems.at[6 + half]))
         leaving[-1].start()
     for copy in out_copies:
         copy.wait()
@@ -561,7 +588,8 @@
             unit = 2 * part + side_unit
             stage[part, side_unit] = grad_in[:, side_unit * UNIT : side_unit * UNIT + UNIT].reshape(16, 48, UNIT)
             source = stage.at[part, side_unit]
-            leaving.append(leave(source, target, unit // 3, at + 48 * (unit % 3), out_sems.at[unit]))
+            rows = pl.ds(at + 48 * (unit % 3), 48)
+            leaving.append(Leaving(own, unit // 3, source, target, every, rows, out_sems.at[unit]))
             leaving[-1].start()
         grad_normed += dot_right(block, flat(w_in[:, :, part * D : (part + 1) * D]))
     vector_grad[0:1] = rows_sum(grad_normed * scaled)
@@ -571,10 +599,16 @@
         copy.wait()
 
 
-def embed_back_kernel(at, carried, upstream, ids, chosen, grad_logits, small, *refs):
-    target, stage, sems = refs[carried:]
-    leaving = [pltpu.make_async_copy(small, target.at[:, :, pl.ds(at + 144, 16), :], sems.at[6])]
-    leaving[0].start()
+def embed_back_kernel(at, size, carried, core, upstream, ids, chosen, grad_logits, small, *refs):
+    target = refs[carried:-2]
+    stage, sems = refs[-2:]
+    own, every = core[0], slice(None)
+    leaving = []
+    for which in range(2):
+        half = own if which == 0 else 1 - own
+        rows, sem = pl.ds(at + 144, 16), sems.at[6 + which]
+        leaving.append(Leaving(own, half, small.at[:, half], target, every, rows, sem, which))
+        leaving[-1].start()
     stream_t = upstream[...].astype(low).T
     chosen_t = chosen[...].T
     for tile in range(3):
@@ -586,7 +620,8 @@
             part = block[:, side_unit * UNIT : side_unit * UNIT + UNIT].astype(low)
             stage[tile, side_unit] = part.reshape(16, 48, UNIT)
             source = stage.at[tile, side_unit]
-            leaving.append(leave(source, target, unit // 3, at + 48 * (unit % 3), sems.at[unit]))
+            rows = pl.ds(at + 48 * (unit % 3), 48)
+            leaving.append(Leaving(own, unit // 3, source, target, every, rows, sems.at[unit]))
             leaving[-1].start()
     for copy in leaving:
         copy.wait()
@@ -711,20 +746,26 @@
 
     def results(self, pieces, before, first):
         names = sorted({self.places[piece][0] for piece in pieces})
-        operands, shapes, aliases = [], [], {}
+        operands, shapes, aliases, sizes = [], [], {}, []
         for name in names:
-            if name in self.arrays:
-                aliases[before + len(operands)] = first + len(shapes)
-                operands.append(self.arrays[name])
-            shapes.append(shape_of(16, 2, height(SCATTER[name]), UNIT, kind=low))
+            middle = [] if name in SCATTER_WAY else [2]
+            sizes.append(2 if name in SCATTER_WAY else 1)
+            for which in range(sizes[-1]):
+                if name in self.arrays:
+                    aliases[before + len(operands)] = first + len(shapes)
+                    operands.append(self.arrays[name][which])
+                shapes.append(shape_of(16, *middle, height(SCATTER[name]), UNIT, kind=low))
         spots = tuple((names.index(self.places[piece][0]), self.places[piece][1]) for piece in pieces)
-        return names, operands, shapes, aliases, spots
+        return names, operands, shapes, aliases, (spots, tuple(sizes))
+
+    def take(self, names, sizes, results):
+        self.arrays.update(zip(names, split_targets(results, sizes)))
 
 
 def feed_forward_back(line, grads, layer, core, upstream, middle, vector, hidden, pairs, ats):
     names, more, shapes, aliases, spots = grads.results((f"D{layer}", f"E{layer}", f"F{layer}"), 11, 2)
     results = line.call(
-        partial(forward_back_kernel, ats, spots, len(more)),
+        partial(forward_back_kernel, ats, *spots, len(more)),
         (core, upstream, middle, vector, hidden, *pairs[0], *pairs[1], *pairs[2], *more),
         [SMEM, VMEM, VMEM, VMEM] + [ANY] * (7 + len(more)),
         (shape_of(TOKENS, D), shape_of(12, D), *shapes),
@@ -745,14 +786,14 @@
         aliases=aliases,
         cost=1,
     )
-    grads.arrays.update(zip(names, results[2:]))
+    grads.take(names, spots[1], results[2:])
     return results[:2]
 
 
 def attention_back(line, grads, layer, core, grad_middle, stream, vector, triple, lse, mixed, pairs, ats):
     names, more, shapes, aliases, spots = grads.results((f"Q{layer}", f"O{layer}"), 11, 2)
     results = line.call(
-        partial(attention_back_kernel, ats, spots, len(more)),
+        partial(attention_back_kernel, ats, *spots, len(more)),
         (core, grad_middle, stream, vector, triple, lse, mixed, *pairs[0], *pairs[1], *more),
         [SMEM] + [VMEM] * 6 + [ANY] * (4 + len(more)),
         (shape_of(TOKENS, D), shape_of(12, D), *shapes),
@@ -769,23 +810,23 @@
         aliases=aliases,
         cost=1,
     )
-    grads.arrays.update(zip(names, results[2:]))
+    grads.take(names, spots[1], results[2:])
     return results[:2]
 
 
-def embed_back(line, grads, upstream, ids, chosen, grad_logits, small):
-    names, more, shapes, aliases, spots = grads.results(("T",), 5, 0)
+def embed_back(line, grads, core, upstream, ids, chosen, grad_logits, small):
+    names, more, shapes, aliases, spots = grads.results(("T",), 6, 0)
     results = line.call(
-        partial(embed_back_kernel, spots[0][1], len(more)),
-        (upstream, ids, chosen, grad_logits, small, *more),
-        [VMEM] * 4 + [ANY] * (1 + len(more)),
+        partial(embed_back_kernel, spots[0][0][1], spots[1][0], len(more)),
+        (core, upstream, ids, chosen, grad_logits, small, *more),
+        [SMEM] + [VMEM] * 4 + [ANY] * (1 + len(more)),
         tuple(shapes),
         (ANY,) * len(shapes),
         [pltpu.VMEM((3, 2, 16, 48, UNIT), low), DMA((8,))],
         aliases=aliases,
         cost=1,
     )
-    grads.arrays.update(zip(names, results))
+    grads.take(names, spots[1], results)
 
 
 def pass_on(line, array):
@@ -846,11 +887,9 @@
                     place.append(0)
                 else:
                     place.append(1 - bits_ref[i] if i == axis else bits_ref[i])
-            if len(shape) == 7:
-                place.append(bits_ref[4])
             return (*place, 0, 0)
 
-        return pl.BlockSpec((*block, *(None,) * (len(shape) - 6), rows, UNIT), index)
+        return pl.BlockSpec((*block, rows, UNIT), index)
 
     def kernel(bits_ref, *refs):
         total = refs[0][...].astype(full)
@@ -1021,11 +1060,10 @@
         for name in names:
             grad = grads.arrays[name]
             if name in SCATTER_WAY:
-                shape = (2, 2, 2, 2) + grad.shape[1:]
-                arrived = swap(pick(grad, 1 - core, 1)[:, 0], "core")
-                parts[name], gone[name] = [grad.reshape(shape), arrived.reshape(shape[:4] + shape[5:])], []
+                shape = (2, 2, 2, 2) + grad[0].shape[1:]
+                parts[name], gone[name] = [grad[0].reshape(shape), swap(grad[1], "core").reshape(shape)], []
             else:
-                grad = grad.reshape(32, -1, UNIT)
+                grad = grad[0].reshape(32, -1, UNIT)
                 total = lax.psum_scatter(grad, BOTH, scatter_dimension=0, tiled=False)
                 parts[name], totals[name] = None, total.astype(full)
                 return total
@@ -1055,7 +1093,7 @@
             gone[step].append(axis)
         elif step == "embed":
             small_grads, block = small_blocks()
-            embed_back(line, grads, upstream, ids, chosen, grad_logits, block)
+            embed_back(line, grads, own, upstream, ids, chosen, grad_logits, block)
             finished(("T",))
         elif step[:-1] == "attention":
             l = int(step[-1])
@@ -1108,7 +1146,9 @@
         small_sum = jnp.concatenate(small_sum)
         for piece, (name, start) in grads.places.items():
             size = 144 if piece == "T" else PIECES[piece][0]
-            shares[piece] = grads.arrays[name][:, :, start : start + size].transpose(1, 0, 2, 3)
+            grad = grads.arrays[name]
+            grad = jnp.stack(grad) if name in SCATTER_WAY else grad[0].transpose(1, 0, 2, 3)
+            shares[piece] = grad[:, :, start : start + size]
         for l in range(L):
             shares[f"U{l}"] = jnp.concatenate([shares[f"E{l}"], shares[f"F{l}"]], 2)
         for piece, block in shares.items():

time: 596 us -> 581 us (0.975)
  local copies, waits for them, and re-layouts: 59.3 us -> 38.2 us
  waiting for transfers between devices: 126 us -> 141 us
    squeeze x5 -> x0, local copies, waits for them, and re-layouts: 15.2 us -> none  [ready(): arrived = swap(pick(grad, 1 - core, 1)[:, 0], 'core')]
    ppermute x54, waiting for transfers between devices: 123 us -> 134 us  [swap(): return lax.ppermute(tensor, axis, [(i, i ^ flip) for i in range(size)])]
    unnamed x164 -> x152, local copies, waits for them, and re-layouts: 19.1 us -> 15.7 us
  transfers between devices with their start and end apart: 57 -> 57, of which waited for: 21 -> 24; matrix products, arithmetic and copies ran while one was open for 10% -> 7% of each run, Pallas kernels for 39% -> 40%
where the time goes in v4:
time: 581 us; the launch traced here: 572 us
  Pallas kernels  289 us (50%)
  waiting for transfers between devices  141 us (24%)
  starting transfers between devices  59.2 us (10%)
  local copies, waits for them, and re-layouts  38.2 us (7%)
  between operations  22.9 us (4%)
  other arithmetic  22.5 us (4%)
    pallas_call x53, Pallas kernels, call(): pl.pallas_call(ordered, out_shape=outs, compiler_params=pltpu.CompilerPar...  289 us
    ppermute x54, waiting for transfers between devices, swap(): return lax.ppermute(tensor, axis, [(i, i ^ flip) for i in range(size)])  134 us
    ppermute x54, starting transfers between devices, swap(): return lax.ppermute(tensor, axis, [(i, i ^ flip) for i in range(size)])  56.9 us
    unnamed x152, local copies, waits for them, and re-layouts  15.7 us
  transfers between devices with their start and end apart: 57, of which 24 were waited for; matrix products, arithmetic and copies ran while one was open for 7% of the time, Pallas kernels for 40%

profile of v4, /device:TPU:0, one launch (start us, length us, event | category | flops | bytes accessed | tf_op | source)
XLA Modules:
  0.0 572.1 jit_solution(8341022579695995241)
XLA Ops:
  15.3 3.0 collective-permute-start.4
  21.5 8.5 %collective-permute-done.1.refs_3_ = bf16[1,1,1,1,160,384]{5,4,3,2,1,0:T(8,128)(2,1)S(1)} collective-permute-done((bf16[1,1,1,1,160,384]{5,4,3,2,1,0:T(8,128)(2,1)S(1)}, bf16[1,1,1,1,160,384]{5,4,3,2,1,0:T(8,128)(2,1)S(1)}, u32[]{:S(2)}, u32[]{:S(2)}) %collective-permute-start.1) | collective-permute-done | bytes 122912 | tf_op jit(solution)/shard_map/ppermute | solution.py:106
  33.0 3.9 collective-permute-start.5
  40.6 3.2 collective-permute-start.6
  48.5 10.5 %collective-permute-done.5.refs_3_ = bf16[1,2,1,1,160,384]{5,4,3,2,1,0:T(8,128)(2,1)S(1)} collective-permute-done((bf16[1,2,1,1,160,384]{5,4,3,2,1,0:T(8,128)(2,1)}, bf16[1,2,1,1,160,384]{5,4,3,2,1,0:T(8,128)(2,1)S(1)}, u32[]{:S(2)}, u32[]{:S(2)}) %collective-permute-start.5) | collective-permute-done | bytes 245792 | tf_op jit(solution)/shard_map/ppermute | solution.py:106
  64.0 3.1 collective-permute-done.6.refs_3_
  71.8 7.8 %collective-permute-done.7.refs_3_ = bf16[2,2,1,1,160,384]{5,4,3,2,1,0:T(8,128)(2,1)} collective-permute-done((bf16[2,2,1,1,160,384]{5,4,3,2,1,0:T(8,128)(2,1)}, bf16[2,2,1,1,160,384]{5,4,3,2,1,0:T(8,128)(2,1)}, u32[]{:S(2)}, u32[]{:S(2)}) %collective-permute-start.7) | collective-permute-done | bytes 491552 | tf_op jit(solution)/shard_map/ppermute | solution.py:106
  79.6 2.8 shard_map.472.refs_0_.refs_2_
  83.9 2.9 collective-permute-start.10
  94.6 14.5 %collective-permute-done.9.refs_3_ = bf16[1,2,1,1,192,384]{5,4,3,2,1,0:T(8,128)(2,1)} collective-permute-done((bf16[1,2,1,1,192,384]{5,4,3,2,1,0:T(8,128)(2,1)S(1)}, bf16[1,2,1,1,192,384]{5,4,3,2,1,0:T(8,128)(2,1)}, u32[]{:S(2)}, u32[]{:S(2)}) %collective-permute-start.9) | collective-permute-done | bytes 294944 | tf_op jit(solution)/shard_map/ppermute | solution.py:106
  111.8 13.1 %collective-permute-done.10.refs_3_ = bf16[1,2,1,1,192,384]{5,4,3,2,1,0:T(8,128)(2,1)} collective-permute-done((bf16[1,2,1,1,192,384]{5,4,3,2,1,0:T(8,128)(2,1)}, bf16[1,2,1,1,192,384]{5,4,3,2,1,0:T(8,128)(2,1)}, u32[]{:S(2)}, u32[]{:S(2)}) %collective-permute-start.10) | collective-permute-done | bytes 294944 | tf_op jit(solution)/shard_map/ppermute | solution.py:106
  127.5 3.0 shard_map.476.refs_0_
  130.7 3.3 shard_map.477.refs_0_
  138.6 6.3 %shard_map.478 = (s32[512,1]{1,0:T(8,128)}, f32[512,768]{1,0:T(8,128)}) custom-call(bf16[2,2,2,2,192,384]{5,4,3,2,1,0:T(8,128)(2,1)} %shard_map.477.refs_0_, s32[1]{0:T(128)} %bitcast.4.refs_0_.refs_1_, s32[512,1]{1,0:T(8,128)} %bitcast.321, s32[1,256]{1,0:T(1,128)} %bitcast.345, f32[1,256]{1,0:T(1,128)} %bitcast.350, bf16[16,160,384]{2,1,0:T(8,128)(2,1)} %bitcast.354, ...), custom_call_target="tpu_custom_call" | custom-call | flops 6900000768 | bytes 1000 | tf_op jit(solution)/shard_map/pallas_call | solution.py:659
  147.0 9.2 %collective-permute-done.14.refs_3_ = bf16[2,2,1,1,192,384]{5,4,3,2,1,0:T(8,128)(2,1)} collective-permute-done((bf16[2,2,1,1,192,384]{5,4,3,2,1,0:T(8,128)(2,1)}, bf16[2,2,1,1,192,384]{5,4,3,2,1,0:T(8,128)(2,1)}, u32[]{:S(2)}, u32[]{:S(2)}) %collective-permute-start.14) | collective-permute-done | bytes 589856 | tf_op jit(solution)/shard_map/ppermute | solution.py:106
  159.3 2.8 shard_map.480.refs_0_.refs_2_
  164.0 14.8 %shard_map.481 = (bf16[3,512,768]{2,1,0:T(8,128)(2,1)}, f32[512,128]{1,0:T(8,128)}, bf16[512,768]{1,0:T(8,128)(2,1)}, f32[512,768]{1,0:T(8,128)}) custom-call(bf16[2,2,1,2,192,384]{5,4,3,2,1,0:T(8,128)(2,1)} %shard_map.480.refs_0_.refs_2_, s32[1]{0:T(128)} %bitcast.4.refs_0_.refs_1_, f32[512,768]{1,0:T(8,128)} %get-tuple-element.67.refs_2_.refs_3_, ...), custom_call_target="tpu_custom_call" | custom-call | flops 17250000896 | bytes 1000 | tf_op jit(solution)/shard_map/pallas_call | solution.py:659
  178.7 8.2 %collective-permute-done.17.refs_3_ = bf16[2,2,2,1,192,384]{5,4,3,2,1,0:T(8,128)(2,1)} collective-permute-done((bf16[2,2,2,1,192,384]{5,4,3,2,1,0:T(8,128)(2,1)}, bf16[2,2,2,1,192,384]{5,4,3,2,1,0:T(8,128)(2,1)}, u32[]{:S(2)}, u32[]{:S(2)}) %collective-permute-start.17) | collective-permute-done | bytes 1179680 | tf_op jit(solution)/shard_map/ppermute | solution.py:106
  187.0 3.3 shard_map.482.refs_0_
  190.3 3.2 shard_map.483.refs_0_
  201.8 12.0 %shard_map.484 = (f32[4,512,768]{2,1,0:T(8,128)}, f32[512,768]{1,0:T(8,128)}) custom-call(bf16[2,2,2,2,192,384]{5,4,3,2,1,0:T(8,128)(2,1)} %shard_map.483.refs_0_, s32[1]{0:T(128)} %bitcast.4.refs_0_.refs_1_, f32[512,768]{1,0:T(8,128)} %get-tuple-element.69.refs_2_.refs_3_, f32[12,768]{1,0:T(8,128)} %reshape.664.refs_3_.refs_4_, ...), custom_call_target="tpu_custom_call" | custom-call | flops 13800000512 | bytes 1000 | tf_op jit(solution)/shard_map/pallas_call | solution.py:659
  213.9 15.0 %shard_map.486 = (bf16[3,512,768]{2,1,0:T(8,128)(2,1)}, f32[512,128]{1,0:T(8,128)}, bf16[512,768]{1,0:T(8,128)(2,1)}, f32[512,768]{1,0:T(8,128)}) custom-call(f32[4,512,768]{2,1,0:T(8,128)} %get-tuple-element.70.refs_0_.refs_5_, s32[1]{0:T(128)} %bitcast.4.refs_0_.refs_1_, f32[512,768]{1,0:T(8,128)} %get-tuple-element.71.refs_2_.refs_3_, ...), custom_call_target="tpu_custom_call" | custom-call | flops 17250000896 | bytes 1000 | tf_op jit(solution)/shard_map/pallas_call | solution.py:659
  228.8 12.0 %shard_map.487 = (f32[4,512,768]{2,1,0:T(8,128)}, f32[512,768]{1,0:T(8,128)}) custom-call(bf16[3,512,768]{2,1,0:T(8,128)(2,1)} %get-tuple-element.72.refs_0_.refs_5_, s32[1]{0:T(128)} %bitcast.4.refs_0_.refs_1_, f32[512,768]{1,0:T(8,128)} %get-tuple-element.73.refs_2_.refs_3_, f32[12,768]{1,0:T(8,128)} %reshape.671.refs_3_.refs_4_, ...), custom_call_target="tpu_custom_call" | custom-call | flops 13800000512 | bytes 1000 | tf_op jit(solution)/shard_map/pallas_call | solution.py:659
  240.8 9.8 %shard_map.488 = (f32[512,768]{1,0:T(8,128)}, bf16[256,768]{1,0:T(8,128)(2,1)}, bf16[256,2304]{1,0:T(8,128)(2,1)}, f32[1,2304]{1,0:T(1,128)}, f32[2,768]{1,0:T(2,128)}, /*index=5*/f32[1,128]{1,0:T(1,128)}) custom-call(f32[4,512,768]{2,1,0:T(8,128)} %get-tuple-element.74.refs_0_.refs_5_, s32[1]{0:T(128)} %bitcast.4.refs_0_.refs_1_, ...), custom_call_target="tpu_custom_call" | custom-call | flops 11500001280 | bytes 1000 | tf_op jit(solution)/shard_map/pallas_call | solution.py:659
  250.7 20.8 %shard_map.489 = (f32[512,768]{1,0:T(8,128)}, f32[12,768]{1,0:T(8,128)}, bf16[16,2,384,384]{3,2,1,0:T(8,128)(2,1)}) custom-call(f32[512,768]{1,0:T(8,128)} %get-tuple-element.76.refs_0_.refs_2_, s32[1]{0:T(128)} %bitcast.4.refs_0_.refs_1_, f32[512,768]{1,0:T(8,128)} %get-tuple-element.76.refs_0_.refs_2_, f32[512,768]{1,0:T(8,128)} %get-tuple-element.73.refs_2_.refs_3_, ...), custom_call_target="tpu_custom_call" | custom-call | flops 1150001024 | bytes 1000 | tf_op jit(solution)/shard_map/pallas_call | solution.py:659
  271.5 23.3 %shard_map.490 = (f32[512,768]{1,0:T(8,128)}, f32[12,768]{1,0:T(8,128)}, bf16[16,192,384]{2,1,0:T(8,128)(2,1)}, bf16[16,192,384]{2,1,0:T(8,128)(2,1)}) custom-call(f32[512,768]{1,0:T(8,128)} %get-tuple-element.77.refs_0_.refs_2_, s32[1]{0:T(128)} %bitcast.4.refs_0_.refs_1_, f32[512,768]{1,0:T(8,128)} %get-tuple-element.77.refs_0_.refs_2_, ...), custom_call_target="tpu_custom_call" | custom-call | flops 1150001024 | bytes 1000 | tf_op jit(solution)/shard_map/pallas_call | solution.py:659
  295.0 20.6 %shard_map.491 = (f32[512,768]{1,0:T(8,128)}, f32[12,768]{1,0:T(8,128)}, bf16[16,192,384]{2,1,0:T(8,128)(2,1)}, bf16[16,192,384]{2,1,0:T(8,128)(2,1)}, bf16[16,1...) custom-call(f32[512,768]{1,0:T(8,128)} %get-tuple-element.80.refs_0_.refs_2_, s32[1]{0:T(128)} %bitcast.4.refs_0_.refs_1_, ...), custom_call_target="tpu_custom_call" | custom-call | flops 1150001024 | bytes 1000 | tf_op jit(solution)/shard_map/pallas_call | solution.py:659
  316.2 3.4 shard_map.492.refs_0_
  321.1 23.5 %shard_map.493 = (f32[512,768]{1,0:T(8,128)}, f32[12,768]{1,0:T(8,128)}, bf16[16,192,384]{2,1,0:T(8,128)(2,1)}, bf16[16,192,384]{2,1,0:T(8,128)(2,1)}) custom-call(bf16[2,2,2,1,192,384]{5,4,3,2,1,0:T(8,128)(2,1)} %shard_map.492.refs_0_, s32[1]{0:T(128)} %bitcast.4.refs_0_.refs_1_, f32[512,768]{1,0:T(8,128)} %get-tuple-element.81.refs_1_.refs_2_, ...), custom_call_target="tpu_custom_call" | custom-call | flops 1150001024 | bytes 1000 | tf_op jit(solution)/shard_map/pallas_call | solution.py:659
  347.1 3.3 shard_map.494.refs_1_
  351.8 3.3 shard_map.495.refs_1_
  356.6 2.9 shard_map.496.refs_1_
  361.0 3.3 shard_map.497.refs_0_
  364.8 15.0 %shard_map.498 = (bf16[16,160,384]{2,1,0:T(8,128)(2,1)}, bf16[16,160,384]{2,1,0:T(8,128)(2,1)}) custom-call(bf16[2,2,1,2,192,384]{5,4,3,2,1,0:T(8,128)(2,1)} %shard_map.497.refs_0_, s32[1]{0:T(128)} %bitcast.4.refs_0_.refs_1_, f32[512,768]{1,0:T(8,128)} %get-tuple-element.86.refs_1_.refs_2_, s32[512,1]{1,0:T(8,128)} %get-tuple-element.66.refs_0_.refs_3_, ...), custom_call_target="tpu_custom_call" | custom-call | flops 1150001024 | bytes 1000 | tf_op jit(solution)/shard_map/pallas_call | solution.py:659
  380.0 7.9 %collective-permute-done.26.refs_4_ = bf16[2,2,1,2,192,384]{5,4,3,2,1,0:T(8,128)(2,1)} collective-permute-done((bf16[2,2,1,2,192,384]{5,4,3,2,1,0:T(8,128)(2,1)}, bf16[2,2,1,2,192,384]{5,4,3,2,1,0:T(8,128)(2,1)}, u32[]{:S(2)}, u32[]{:S(2)}) %collective-permute-start.26) | collective-permute-done | bytes 1179680 | tf_op jit(solution)/shard_map/ppermute | solution.py:106
  387.9 2.9 shard_map.499.refs_1_
  393.3 2.9 shard_map.500.refs_1_
  396.2 3.1 shard_map.501.refs_1_
  401.6 7.3 %collective-permute-done.29.refs_5_ = bf16[2,2,1,1,192,384]{5,4,3,2,1,0:T(8,128)(2,1)} collective-permute-done((bf16[2,2,1,1,192,384]{5,4,3,2,1,0:T(8,128)(2,1)}, bf16[2,2,1,1,192,384]{5,4,3,2,1,0:T(8,128)(2,1)}, u32[]{:S(2)}, u32[]{:S(2)}) %collective-permute-start.29) | collective-permute-done | bytes 589856 | tf_op jit(solution)/shard_map/ppermute | solution.py:106
  408.9 2.8 shard_map.502.refs_1_
  411.8 3.0 collective-permute-start.34
  414.7 21.6 %collective-permute-done.30.refs_4_ = bf16[2,2,1,2,192,384]{5,4,3,2,1,0:T(8,128)(2,1)} collective-permute-done((bf16[2,2,1,2,192,384]{5,4,3,2,1,0:T(8,128)(2,1)}, bf16[2,2,1,2,192,384]{5,4,3,2,1,0:T(8,128)(2,1)}, u32[]{:S(2)}, u32[]{:S(2)}) %collective-permute-start.30) | collective-permute-done | bytes 1179680 | tf_op jit(solution)/shard_map/ppermute | solution.py:106
  436.3 3.0 shard_map.503.refs_1_
  439.9 4.2 reduce-scatter.2.cloned.1.call-done
  444.1 3.0 shard_map.504.refs_1_
  463.7 8.7 %collective-permute-done.35.refs_6_ = bf16[1,2,1,1,192,384]{5,4,3,2,1,0:T(8,128)(2,1)} collective-permute-done((bf16[1,2,1,1,192,384]{5,4,3,2,1,0:T(8,128)(2,1)}, bf16[1,2,1,1,192,384]{5,4,3,2,1,0:T(8,128)(2,1)}, u32[]{:S(2)}, u32[]{:S(2)}) %collective-permute-start.35) | collective-permute-done | bytes 294944 | tf_op jit(solution)/shard_map/ppermute | solution.py:106
  475.0 3.0 shard_map.509.refs_1_
  524.2 2.9 shard_map.518
  (448 shorter events, 177.2 us)
Async XLA Ops:
  7.2 206.6 %all-gather.3.cloned.1.call-start = ((), (), s32[]{:S(2)}) async-start(), calls=%async_computation.2 | async-start | bytes 14598144 | tf_op jit(solution)/shard_map/all_gather | solution.py:1017
  14.2 429.9 %reduce-scatter.2.cloned.1.call-start = ((), (), s32[]{:S(2)}) async-start(), calls=%async_computation.1 | async-start | bytes 9732096 | tf_op jit(solution)/shard_map/reduce_scatter | solution.py:1067
  15.3 30.9 %collective-permute-start.4 = (bf16[1,1,1,1,192,384]{5,4,3,2,1,0:T(8,128)(2,1)S(1)}, bf16[1,1,1,1,192,384]{5,4,3,2,1,0:T(8,128)(2,1)}, u32[]{:S(2)}, u32[]{:S(2)}) collective-permute-start(bf16[1,1,1,1,192,384]{5,4,3,2,1,0:T(8,128)(2,1)S(1)} %maximum_bitcast_fusion.3.refs_2_), channel_id=1, source_target_pairs={{0,8},{4,12},{8,0},{12,4},{16,24},{20,28},{24,16},{28,20},{1,9},{5... | collective-permute-start | bytes 442376 | tf_op jit(solution)/shard_map/ppermute | solution.py:106
  18.3 25.5 %collective-permute-start.3 = (bf16[1,1,1,1,192,384]{5,4,3,2,1,0:T(8,128)(2,1)S(1)}, bf16[1,1,1,1,192,384]{5,4,3,2,1,0:T(8,128)(2,1)}, u32[]{:S(2)}, u32[]{:S(2)}) collective-permute-start(bf16[1,1,1,1,192,384]{5,4,3,2,1,0:T(8,128)(2,1)S(1)} %bitcast.339), channel_id=1, source_target_pairs={{0,8},{4,12},{8,0},{12,4},{16,24},{20,28},{24,16},{28,20},{1,9},{5... | collective-permute-start | bytes 442376 | tf_op jit(solution)/shard_map/ppermute | solution.py:106
  18.5 11.6 %collective-permute-start.1 = (bf16[1,1,1,1,160,384]{5,4,3,2,1,0:T(8,128)(2,1)S(1)}, bf16[1,1,1,1,160,384]{5,4,3,2,1,0:T(8,128)(2,1)S(1)}, u32[]{:S(2)}, u32[]{:S(2)}) collective-permute-start(bf16[1,1,1,1,160,384]{5,4,3,2,1,0:T(8,128)(2,1)S(1)} %fusion.3.refs_2_), channel_id=1, source_target_pairs={{0,8},{4,12},{8,0},{12,4},{16,24},{20,28},{24,16},{28,20},{1,9},{5... | collective-permute-start | bytes 368648 | tf_op jit(solution)/shard_map/ppermute | solution.py:106
  21.4 16.8 %collective-permute-start.2 = (bf16[1,1,1,1,192,384]{5,4,3,2,1,0:T(8,128)(2,1)S(1)}, bf16[1,1,1,1,192,384]{5,4,3,2,1,0:T(8,128)(2,1)}, u32[]{:S(2)}, u32[]{:S(2)}) collective-permute-start(bf16[1,1,1,1,192,384]{5,4,3,2,1,0:T(8,128)(2,1)S(1)} %maximum_bitcast_fusion.2.refs_2_), channel_id=1, source_target_pairs={{0,8},{4,12},{8,0},{12,4},{16,24},{20,28},{24,16},{28,20},{1,9},{5... | collective-permute-start | bytes 442376 | tf_op jit(solution)/shard_map/ppermute | solution.py:106
  33.0 26.0 %collective-permute-start.5 = (bf16[1,2,1,1,160,384]{5,4,3,2,1,0:T(8,128)(2,1)}, bf16[1,2,1,1,160,384]{5,4,3,2,1,0:T(8,128)(2,1)S(1)}, u32[]{:S(2)}, u32[]{:S(2)}) collective-permute-start(bf16[1,2,1,1,160,384]{5,4,3,2,1,0:T(8,128)(2,1)} %shard_map.466.refs_0_.refs_2_), channel_id=1, source_target_pairs={{0,16},{4,20},{8,24},{12,28},{16,0},{20,4},{24,8},{28,12},{1,17},{... | collective-permute-start | bytes 737288 | tf_op jit(solution)/shard_map/ppermute | solution.py:106
  40.6 26.5 %collective-permute-start.6 = (bf16[1,2,1,1,192,384]{5,4,3,2,1,0:T(8,128)(2,1)}, bf16[1,2,1,1,192,384]{5,4,3,2,1,0:T(8,128)(2,1)S(1)}, u32[]{:S(2)}, u32[]{:S(2)}) collective-permute-start(bf16[1,2,1,1,192,384]{5,4,3,2,1,0:T(8,128)(2,1)} %shard_map.467.refs_0_.refs_2_), channel_id=1, source_target_pairs={{0,16},{4,20},{8,24},{12,28},{16,0},{20,4},{24,8},{28,12},{1,17},{... | collective-permute-start | bytes 884744 | tf_op jit(solution)/shard_map/ppermute | solution.py:106
  62.3 17.3 %collective-permute-start.7 = (bf16[2,2,1,1,160,384]{5,4,3,2,1,0:T(8,128)(2,1)}, bf16[2,2,1,1,160,384]{5,4,3,2,1,0:T(8,128)(2,1)}, u32[]{:S(2)}, u32[]{:S(2)}) collective-permute-start(bf16[2,2,1,1,160,384]{5,4,3,2,1,0:T(8,128)(2,1)} %shard_map.470.refs_0_.refs_2_), channel_id=1, source_target_pairs={{0,4},{4,0},{8,12},{12,8},{16,20},{20,16},{24,28},{28,24},{1,5},{5... | collective-permute-start | bytes 1474568 | tf_op jit(solution)/shard_map/ppermute | solution.py:106
  70.3 19.2 %collective-permute-start.8 = (bf16[2,2,1,1,192,384]{5,4,3,2,1,0:T(8,128)(2,1)}, bf16[2,2,1,1,192,384]{5,4,3,2,1,0:T(8,128)(2,1)S(1)}, u32[]{:S(2)}, u32[]{:S(2)}) collective-permute-start(bf16[2,2,1,1,192,384]{5,4,3,2,1,0:T(8,128)(2,1)} %shard_map.471.refs_0_.refs_2_), channel_id=1, source_target_pairs={{0,2},{1,3},{2,0},{3,1},{4,6},{5,7},{6,4},{7,5},{8,10},{9,11},{10,... | collective-permute-start | bytes 1769480 | tf_op jit(solution)/shard_map/ppermute | solution.py:106
  82.4 45.1 %collective-permute-start.11 = (bf16[2,2,2,1,160,384]{5,4,3,2,1,0:T(8,128)(2,1)}, bf16[2,2,2,1,160,384]{5,4,3,2,1,0:T(8,128)(2,1)}, u32[]{:S(2)}, u32[]{:S(2)}) collective-permute-start(bf16[2,2,2,1,160,384]{5,4,3,2,1,0:T(8,128)(2,1)} %shard_map.472.refs_0_.refs_2_), channel_id=1, source_target_pairs={{0,2},{1,3},{2,0},{3,1},{4,6},{5,7},{6,4},{7,5},{8,10},{9,11},{10,... | collective-permute-start | bytes 2949128 | tf_op jit(solution)/shard_map/ppermute | solution.py:106
  83.9 25.2 %collective-permute-start.9 = (bf16[1,2,1,1,192,384]{5,4,3,2,1,0:T(8,128)(2,1)S(1)}, bf16[1,2,1,1,192,384]{5,4,3,2,1,0:T(8,128)(2,1)}, u32[]{:S(2)}, u32[]{:S(2)}) collective-permute-start(bf16[1,2,1,1,192,384]{5,4,3,2,1,0:T(8,128)(2,1)S(1)} %copy-done.55), channel_id=1, source_target_pairs={{0,16},{4,20},{8,24},{12,28},{16,0},{20,4},{24,8},{28,12},{1,17},{... | collective-permute-start | bytes 884744 | tf_op jit(solution)/shard_map/ppermute | solution.py:106
  83.9 41.1 %collective-permute-start.10 = (bf16[1,2,1,1,192,384]{5,4,3,2,1,0:T(8,128)(2,1)}, bf16[1,2,1,1,192,384]{5,4,3,2,1,0:T(8,128)(2,1)}, u32[]{:S(2)}, u32[]{:S(2)}) collective-permute-start(bf16[1,2,1,1,192,384]{5,4,3,2,1,0:T(8,128)(2,1)} %shard_map.469.refs_0_.refs_2_), channel_id=1, source_target_pairs={{0,16},{4,20},{8,24},{12,28},{16,0},{20,4},{24,8},{28,12},{1,17},{... | collective-permute-start | bytes 884744 | tf_op jit(solution)/shard_map/ppermute | solution.py:106
  93.1 37.6 %collective-permute-start.12 = (bf16[2,2,1,2,192,384]{5,4,3,2,1,0:T(8,128)(2,1)}, bf16[2,2,1,2,192,384]{5,4,3,2,1,0:T(8,128)(2,1)}, u32[]{:S(2)}, u32[]{:S(2)}) collective-permute-start(bf16[2,2,1,2,192,384]{5,4,3,2,1,0:T(8,128)(2,1)} %shard_map.473.refs_0_.refs_2_), channel_id=1, source_target_pairs={{0,4},{4,0},{8,12},{12,8},{16,20},{20,16},{24,28},{28,24},{1,5},{5... | collective-permute-start | bytes 3538952 | tf_op jit(solution)/shard_map/ppermute | solution.py:106
  130.6 8.1 %collective-permute-start.13 = (bf16[2,2,2,2,160,384]{5,4,3,2,1,0:T(8,128)(2,1)}, bf16[2,2,2,2,160,384]{5,4,3,2,1,0:T(8,128)(2,1)}, u32[]{:S(2)}, u32[]{:S(2)}) collective-permute-start(bf16[2,2,2,2,160,384]{5,4,3,2,1,0:T(8,128)(2,1)} %shard_map.476.refs_0_), channel_id=1, source_target_pairs={{0,1},{1,0},{2,3},{3,2},{4,5},{5,4},{6,7},{7,6},{8,9},{9,8},{10,11... | collective-permute-start | bytes 5898248 | tf_op jit(solution)/shard_map/ppermute | solution.py:106
  134.0 30.0 %collective-permute-start.16 = (bf16[2,2,2,2,192,384]{5,4,3,2,1,0:T(8,128)(2,1)}, bf16[2,2,2,2,192,384]{5,4,3,2,1,0:T(8,128)(2,1)}, u32[]{:S(2)}, u32[]{:S(2)}) collective-permute-start(bf16[2,2,2,2,192,384]{5,4,3,2,1,0:T(8,128)(2,1)} %shard_map.477.refs_0_), channel_id=1, source_target_pairs={{0,1},{1,0},{2,3},{3,2},{4,5},{5,4},{6,7},{7,6},{8,9},{9,8},{10,11... | collective-permute-start | bytes 7077896 | tf_op jit(solution)/shard_map/ppermute | solution.py:106
  136.6 19.6 %collective-permute-start.14 = (bf16[2,2,1,1,192,384]{5,4,3,2,1,0:T(8,128)(2,1)}, bf16[2,2,1,1,192,384]{5,4,3,2,1,0:T(8,128)(2,1)}, u32[]{:S(2)}, u32[]{:S(2)}) collective-permute-start(bf16[2,2,1,1,192,384]{5,4,3,2,1,0:T(8,128)(2,1)} %shard_map.474.refs_0_.refs_2_), channel_id=1, source_target_pairs={{0,4},{4,0},{8,12},{12,8},{16,20},{20,16},{24,28},{28,24},{1,5},{5... | collective-permute-start | bytes 1769480 | tf_op jit(solution)/shard_map/ppermute | solution.py:106
  137.7 21.6 %collective-permute-start.15 = (bf16[2,2,1,1,192,384]{5,4,3,2,1,0:T(8,128)(2,1)S(1)}, bf16[2,2,1,1,192,384]{5,4,3,2,1,0:T(8,128)(2,1)}, u32[]{:S(2)}, u32[]{:S(2)}) collective-permute-start(bf16[2,2,1,1,192,384]{5,4,3,2,1,0:T(8,128)(2,1)S(1)} %copy-done.53), channel_id=1, source_target_pairs={{0,2},{1,3},{2,0},{3,1},{4,6},{5,7},{6,4},{7,5},{8,10},{9,11},{10,... | collective-permute-start | bytes 1769480 | tf_op jit(solution)/shard_map/ppermute | solution.py:106
  158.9 28.1 %collective-permute-start.17 = (bf16[2,2,2,1,192,384]{5,4,3,2,1,0:T(8,128)(2,1)}, bf16[2,2,2,1,192,384]{5,4,3,2,1,0:T(8,128)(2,1)}, u32[]{:S(2)}, u32[]{:S(2)}) collective-permute-start(bf16[2,2,2,1,192,384]{5,4,3,2,1,0:T(8,128)(2,1)} %shard_map.479.refs_0_.refs_2_), channel_id=1, source_target_pairs={{0,2},{1,3},{2,0},{3,1},{4,6},{5,7},{6,4},{7,5},{8,10},{9,11},{10,... | collective-permute-start | bytes 3538952 | tf_op jit(solution)/shard_map/ppermute | solution.py:106
  162.1 28.2 %collective-permute-start.18 = (bf16[2,2,1,2,192,384]{5,4,3,2,1,0:T(8,128)(2,1)}, bf16[2,2,1,2,192,384]{5,4,3,2,1,0:T(8,128)(2,1)}, u32[]{:S(2)}, u32[]{:S(2)}) collective-permute-start(bf16[2,2,1,2,192,384]{5,4,3,2,1,0:T(8,128)(2,1)} %shard_map.480.refs_0_.refs_2_), channel_id=1, source_target_pairs={{0,4},{4,0},{8,12},{12,8},{16,20},{20,16},{24,28},{28,24},{1,5},{5... | collective-permute-start | bytes 3538952 | tf_op jit(solution)/shard_map/ppermute | solution.py:106
  193.6 8.2 %collective-permute-start.19 = (bf16[2,2,2,2,192,384]{5,4,3,2,1,0:T(8,128)(2,1)}, bf16[2,2,2,2,192,384]{5,4,3,2,1,0:T(8,128)(2,1)}, u32[]{:S(2)}, u32[]{:S(2)}) collective-permute-start(bf16[2,2,2,2,192,384]{5,4,3,2,1,0:T(8,128)(2,1)} %shard_map.482.refs_0_), channel_id=1, source_target_pairs={{0,1},{1,0},{2,3},{3,2},{4,5},{5,4},{6,7},{7,6},{8,9},{9,8},{10,11... | collective-permute-start | bytes 7077896 | tf_op jit(solution)/shard_map/ppermute | solution.py:106
  294.8 21.3 %collective-permute-start.21 = (bf16[16,192,384]{2,1,0:T(8,128)(2,1)}, bf16[16,192,384]{2,1,0:T(8,128)(2,1)}, u32[]{:S(2)}, u32[]{:S(2)}) collective-permute-start(bf16[16,192,384]{2,1,0:T(8,128)(2,1)} %get-tuple-element.83), channel_id=1, source_target_pairs={{0,1},{1,0},{2,3},{3,2},{4,5},{5,4},{6,7},{7,6},{8,9},{9,8},{10,11... | collective-permute-start | bytes 7077896 | tf_op jit(solution)/shard_map/ppermute | solution.py:106
  315.6 31.5 %collective-permute-start.22 = (bf16[16,192,384]{2,1,0:T(8,128)(2,1)}, bf16[16,192,384]{2,1,0:T(8,128)(2,1)}, u32[]{:S(2)}, u32[]{:S(2)}) collective-permute-start(bf16[16,192,384]{2,1,0:T(8,128)(2,1)} %get-tuple-element.88), channel_id=1, source_target_pairs={{0,1},{1,0},{2,3},{3,2},{4,5},{5,4},{6,7},{7,6},{8,9},{9,8},{10,11... | collective-permute-start | bytes 7077896 | tf_op jit(solution)/shard_map/ppermute | solution.py:106
  316.0 35.7 %collective-permute-start.23 = (bf16[16,192,384]{2,1,0:T(8,128)(2,1)}, bf16[16,192,384]{2,1,0:T(8,128)(2,1)}, u32[]{:S(2)}, u32[]{:S(2)}) collective-permute-start(bf16[16,192,384]{2,1,0:T(8,128)(2,1)} %get-tuple-element.90), channel_id=1, source_target_pairs={{0,1},{1,0},{2,3},{3,2},{4,5},{5,4},{6,7},{7,6},{8,9},{9,8},{10,11... | collective-permute-start | bytes 7077896 | tf_op jit(solution)/shard_map/ppermute | solution.py:106
  319.6 37.0 %collective-permute-start.24 = (bf16[2,2,2,1,192,384]{5,4,3,2,1,0:T(8,128)(2,1)}, bf16[2,2,2,1,192,384]{5,4,3,2,1,0:T(8,128)(2,1)}, u32[]{:S(2)}, u32[]{:S(2)}) collective-permute-start(bf16[2,2,2,1,192,384]{5,4,3,2,1,0:T(8,128)(2,1)} %shard_map.492.refs_0_), channel_id=1, source_target_pairs={{0,2},{1,3},{2,0},{3,1},{4,6},{5,7},{6,4},{7,5},{8,10},{9,11},{10,... | collective-permute-start | bytes 3538952 | tf_op jit(solution)/shard_map/ppermute | solution.py:106
  344.6 16.4 %collective-permute-start.25 = (bf16[16,192,384]{2,1,0:T(8,128)(2,1)}, bf16[16,192,384]{2,1,0:T(8,128)(2,1)}, u32[]{:S(2)}, u32[]{:S(2)}) collective-permute-start(bf16[16,192,384]{2,1,0:T(8,128)(2,1)} %get-tuple-element.92), channel_id=1, source_target_pairs={{0,1},{1,0},{2,3},{3,2},{4,5},{5,4},{6,7},{7,6},{8,9},{9,8},{10,11... | collective-permute-start | bytes 7077896 | tf_op jit(solution)/shard_map/ppermute | solution.py:106
  350.3 37.5 %collective-permute-start.26 = (bf16[2,2,1,2,192,384]{5,4,3,2,1,0:T(8,128)(2,1)}, bf16[2,2,1,2,192,384]{5,4,3,2,1,0:T(8,128)(2,1)}, u32[]{:S(2)}, u32[]{:S(2)}) collective-permute-start(bf16[2,2,1,2,192,384]{5,4,3,2,1,0:T(8,128)(2,1)} %shard_map.494.refs_1_), channel_id=1, source_target_pairs={{0,4},{4,0},{8,12},{12,8},{16,20},{20,16},{24,28},{28,24},{1,5},{5... | collective-permute-start | bytes 3538952 | tf_op jit(solution)/shard_map/ppermute | solution.py:106
  355.0 38.2 %collective-permute-start.27 = (bf16[2,2,2,1,192,384]{5,4,3,2,1,0:T(8,128)(2,1)}, bf16[2,2,2,1,192,384]{5,4,3,2,1,0:T(8,128)(2,1)}, u32[]{:S(2)}, u32[]{:S(2)}) collective-permute-start(bf16[2,2,2,1,192,384]{5,4,3,2,1,0:T(8,128)(2,1)} %shard_map.495.refs_1_), channel_id=1, source_target_pairs={{0,2},{1,3},{2,0},{3,1},{4,6},{5,7},{6,4},{7,5},{8,10},{9,11},{10,... | collective-permute-start | bytes 3538952 | tf_op jit(solution)/shard_map/ppermute | solution.py:106
  359.5 49.4 %collective-permute-start.29 = (bf16[2,2,1,1,192,384]{5,4,3,2,1,0:T(8,128)(2,1)}, bf16[2,2,1,1,192,384]{5,4,3,2,1,0:T(8,128)(2,1)}, u32[]{:S(2)}, u32[]{:S(2)}) collective-permute-start(bf16[2,2,1,1,192,384]{5,4,3,2,1,0:T(8,128)(2,1)} %shard_map.496.refs_1_), channel_id=1, source_target_pairs={{0,4},{4,0},{8,12},{12,8},{16,20},{20,16},{24,28},{28,24},{1,5},{5... | collective-permute-start | bytes 1769480 | tf_op jit(solution)/shard_map/ppermute | solution.py:106
  364.4 71.9 %collective-permute-start.30 = (bf16[2,2,1,2,192,384]{5,4,3,2,1,0:T(8,128)(2,1)}, bf16[2,2,1,2,192,384]{5,4,3,2,1,0:T(8,128)(2,1)}, u32[]{:S(2)}, u32[]{:S(2)}) collective-permute-start(bf16[2,2,1,2,192,384]{5,4,3,2,1,0:T(8,128)(2,1)} %shard_map.497.refs_0_), channel_id=1, source_target_pairs={{0,4},{4,0},{8,12},{12,8},{16,20},{20,16},{24,28},{28,24},{1,5},{5... | collective-permute-start | bytes 3538952 | tf_op jit(solution)/shard_map/ppermute | solution.py:106
  379.9 16.3 %collective-permute-start.28 = (bf16[16,160,384]{2,1,0:T(8,128)(2,1)}, bf16[16,160,384]{2,1,0:T(8,128)(2,1)}, u32[]{:S(2)}, u32[]{:S(2)}) collective-permute-start(bf16[16,160,384]{2,1,0:T(8,128)(2,1)} %get-tuple-element.102), channel_id=1, source_target_pairs={{0,1},{1,0},{2,3},{3,2},{4,5},{5,4},{6,7},{7,6},{8,9},{9,8},{10,11... | collective-permute-start | bytes 5898248 | tf_op jit(solution)/shard_map/ppermute | solution.py:106
  399.3 40.6 %collective-permute-start.31 = (bf16[2,2,2,1,160,384]{5,4,3,2,1,0:T(8,128)(2,1)}, bf16[2,2,2,1,160,384]{5,4,3,2,1,0:T(8,128)(2,1)S(1)}, u32[]{:S(2)}, u32[]{:S(2)}) collective-permute-start(bf16[2,2,2,1,160,384]{5,4,3,2,1,0:T(8,128)(2,1)} %shard_map.501.refs_1_), channel_id=1, source_target_pairs={{0,2},{1,3},{2,0},{3,1},{4,6},{5,7},{6,4},{7,5},{8,10},{9,11},{10,... | collective-permute-start | bytes 2949128 | tf_op jit(solution)/shard_map/ppermute | solution.py:106
  400.8 46.8 %collective-permute-start.32 = (bf16[2,2,1,1,192,384]{5,4,3,2,1,0:T(8,128)(2,1)}, bf16[2,2,1,1,192,384]{5,4,3,2,1,0:T(8,128)(2,1)}, u32[]{:S(2)}, u32[]{:S(2)}) collective-permute-start(bf16[2,2,1,1,192,384]{5,4,3,2,1,0:T(8,128)(2,1)} %shard_map.499.refs_1_), channel_id=1, source_target_pairs={{0,2},{1,3},{2,0},{3,1},{4,6},{5,7},{6,4},{7,5},{8,10},{9,11},{10,... | collective-permute-start | bytes 1769480 | tf_op jit(solution)/shard_map/ppermute | solution.py:106
  401.3 50.6 %collective-permute-start.33 = (bf16[2,2,1,1,192,384]{5,4,3,2,1,0:T(8,128)(2,1)}, bf16[2,2,1,1,192,384]{5,4,3,2,1,0:T(8,128)(2,1)}, u32[]{:S(2)}, u32[]{:S(2)}) collective-permute-start(bf16[2,2,1,1,192,384]{5,4,3,2,1,0:T(8,128)(2,1)} %shard_map.500.refs_1_), channel_id=1, source_target_pairs={{0,4},{4,0},{8,12},{12,8},{16,20},{20,16},{24,28},{28,24},{1,5},{5... | collective-permute-start | bytes 1769480 | tf_op jit(solution)/shard_map/ppermute | solution.py:106
  411.8 44.4 %collective-permute-start.34 = (bf16[1,2,1,1,192,384]{5,4,3,2,1,0:T(8,128)(2,1)}, bf16[1,2,1,1,192,384]{5,4,3,2,1,0:T(8,128)(2,1)}, u32[]{:S(2)}, u32[]{:S(2)}) collective-permute-start(bf16[1,2,1,1,192,384]{5,4,3,2,1,0:T(8,128)(2,1)} %shard_map.502.refs_1_), channel_id=1, source_target_pairs={{0,16},{4,20},{8,24},{12,28},{16,0},{20,4},{24,8},{28,12},{1,17},{... | collective-permute-start | bytes 884744 | tf_op jit(solution)/shard_map/ppermute | solution.py:106
  439.3 35.7 %collective-permute-start.36 = (bf16[2,2,1,1,192,384]{5,4,3,2,1,0:T(8,128)(2,1)}, bf16[2,2,1,1,192,384]{5,4,3,2,1,0:T(8,128)(2,1)}, u32[]{:S(2)}, u32[]{:S(2)}) collective-permute-start(bf16[2,2,1,1,192,384]{5,4,3,2,1,0:T(8,128)(2,1)} %shard_map.503.refs_1_), channel_id=1, source_target_pairs={{0,2},{1,3},{2,0},{3,1},{4,6},{5,7},{6,4},{7,5},{8,10},{9,11},{10,... | collective-permute-start | bytes 1769480 | tf_op jit(solution)/shard_map/ppermute | solution.py:106
  447.1 33.3 %collective-permute-start.37 = (bf16[2,2,1,1,160,384]{5,4,3,2,1,0:T(8,128)(2,1)}, bf16[2,2,1,1,160,384]{5,4,3,2,1,0:T(8,128)(2,1)}, u32[]{:S(2)}, u32[]{:S(2)}) collective-permute-start(bf16[2,2,1,1,160,384]{5,4,3,2,1,0:T(8,128)(2,1)} %shard_map.504.refs_1_), channel_id=1, source_target_pairs={{0,4},{4,0},{8,12},{12,8},{16,20},{20,16},{24,28},{28,24},{1,5},{5... | collective-permute-start | bytes 1474568 | tf_op jit(solution)/shard_map/ppermute | solution.py:106
  450.3 22.0 %collective-permute-start.35 = (bf16[1,2,1,1,192,384]{5,4,3,2,1,0:T(8,128)(2,1)}, bf16[1,2,1,1,192,384]{5,4,3,2,1,0:T(8,128)(2,1)}, u32[]{:S(2)}, u32[]{:S(2)}) collective-permute-start(bf16[1,2,1,1,192,384]{5,4,3,2,1,0:T(8,128)(2,1)} %shard_map.505.refs_1_), channel_id=1, source_target_pairs={{0,16},{4,20},{8,24},{12,28},{16,0},{20,4},{24,8},{28,12},{1,17},{... | collective-permute-start | bytes 884744 | tf_op jit(solution)/shard_map/ppermute | solution.py:106
  454.7 29.0 %collective-permute-start.38 = (bf16[1,2,1,1,192,384]{5,4,3,2,1,0:T(8,128)(2,1)}, bf16[1,2,1,1,192,384]{5,4,3,2,1,0:T(8,128)(2,1)}, u32[]{:S(2)}, u32[]{:S(2)}) collective-permute-start(bf16[1,2,1,1,192,384]{5,4,3,2,1,0:T(8,128)(2,1)} %shard_map.506.refs_1_), channel_id=1, source_target_pairs={{0,16},{4,20},{8,24},{12,28},{16,0},{20,4},{24,8},{28,12},{1,17},{... | collective-permute-start | bytes 884744 | tf_op jit(solution)/shard_map/ppermute | solution.py:106
  458.8 29.6 %collective-permute-start.39 = (bf16[1,1,1,1,192,384]{5,4,3,2,1,0:T(8,128)(2,1)}, bf16[1,1,1,1,192,384]{5,4,3,2,1,0:T(8,128)(2,1)}, u32[]{:S(2)}, u32[]{:S(2)}) collective-permute-start(bf16[1,1,1,1,192,384]{5,4,3,2,1,0:T(8,128)(2,1)} %shard_map.507.refs_1_), channel_id=1, source_target_pairs={{0,8},{4,12},{8,0},{12,4},{16,24},{20,28},{24,16},{28,20},{1,9},{5... | collective-permute-start | bytes 442376 | tf_op jit(solution)/shard_map/ppermute | solution.py:106
  475.0 20.7 %collective-permute-start.40 = (bf16[1,1,1,1,192,384]{5,4,3,2,1,0:T(8,128)(2,1)}, bf16[1,1,1,1,192,384]{5,4,3,2,1,0:T(8,128)(2,1)S(1)}, u32[]{:S(2)}, u32[]{:S(2)}) collective-permute-start(bf16[1,1,1,1,192,384]{5,4,3,2,1,0:T(8,128)(2,1)} %shard_map.508.refs_1_), channel_id=1, source_target_pairs={{0,8},{4,12},{8,0},{12,4},{16,24},{20,28},{24,16},{28,20},{1,9},{5... | collective-permute-start | bytes 442376 | tf_op jit(solution)/shard_map/ppermute | solution.py:106
  478.0 31.2 %collective-permute-start.43 = (bf16[1,2,1,1,192,384]{5,4,3,2,1,0:T(8,128)(2,1)}, bf16[1,2,1,1,192,384]{5,4,3,2,1,0:T(8,128)(2,1)}, u32[]{:S(2)}, u32[]{:S(2)}) collective-permute-start(bf16[1,2,1,1,192,384]{5,4,3,2,1,0:T(8,128)(2,1)} %shard_map.509.refs_1_), channel_id=1, source_target_pairs={{0,16},{4,20},{8,24},{12,28},{16,0},{20,4},{24,8},{28,12},{1,17},{... | collective-permute-start | bytes 884744 | tf_op jit(solution)/shard_map/ppermute | solution.py:106
  483.0 20.9 %collective-permute-start.41 = (bf16[1,2,1,1,160,384]{5,4,3,2,1,0:T(8,128)(2,1)}, bf16[1,2,1,1,160,384]{5,4,3,2,1,0:T(8,128)(2,1)}, u32[]{:S(2)}, u32[]{:S(2)}) collective-permute-start(bf16[1,2,1,1,160,384]{5,4,3,2,1,0:T(8,128)(2,1)} %shard_map.510.refs_1_), channel_id=1, source_target_pairs={{0,16},{4,20},{8,24},{12,28},{16,0},{20,4},{24,8},{28,12},{1,17},{... | collective-permute-start | bytes 737288 | tf_op jit(solution)/shard_map/ppermute | solution.py:106
  486.3 20.2 %collective-permute-start.42 = (bf16[1,1,1,1,192,384]{5,4,3,2,1,0:T(8,128)(2,1)}, bf16[1,1,1,1,192,384]{5,4,3,2,1,0:T(8,128)(2,1)}, u32[]{:S(2)}, u32[]{:S(2)}) collective-permute-start(bf16[1,1,1,1,192,384]{5,4,3,2,1,0:T(8,128)(2,1)} %shard_map.511.refs_1_), channel_id=1, source_target_pairs={{0,8},{4,12},{8,0},{12,4},{16,24},{20,28},{24,16},{28,20},{1,9},{5... | collective-permute-start | bytes 442376 | tf_op jit(solution)/shard_map/ppermute | solution.py:106
  495.0 55.9 %collective-permute-start.54 = (f32[288,384]{1,0:T(8,128)}, f32[288,384]{1,0:T(8,128)}, u32[]{:S(2)}, u32[]{:S(2)}) collective-permute-start(f32[288,384]{1,0:T(8,128)} %get-tuple-element.194), channel_id=1, source_target_pairs={{0,1},{1,0},{2,3},{3,2},{4,5},{5,4},{6,7},{7,6},{8,9},{9,8},{10,11... | collective-permute-start | bytes 1327112 | tf_op jit(solution)/shard_map/ppermute | solution.py:106
  506.5 10.2 %collective-permute-start.44 = (bf16[1,1,1,1,160,384]{5,4,3,2,1,0:T(8,128)(2,1)}, bf16[1,1,1,1,160,384]{5,4,3,2,1,0:T(8,128)(2,1)S(1)}, u32[]{:S(2)}, u32[]{:S(2)}) collective-permute-start(bf16[1,1,1,1,160,384]{5,4,3,2,1,0:T(8,128)(2,1)} %shard_map.514.refs_1_), channel_id=1, source_target_pairs={{0,8},{4,12},{8,0},{12,4},{16,24},{20,28},{24,16},{28,20},{1,9},{5... | collective-permute-start | bytes 368648 | tf_op jit(solution)/shard_map/ppermute | solution.py:106
  512.7 11.5 %collective-permute-start.45 = (bf16[1,1,1,1,192,384]{5,4,3,2,1,0:T(8,128)(2,1)}, bf16[1,1,1,1,192,384]{5,4,3,2,1,0:T(8,128)(2,1)}, u32[]{:S(2)}, u32[]{:S(2)}) collective-permute-start(bf16[1,1,1,1,192,384]{5,4,3,2,1,0:T(8,128)(2,1)} %shard_map.516.refs_1_), channel_id=1, source_target_pairs={{0,8},{4,12},{8,0},{12,4},{16,24},{20,28},{24,16},{28,20},{1,9},{5... | collective-permute-start | bytes 442376 | tf_op jit(solution)/shard_map/ppermute | solution.py:106
  544.7 9.4 %collective-permute-start.53 = (f32[360,384]{1,0:T(8,128)}, f32[360,384]{1,0:T(8,128)S(1)}, u32[]{:S(2)}, u32[]{:S(2)}) collective-permute-start(f32[360,384]{1,0:T(8,128)} %get-tuple-element.196), channel_id=1, source_target_pairs={{0,1},{1,0},{2,3},{3,2},{4,5},{5,4},{6,7},{7,6},{8,9},{9,8},{10,11... | collective-permute-start | bytes 1658888 | tf_op jit(solution)/shard_map/ppermute | solution.py:106
  (71 other events, 496.1 us)
Sparse Core Ops, SparseCore 0:
  14.3 152.4 all-gather.2
  271.6 172.4 reduce-scatter.1
